TPU v7x, 32 devices: a whole 2x2x4 slice. The times are simulated.
32 devices in a mesh: gx: 8 (over y, x, core), gy: 4 (over z).
Axes of the slice: x: 2, y: 2, z: 4, core: 2. Of those that a mesh axis runs over, the one named last changes fastest.
Arguments:
- basis: bfloat16 [16, 4, 128, 1024], P(None, None, 'gy', 'gx'), may hold values from -56 to 56
- mobility: bfloat16 [4, 128, 1024], P(None, 'gy', 'gx'), may hold values from 0.12 to 8.2
- accumulation: float32 [4, 128, 1024], P(None, 'gy', 'gx'), may hold values from 0.03 to 0.32
- residual: float32 [4, 128, 1024], P(None, 'gy', 'gx'), may hold values from -140 to 140
Outputs:
- correction: float32 [4, 128, 1024], P(None, 'gy', 'gx')
- coarse_solution: float32 [8, 4, 16], P('gx', 'gy')
All inputs are finite; a program needn't handle non-finite values.
Results may differ from a plain program's by a relative error of at most 0.0003.
Values may be sent and summed in bfloat16 or wider, within the bound.
No kernel may reach another device: no remote copies, remote signals or barrier semaphores. Data moves between devices by JAX's collectives and lax.ppermute only.
A program may use at most 64 MiB of HBM per device.

v0:
```python
import jax
import jax.numpy as jnp
from jax import lax
from jax.sharding import PartitionSpec as P

K = 16
ITERS = 2


epsilon = 1e-06
vertical_ratio = 0.1


def with_halo(x, sides, width):
    for axis, dim in sides:
        peers, length = (lax.axis_size(axis), x.shape[dim])
        up = [(i, (i + 1) % peers) for i in range(peers - 1)]
        down = [(j, i) for i, j in up]
        last = lax.slice_in_dim(x, length - width, length, axis=dim)
        initial = lax.slice_in_dim(x, 0, width, axis=dim)
        before = lax.ppermute(last, axis, up)
        after = lax.ppermute(initial, axis, down)
        x = jnp.concatenate([before, x, after], axis=dim)
    return x


def harmonic(first, second):
    return 2.0 * first * second / (first + second)


def gram_sum(weighted, other):
    return jnp.einsum("kzyx,lzyx->kl", weighted, other, precision=lax.Precision.HIGHEST)


def face_blocks(padded_basis, padded_mobility, accumulation):
    interior = padded_basis[:, :, 1:-1, 1:-1]
    cell_mobility = padded_mobility[:, 1:-1, 1:-1]
    self_block = gram_sum(interior * accumulation, interior)
    conduct_x = harmonic(cell_mobility[:, :, :-1], cell_mobility[:, :, 1:])
    change_x = interior[:, :, :, 1:] - interior[:, :, :, :-1]
    self_block = self_block + gram_sum(change_x * conduct_x, change_x)
    conduct_y = harmonic(cell_mobility[:, :-1, :], cell_mobility[:, 1:, :])
    change_y = interior[:, :, 1:, :] - interior[:, :, :-1, :]
    self_block = self_block + gram_sum(change_y * conduct_y, change_y)
    conduct_z = vertical_ratio * harmonic(cell_mobility[:-1], cell_mobility[1:])
    change_z = interior[:, 1:] - interior[:, :-1]
    self_block = self_block + gram_sum(change_z * conduct_z, change_z)
    edges = (
        (
            interior[:, :, :, :1],
            padded_basis[:, :, 1:-1, :1],
            cell_mobility[:, :, :1],
            padded_mobility[:, 1:-1, :1],
        ),
        (
            interior[:, :, :, -1:],
            padded_basis[:, :, 1:-1, -1:],
            cell_mobility[:, :, -1:],
            padded_mobility[:, 1:-1, -1:],
        ),
        (
            interior[:, :, :1, :],
            padded_basis[:, :, :1, 1:-1],
            cell_mobility[:, :1, :],
            padded_mobility[:, :1, 1:-1],
        ),
        (
            interior[:, :, -1:, :],
            padded_basis[:, :, -1:, 1:-1],
            cell_mobility[:, -1:, :],
            padded_mobility[:, -1:, 1:-1],
        ),
    )
    side_blocks = []
    for edge_cells, ghost_cells, edge_mobility, ghost_mobility in edges:
        weighted = edge_cells * harmonic(edge_mobility, ghost_mobility)
        self_block = self_block + gram_sum(weighted, edge_cells)
        side_blocks.append(-gram_sum(weighted, ghost_cells))
    return jnp.stack([self_block] + side_blocks)


def coarse_apply(blocks, vector):
    padded = jnp.pad(vector, ((1, 1), (1, 1), (0, 0)))
    beside = jnp.stack(
        [vector, padded[:-2, 1:-1], padded[2:, 1:-1], padded[1:-1, :-2], padded[1:-1, 2:]], axis=2
    )
    return jnp.einsum("abnkl,abnl->abk", blocks, beside, precision=lax.Precision.HIGHEST)


def coarse_solve(blocks, coarse_source):
    solution = jnp.zeros_like(coarse_source)
    remainder = coarse_source
    direction = coarse_source
    energy = jnp.sum(remainder * remainder)
    for iteration in range(ITERS):
        operator_image = coarse_apply(blocks, direction)
        step_length = energy / (jnp.sum(direction * operator_image) + epsilon)
        solution = solution + step_length * direction
        if iteration + 1 < ITERS:
            remainder = remainder - step_length * operator_image
            renewed = jnp.sum(remainder * remainder)
            direction = remainder + renewed / (energy + epsilon) * direction
            energy = renewed
    return solution


def per_device(basis, mobility, accumulation, residual):
    stacked = jnp.concatenate([basis, mobility[None]], axis=0)
    padded = with_halo(stacked, (("gx", 3), ("gy", 2)), 1)
    padded_basis = padded[:-1].astype(jnp.float32)
    padded_mobility = padded[-1].astype(jnp.float32)
    blocks = face_blocks(padded_basis, padded_mobility, accumulation)
    interior = padded_basis[:, :, 1:-1, 1:-1]
    coarse_source = jnp.einsum("kzyx,zyx->k", interior, residual, precision=lax.Precision.HIGHEST)
    every_block, every_source = (
        lax.all_gather(blocks[None], ("gx", "gy"), axis=0, tiled=True),
        lax.all_gather(coarse_source[None], ("gx", "gy"), axis=0, tiled=True),
    )
    count_x = lax.axis_size("gx")
    count_y = lax.axis_size("gy")
    solution_grid = coarse_solve(
        every_block.reshape(count_x, count_y, 5, K, K), every_source.reshape(count_x, count_y, K)
    )
    anchor = jnp.zeros((), jnp.int32)
    solution = lax.dynamic_slice(
        solution_grid, (lax.axis_index("gx"), lax.axis_index("gy"), anchor), (1, 1, K)
    )[0, 0]
    correction = jnp.einsum("kzyx,k->zyx", interior, solution, precision=lax.Precision.HIGHEST)
    return (correction, solution.reshape(1, 1, K))


def solution(mesh):
    placed = (
        P(None, None, "gy", "gx"),
        P(None, "gy", "gx"),
        P(None, "gy", "gx"),
        P(None, "gy", "gx"),
    )
    return jax.shard_map(
        per_device,
        mesh=mesh,
        in_specs=placed,
        out_specs=(P(None, "gy", "gx"), P("gx", "gy", None)),
        check_vma=False,
    )
```

profile of v0, /device:TPU:0, one launch (start us, length us, event | category | flops | bytes accessed | tf_op | source)
XLA Modules:
  0.0 184.5 jit_solution(14101931282482318440)
XLA Ops:
  0.7 1.6 slice_maximum_fusion
  2.3 0.5 copy.293
  2.7 1.3 collective-permute-start.1
  4.0 0.5 copy.292
  4.5 3.0 %collective-permute-start = (bf16[17,4,32,1]{2,1,3,0:T(4,128)(2,1)S(1)}, bf16[17,4,32,1]{2,1,3,0:T(4,128)(2,1)S(1)}, u32[]{:S(2)}, u32[]{:S(2)}) collective-permute-start(bf16[17,4,32,1]{2,1,3,0:T(4,128)(2,1)S(1)} %copy.292), channel_id=1, source_target_pairs={{0,4},{4,8},{8,12},{12,16},{16,20},{20,24},{24,28},{1,5},{5,9},{9,... | collective-permute-start | bytes 13064 | tf_op jit(solution)/shard_map/ppermute | solution.py:21
  7.6 0.2 fusion.65
  7.8 0.9 convolution_bitcast_fusion.12
  9.0 42.4 %all-reduce.2 = f32[512]{0:T(512)S(1)} all-reduce(f32[512]{0:T(512)S(1)} %dynamic-update-slice), channel_id=2, replica_groups=mesh['gx'=8,'gy'=4] {'gx','gy'}, use_global_device_ids=true, to_apply=%add.2 | all-reduce | flops 512 | bytes 4096
  51.7 0.6 copy-done.4
  52.3 0.5 copy.240
  52.8 0.5 copy.239
  53.4 0.4 pad_maximum_fusion.5
  53.8 1.3 collective-permute-start.3
  55.1 4.7 %collective-permute-start.2 = (bf16[17,4,1,130]{3,1,2,0:T(4,128)(2,1)S(1)}, bf16[17,4,1,130]{3,1,2,0:T(4,128)(2,1)S(1)}, u32[]{:S(2)}, u32[]{:S(2)}) collective-permute-start(bf16[17,4,1,130]{3,1,2,0:T(4,128)(2,1)S(1)} %copy.241), channel_id=1, source_target_pairs={{0,1},{1,2},{2,3},{4,5},{5,6},{6,7},{8,9},{9,10},{10,11},{12,13},{... | collective-permute-start | bytes 53048 | tf_op jit(solution)/shard_map/ppermute | solution.py:21
  59.9 0.6 multiply_reduce_fusion.3
  60.5 1.1 copy.270
  61.6 1.1 copy.299
  62.7 1.1 copy.298
  64.5 2.5 %pad_maximum_fusion = bf16[17,4,34,130]{3,2,1,0:T(8,128)(2,1)} fusion(bf16[17,4,1,130]{3,2,1,0:T(2,128)(2,1)S(1)} %copy.244, bf16[17,4,32,1]{3,2,1,0:T(8,128)(2,1)S(1)} %copy.240, bf16[1,4,32,128]{3,2,1,0:T(8,128)(2,1)S(1)} %bitcast.222, bf16[16,4,32,128]{3,2,1,0:T(8,128)(2,1)S(1)} %copy-done.1, bf16[17,4,32,1]{3,2,1,0:T(8,128)(2,1)S(1)} %copy.239, ...), kind=kLoop, calls=%fused_computation | loop fusion | flops 3606720 | bytes 1202240 | tf_op jit(solution)/shard_map/concatenate | solution.py:23
  67.2 0.9 copy.288
  68.2 0.8 fusion.67
  68.9 0.8 add_divide_fusion.1
  69.8 1.6 slice_convert_fusion
  71.6 1.5 convolution_bitcast_fusion.6
  73.1 1.5 convolution_bitcast_fusion.7
  74.6 0.8 fusion.57
  75.4 1.8 slice_multiply_fusion.1
  77.1 1.7 copy.265
  78.8 1.7 copy.261
  80.5 0.9 divide_multiply_fusion
  81.4 0.5 broadcast_multiply_fusion.2
  81.8 0.3 copy-done.3
  82.2 0.6 broadcast_multiply_fusion
  83.0 0.3 slice_multiply_fusion.2
  83.4 1.9 %convolution_bitcast_fusion.1 = f32[16,16]{1,0:T(8,128)S(1)} fusion(f32[16,4,32,128]{3,2,1,0:T(8,128)S(1)} %slice_multiply_fusion.2, bf16[16,4,32,128]{3,2,1,0:T(8,128)(2,1)S(1)} %copy-done.1), kind=kOutput, calls=%fused_computation.3 | convolution fusion | flops 50331648 | bytes 1573888 | tf_op jit(solution)/shard_map/kzyx,lzyx->kl/dot_general | solution.py:32
  85.3 0.6 broadcast_multiply_fusion.1
  86.3 2.0 %convolution_bitcast_fusion = f32[16,16]{1,0:T(8,128)S(1)} fusion(f32[16,3,32,128]{3,2,1,0:T(8,128)S(1)} %get-tuple-element.9, f32[16,3,32,128]{3,2,1,0:T(8,128)S(1)} %get-tuple-element.8), kind=kOutput, calls=%fused_computation.2 | convolution fusion | flops 37748736 | bytes 1573888 | tf_op jit(solution)/shard_map/kzyx,lzyx->kl/dot_general | solution.py:32
  88.4 2.9 %convolution_bitcast_fusion.10 = f32[16,16]{1,0:T(8,128)S(1)} fusion(f32[16,4,31,128]{3,2,1,0:T(8,128)S(1)} %get-tuple-element.7, f32[16,4,31,128]{3,2,1,0:T(8,128)S(1)} %get-tuple-element.6), kind=kOutput, calls=%fused_computation.24 | convolution fusion | flops 48758784 | bytes 2032640 | tf_op jit(solution)/shard_map/kzyx,lzyx->kl/dot_general | solution.py:32
  91.3 2.9 %fusion.20 = f32[5,16,16]{2,1,0:T(8,128)S(1)} fusion(f32[16,16]{1,0:T(8,128)S(1)} %copy-done.13, f32[16,16]{1,0:T(8,128)S(1)} %copy-done.14, f32[16,16]{1,0:T(8,128)S(1)} %convolution_bitcast_fusion.8, f32[16,16]{1,0:T(8,128)S(1)} %convolution_bitcast_fusion.9, f32[16,16]{1,0:T(8,128)S(1)} %convolution_bitcast_fusion, ...), kind=kOutput, calls=%fused_computation.34 | convolution fusion | flops 49940224 | bytes 2096128 | tf_op jit(solution)/shard_map/kzyx,lzyx->kl/dot_general | solution.py:32
  94.6 0.9 slice.251
  95.5 0.9 slice.252
  96.5 77.7 %all-gather.1 = f32[160,16,16]{2,1,0:T(8,128)S(1)} all-gather(f32[5,16,16]{2,1,0:T(8,128)S(1)} %fusion.2), channel_id=3, replica_groups=mesh['gx'=8,'gy'=4] {'gx','gy'}, dimensions={0}, use_global_device_ids=true | all-gather | bytes 168960 | tf_op jit(solution)/shard_map/all_gather | solution.py:116
  174.3 1.9 %fusion.32 = f32[8,4,1,16,1]{3,2,4,1,0:T(1,128)S(1)} fusion(f32[8,4,5,16,16]{4,3,2,1,0:T(8,128)S(1)} %bitcast.214, f32[8,4,5,16,1]{3,1,0,2,4:T(4,128)S(1)} %bitcast.228), kind=kOutput, calls=%fused_computation.60 | convolution fusion | flops 491520 | bytes 176128 | tf_op jit(solution)/shard_map/abnkl,abnl->abk/dot_general | solution.py:87
  176.2 0.6 multiply_reduce_fusion.2
  178.1 0.6 multiply_reduce_fusion.1
  179.5 1.9 %fusion.30 = f32[8,4,1,16,1]{3,2,4,1,0:T(1,128)S(1)} fusion(f32[8,4,5,16,16]{4,3,2,1,0:T(8,128)S(1)} %bitcast.215, f32[8,4,5,16,1]{3,1,0,2,4:T(4,128)S(1)} %bitcast.229), kind=kOutput, calls=%fused_computation.58 | convolution fusion | flops 491520 | bytes 176128 | tf_op jit(solution)/shard_map/abnkl,abnl->abk/dot_general | solution.py:87
  181.4 0.6 multiply_reduce_fusion
  183.3 1.2 fusion.28
  (70 shorter events, 2.5 us)
Async XLA Ops:
  0.6 7.2 %copy-start = (f32[4,32,128]{2,1,0:T(8,128)S(1)}, f32[4,32,128]{2,1,0:T(8,128)}, u32[]{:S(2)}) copy-start(f32[4,32,128]{2,1,0:T(8,128)} %param.7) | copy-start | bytes 196612
  0.6 6.9 %copy-start.1 = (bf16[16,4,32,128]{3,2,1,0:T(8,128)(2,1)S(1)}, bf16[16,4,32,128]{3,2,1,0:T(8,128)(2,1)}, u32[]{:S(2)}) copy-start(bf16[16,4,32,128]{3,2,1,0:T(8,128)(2,1)} %param.4) | copy-start | bytes 1572868
  2.7 49.6 %collective-permute-start.1 = (bf16[17,4,32,1]{2,1,3,0:T(4,128)(2,1)S(1)}, bf16[17,4,32,1]{2,1,3,0:T(4,128)(2,1)S(1)}, u32[]{:S(2)}, u32[]{:S(2)}) collective-permute-start(bf16[17,4,32,1]{2,1,3,0:T(4,128)(2,1)S(1)} %copy.293), channel_id=1, source_target_pairs={{4,0},{8,4},{12,8},{16,12},{20,16},{24,20},{28,24},{5,1},{9,5},{13... | collective-permute-start | bytes 13064 | tf_op jit(solution)/shard_map/ppermute | solution.py:22
  4.5 48.3 %collective-permute-start = (bf16[17,4,32,1]{2,1,3,0:T(4,128)(2,1)S(1)}, bf16[17,4,32,1]{2,1,3,0:T(4,128)(2,1)S(1)}, u32[]{:S(2)}, u32[]{:S(2)}) collective-permute-start(bf16[17,4,32,1]{2,1,3,0:T(4,128)(2,1)S(1)} %copy.292), channel_id=1, source_target_pairs={{0,4},{4,8},{8,12},{12,16},{16,20},{20,24},{24,28},{1,5},{5,9},{9,... | collective-permute-start | bytes 13064 | tf_op jit(solution)/shard_map/ppermute | solution.py:21
  7.8 45.5 %copy-start.2 = (bf16[4,32,128]{2,1,0:T(8,128)(2,1)S(1)}, bf16[4,32,128]{2,1,0:T(8,128)(2,1)}, u32[]{:S(2)}) copy-start(bf16[4,32,128]{2,1,0:T(8,128)(2,1)} %param.5) | copy-start | bytes 98308
  51.7 0.6 copy-start.4
  52.3 12.1 %copy-start.8 = (bf16[17,4,32,1]{2,1,3,0:T(4,128)(2,1)}, bf16[17,4,32,1]{2,1,3,0:T(4,128)(2,1)S(1)}, u32[]{:S(2)}) copy-start(bf16[17,4,32,1]{2,1,3,0:T(4,128)(2,1)S(1)} %collective-permute-done.1) | copy-start | bytes 13060
  52.8 11.5 %copy-start.9 = (bf16[17,4,32,1]{2,1,3,0:T(4,128)(2,1)}, bf16[17,4,32,1]{2,1,3,0:T(4,128)(2,1)S(1)}, u32[]{:S(2)}) copy-start(bf16[17,4,32,1]{2,1,3,0:T(4,128)(2,1)S(1)} %collective-permute-done) | copy-start | bytes 13060
  53.8 10.6 %collective-permute-start.3 = (bf16[17,4,1,130]{3,1,2,0:T(4,128)(2,1)S(1)}, bf16[17,4,1,130]{3,1,2,0:T(4,128)(2,1)S(1)}, u32[]{:S(2)}, u32[]{:S(2)}) collective-permute-start(bf16[17,4,1,130]{3,1,2,0:T(4,128)(2,1)S(1)} %copy.242), channel_id=1, source_target_pairs={{1,0},{2,1},{3,2},{5,4},{6,5},{7,6},{9,8},{10,9},{11,10},{13,12},{... | collective-permute-start | bytes 53048 | tf_op jit(solution)/shard_map/ppermute | solution.py:22
  55.1 9.3 %collective-permute-start.2 = (bf16[17,4,1,130]{3,1,2,0:T(4,128)(2,1)S(1)}, bf16[17,4,1,130]{3,1,2,0:T(4,128)(2,1)S(1)}, u32[]{:S(2)}, u32[]{:S(2)}) collective-permute-start(bf16[17,4,1,130]{3,1,2,0:T(4,128)(2,1)S(1)} %copy.241), channel_id=1, source_target_pairs={{0,1},{1,2},{2,3},{4,5},{5,6},{6,7},{8,9},{9,10},{10,11},{12,13},{... | collective-permute-start | bytes 53048 | tf_op jit(solution)/shard_map/ppermute | solution.py:21
  64.4 2.6 %copy-start.6 = (bf16[17,4,1,130]{3,1,2,0:T(4,128)(2,1)}, bf16[17,4,1,130]{3,1,2,0:T(4,128)(2,1)S(1)}, u32[]{:S(2)}) copy-start(bf16[17,4,1,130]{3,1,2,0:T(4,128)(2,1)S(1)} %collective-permute-done.3) | copy-start | bytes 53044
  64.5 2.5 %copy-start.7 = (bf16[17,4,1,130]{3,1,2,0:T(4,128)(2,1)}, bf16[17,4,1,130]{3,1,2,0:T(4,128)(2,1)S(1)}, u32[]{:S(2)}) copy-start(bf16[17,4,1,130]{3,1,2,0:T(4,128)(2,1)S(1)} %collective-permute-done.2) | copy-start | bytes 53044
  81.3 0.8 copy-start.3
  82.2 0.8 copy-start.10
  85.3 0.7 copy-start.11
  85.3 0.8 copy-start.12
  88.3 3.0 %copy-start.13 = (f32[16,16]{1,0:T(8,128)S(1)}, f32[16,16]{1,0:T(8,128)}, u32[]{:S(2)}) copy-start(f32[16,16]{1,0:T(8,128)} %convolution_bitcast_fusion.6) | copy-start | bytes 3076
  88.3 3.0 %copy-start.14 = (f32[16,16]{1,0:T(8,128)S(1)}, f32[16,16]{1,0:T(8,128)}, u32[]{:S(2)}) copy-start(f32[16,16]{1,0:T(8,128)} %convolution_bitcast_fusion.7) | copy-start | bytes 3076
  91.3 3.0 %slice-start.1 = ((bf16[17,4,32,1]{2,1,3,0:T(4,128)(2,1)}), bf16[16,4,32,1]{2,1,3,0:T(4,128)(2,1)S(1)}, s32[]{:S(2)}) async-start(bf16[17,4,32,1]{2,1,3,0:T(4,128)(2,1)} %copy-done.9), calls=%async_computation.1 | async-start | bytes 32768 | tf_op jit(solution)/shard_map/slice | solution.py:51
  91.3 3.1 %slice-start = ((bf16[17,4,32,1]{2,1,3,0:T(4,128)(2,1)}), bf16[16,4,32,1]{2,1,3,0:T(4,128)(2,1)S(1)}, s32[]{:S(2)}) async-start(bf16[17,4,32,1]{2,1,3,0:T(4,128)(2,1)} %copy-done.8), calls=%async_computation | async-start | bytes 32768 | tf_op jit(solution)/shard_map/slice | solution.py:57
  91.3 82.9 %copy-start.5 = (f32[8,4,5,16]{3,1,0,2:T(4,128)S(1)}, f32[8,4,5,16]{3,1,0,2:T(4,128)}, u32[]{:S(2)}) copy-start(f32[8,4,5,16]{3,1,0,2:T(4,128)} %copy-done.4) | copy-start | bytes 30724
  183.3 1.2 copy-start.15
where the time goes:
time: 185 us
  blocking collectives  120 us (65%)
  matrix products  19.4 us (10%)
  other arithmetic  15.2 us (8%)
  local copies, waits for them, and re-layouts  14.4 us (8%)
  starting transfers between devices  10.3 us (6%)
  between operations  4.99 us (3%)
    all_gather x1, blocking collectives, per_device(): lax.all_gather(blocks[None], ('gx', 'gy'), axis=0, tiled=True)  77.7 us
    unnamed x1, blocking collectives  42.4 us
    dot_general x12, matrix products, gram_sum(): jnp.einsum('kzyx,lzyx->kl', weighted, other, precision=lax.Precision.HIGH...  13.5 us
    ppermute x2, starting transfers between devices, with_halo(): before = lax.ppermute(last, axis, up)  7.76 us
    unnamed x46, local copies, waits for them, and re-layouts  5.82 us
    dot_general x2, matrix products, coarse_apply(): jnp.einsum('abnkl,abnl->abk', blocks, beside, precision=lax.Precision.HIG...  3.82 us
  transfers between devices with their start and end apart: 4, of which 0 were waited for; matrix products, arithmetic and copies ran while one was open for 4% of the time, Pallas kernels for 0%

commit v1 on v0

v1 whole, which is shorter than its diff:
```python
import functools

import jax
import jax.numpy as jnp
from jax import lax
from jax.experimental import pallas as pl
from jax.experimental.pallas import tpu as pltpu
from jax.sharding import PartitionSpec as P

ITERS = 2
EPSILON = 1e-6
VERTICAL_RATIO = 0.1
TINY = 1e-30
TILE = 16
LANES = 128

F32 = jnp.float32
BF16 = jnp.bfloat16
VMEM = pl.BlockSpec(memory_space=pltpu.VMEM)


def iota(shape, dim):
    return lax.broadcasted_iota(jnp.int32, shape, dim)


def round_up(n, m):
    return (n + m - 1) // m * m


def harmonic(first, second):
    return 2.0 * first * second / jnp.maximum(first + second, TINY)


def dot_nt(a, b):
    return lax.dot_general(a, b, (((1,), (1,)), ((), ())), preferred_element_type=F32)


def three_terms(x):
    high = x.astype(BF16).astype(F32)
    rest = x - high
    middle = rest.astype(BF16).astype(F32)
    return high, middle, rest - middle


def position(axis, count):
    index = lax.axis_index(axis)
    odd = lax.rem(index, 2) == 1
    inner = jnp.logical_and(index > 0, index < count - 1)
    return odd, inner


def edges_kernel(counts, basis_ref, mobility_ref, residual_ref, x1_ref, x2_ref, y1_ref, y2_ref, b_ref):
    k_count, cz, cy, cx = basis_ref.shape
    cells = cz * cy
    odd_x, inner_x = position("gx", counts[0])
    odd_y, inner_y = position("gy", counts[1])

    residual = residual_ref[...]
    row = iota((k_count, cx), 0)
    partial = jnp.zeros((k_count, cx), F32)
    for k in range(k_count):
        product = basis_ref[k].astype(F32) * residual
        total = jnp.sum(jnp.sum(product, axis=0), axis=0, keepdims=True)
        partial = jnp.where(row == k, total, partial)
    b = jnp.broadcast_to(jnp.sum(partial, axis=1, keepdims=True), (k_count, LANES))
    b_ref[...] = b

    first = jnp.where(odd_x, 0, cx - 1)
    second = jnp.where(odd_x, cx - 1, 0)
    pick_row = iota((2 * k_count, cx), 0)
    pick_lane = iota((2 * k_count, cx), 1)
    wanted = pick_lane == jnp.where(pick_row < k_count, first, second)
    pick_k = jnp.where(pick_row < k_count, pick_row, pick_row - k_count)
    columns = jnp.zeros((2 * k_count, cells), F32)
    for k in range(k_count):
        pick = jnp.where(jnp.logical_and(wanted, pick_k == k), 1.0, 0.0).astype(BF16)
        columns = columns + dot_nt(pick, basis_ref[k].reshape(cells, cx))
    pick_row = iota((TILE, cx), 0)
    pick_lane = iota((TILE, cx), 1)
    pick = jnp.where(pick_lane == jnp.where(pick_row == 0, first, second), 1.0, 0.0).astype(BF16)
    edge_mobility = dot_nt(pick, mobility_ref[...].reshape(cells, cx))

    for number, ref in ((0, x1_ref), (1, x2_ref)):
        edge = columns[number * k_count : (number + 1) * k_count]
        ref[0:k_count, :] = edge.astype(BF16)
        field = jnp.sum(edge * b[:, :1], axis=0, keepdims=True)
        mobility = edge_mobility[number : number + 1]
        if number == 1:
            mobility = jnp.where(inner_x, mobility, 0.0)
        row = iota((TILE, cells), 0)
        extra = jnp.zeros((TILE, cells), F32)
        for place, value in enumerate((mobility, *three_terms(field))):
            extra = jnp.where(row == place, value, extra)
        ref[k_count : k_count + TILE, :] = extra.astype(BF16)

    row = iota((k_count, cx), 0)
    extra_rows = round_up(4 * cz, TILE)
    extra_row = iota((extra_rows, cx), 0)
    extras = [jnp.zeros((extra_rows, cx), F32) for _ in range(2)]
    for z in range(cz):
        low = jnp.zeros((k_count, cx), F32)
        high = jnp.zeros((k_count, cx), F32)
        for k in range(k_count):
            low = jnp.where(row == k, basis_ref[k, z, 0:TILE, :].astype(F32)[0:1], low)
            high = jnp.where(row == k, basis_ref[k, z, cy - TILE : cy, :].astype(F32)[TILE - 1 : TILE], high)
        low_mobility = mobility_ref[z, 0:TILE, :].astype(F32)[0:1]
        high_mobility = mobility_ref[z, cy - TILE : cy, :].astype(F32)[TILE - 1 : TILE]
        for number, ref in ((0, y1_ref), (1, y2_ref)):
            use_low = odd_y if number == 0 else jnp.logical_not(odd_y)
            edge = jnp.where(use_low, low, high)
            mobility = jnp.where(use_low, low_mobility, high_mobility)
            if number == 1:
                mobility = jnp.where(inner_y, mobility, 0.0)
            ref[z * k_count : (z + 1) * k_count, :] = edge.astype(BF16)
            field = jnp.sum(edge * b[:, :1], axis=0, keepdims=True)
            for place, value in enumerate((mobility, *three_terms(field))):
                extras[number] = jnp.where(extra_row == place * cz + z, value, extras[number])
    for number, ref in ((0, y1_ref), (1, y2_ref)):
        ref[cz * k_count : cz * k_count + extra_rows, :] = extras[number].astype(BF16)


def gram_kernel(basis_ref, mobility_ref, accumulation_ref, gram_ref, left_ref):
    k_count, cz, cy, cx = basis_ref.shape
    mobility = mobility_ref[...].astype(F32)
    accumulation = accumulation_ref[...]
    shape = mobility.shape
    along_x = jnp.where(iota(shape, 2) < cx - 1, harmonic(mobility, pltpu.roll(mobility, cx - 1, 2)), 0.0)
    along_y = jnp.where(iota(shape, 1) < cy - 1, harmonic(mobility, pltpu.roll(mobility, cy - 1, 1)), 0.0)
    along_z = VERTICAL_RATIO * harmonic(mobility[:-1], mobility[1:])
    rows = k_count * TILE
    strips = [(z, y) for z in range(cz) for y in range(0, cy, TILE)]
    for k in range(k_count):
        field = basis_ref[k].astype(F32)
        flow_x = along_x * (field - pltpu.roll(field, cx - 1, 2))
        image = accumulation * field + flow_x - pltpu.roll(flow_x, 1, 2)
        flow_y = along_y * (field - pltpu.roll(field, cy - 1, 1))
        image = image + flow_y - pltpu.roll(flow_y, 1, 1)
        flow_z = along_z * (field[:-1] - field[1:])
        nothing = jnp.zeros_like(field[:1])
        image = image + jnp.concatenate([flow_z, nothing], axis=0) - jnp.concatenate([nothing, flow_z], axis=0)
        high = image.astype(BF16)
        low = (image - high.astype(F32)).astype(BF16)
        for place, (z, y) in enumerate(strips):
            lanes = slice(place * cx, (place + 1) * cx)
            left_ref[k * TILE : (k + 1) * TILE, lanes] = high[z, y : y + TILE]
            left_ref[rows + k * TILE : rows + (k + 1) * TILE, lanes] = low[z, y : y + TILE]
    total = jnp.zeros((2 * rows, rows), F32)
    for place, (z, y) in enumerate(strips):
        right = basis_ref[:, z, y : y + TILE, :].reshape(rows, cx)
        total = total + dot_nt(left_ref[:, place * cx : (place + 1) * cx], right)
    total = total[:rows] + total[rows:]
    same = lax.rem(iota((rows, rows), 0), TILE) == lax.rem(iota((rows, rows), 1), TILE)
    total = jnp.where(same, total, 0.0)
    gram_ref[...] = jnp.sum(total.reshape(k_count, TILE, rows), axis=1)


def couple_kernel(
    cz, counts, x1_ref, x2_ref, y1_ref, y2_ref, rx1_ref, rx2_ref, ry1_ref, ry2_ref, b_ref, gram_ref, out_ref
):
    k_count = b_ref.shape[0]
    odd_x, _ = position("gx", counts[0])
    odd_y, _ = position("gy", counts[1])
    b = b_ref[...]
    gram = gram_ref[...]
    wide = gram.shape[1]
    spread = iota((k_count, wide), 1) // TILE == iota((k_count, wide), 0)

    def as_row(column):
        return jnp.sum(jnp.where(spread, column[:, :1], 0.0), axis=0, keepdims=True)

    def unpack(ref, layers):
        blocks = [ref[z * k_count : (z + 1) * k_count, :].astype(F32) for z in range(layers)]
        start = layers * k_count
        extra = ref[start : start + round_up(4 * layers, TILE), :].astype(F32)
        mobility, high, middle, low = (extra[n * layers : (n + 1) * layers] for n in range(4))
        return blocks, mobility, high + middle + low

    faces = []
    for own_ref, other_ref, layers in (
        (x1_ref, rx1_ref, 1),
        (x2_ref, rx2_ref, 1),
        (y1_ref, ry1_ref, cz),
        (y2_ref, ry2_ref, cz),
    ):
        own, own_mobility, own_field = unpack(own_ref, layers)
        other, other_mobility, other_field = unpack(other_ref, layers)
        faces.append((own, other, harmonic(own_mobility, other_mobility), own_field, other_field))

    b_row = as_row(b)
    along = jnp.zeros((k_count, LANES), F32)
    for own, _, conductance, own_field, other_field in faces:
        flow = conductance * (own_field - other_field)
        for z, block in enumerate(own):
            along = along + block * flow[z : z + 1]
    image = jnp.sum(along, axis=1, keepdims=True) + jnp.sum(gram * b_row, axis=1, keepdims=True)
    b_col = b[:, :1]
    source_square = jnp.sum(b_col * b_col, axis=0, keepdims=True)
    source_image = jnp.sum(b_col * image, axis=0, keepdims=True)
    quotient = source_image / jnp.maximum(source_square, TINY)
    v_col = image - quotient * b_col
    v_row = as_row(v_col)

    squares = [jnp.zeros((1, LANES), F32) for _ in range(3)]
    toward = []
    for own, other, conductance, own_field, _ in faces:
        v_field = jnp.concatenate([jnp.sum(block * v_col, axis=0, keepdims=True) for block in own], axis=0)
        flow_b = conductance * own_field
        flow_v = conductance * v_field
        for n, value in enumerate((flow_b * own_field, flow_b * v_field, flow_v * v_field)):
            squares[n] = squares[n] + jnp.sum(value, axis=0, keepdims=True)
        toward.append((other, flow_b, flow_v))
    for n, (left, right) in enumerate(((b_col, b_row), (b_col, v_row), (v_col, v_row))):
        value = jnp.sum(left * gram, axis=0, keepdims=True) * right
        for start in range(0, wide, LANES):
            squares[n] = squares[n] + value[:, start : start + LANES]
    squares = [jnp.sum(value, axis=1, keepdims=True) for value in squares]

    columns = [b_col, v_col]
    for first, second, odd in ((toward[0], toward[1], odd_x), (toward[2], toward[3], odd_y)):
        for which in (1, 2):
            product = jnp.zeros((k_count, LANES), F32)
            for z in range(len(first[0])):
                block = jnp.where(odd, second[0][z], first[0][z])
                flow = jnp.where(odd, second[which], first[which])
                product = product - block * flow[z : z + 1]
            columns.append(jnp.sum(product, axis=1, keepdims=True))
    lane = iota((k_count, LANES), 1)
    own_lane = lane - iota((k_count, LANES), 0)
    placed = jnp.zeros((k_count, LANES), F32)
    for n, column in enumerate(columns):
        placed = jnp.where(own_lane == n * k_count, column, placed)
    packed = jnp.sum(placed, axis=0, keepdims=True)
    lane = iota((1, LANES), 1)
    base = len(columns) * k_count
    for n, value in enumerate((quotient, *squares, source_square, source_image)):
        packed = jnp.where(lane == base + n, value, packed)
    out_ref[...] = jnp.broadcast_to(packed, out_ref.shape)


def finish_kernel(count_y, gathered_ref, own_ref, basis_ref, correction_ref, solution_ref):
    k_count, cz, cy, cx = basis_ref.shape
    base = 6 * k_count
    every = gathered_ref[...]
    lane = iota(every.shape, 1)

    def total(x):
        return jnp.sum(jnp.sum(x, axis=0, keepdims=True), axis=1, keepdims=True)

    def shifted(x, amount):
        return pltpu.roll(x, LANES - amount, 1)

    def up_rows(x, amount):
        return jnp.concatenate([x[amount:], x[:amount]], axis=0)

    sums = jnp.sum(every, axis=0, keepdims=True)
    energy = sums[:, base + 4 : base + 5]
    step = energy / (sums[:, base + 5 : base + 6] + EPSILON)
    quotient = every[:, base : base + 1]
    beside = shifted(every, k_count)
    remainder = every - step * (quotient * every + beside)
    renewed = total(jnp.where(lane < k_count, remainder * remainder, 0.0))
    ratio = renewed / (energy + EPSILON)
    weight = 1.0 + ratio - step * quotient
    mixed = weight * every - step * beside
    direction = jnp.where(lane < k_count, mixed, 0.0)
    cross = shifted(mixed, 2 * k_count) * up_rows(direction, count_y) + shifted(mixed, 4 * k_count) * up_rows(direction, 1)
    own_part = (
        weight * weight * every[:, base + 1 : base + 2]
        - 2.0 * weight * step * every[:, base + 2 : base + 3]
        + step * step * every[:, base + 3 : base + 4]
    )
    curvature = total(2.0 * cross) + jnp.sum(own_part, axis=0, keepdims=True)
    last_step = renewed / (curvature + EPSILON)

    own = own_ref[0:1, :]
    own_weight = 1.0 + ratio - step * own[:, base : base + 1]
    own_direction = own_weight * own - step * shifted(own, k_count)
    solution = step * own + last_step * own_direction
    solution_ref[...] = solution[:, :k_count]
    spread = iota((k_count, LANES), 0) == iota((k_count, LANES), 1)
    column = jnp.sum(jnp.where(spread, solution, 0.0), axis=1, keepdims=True)
    correction = jnp.zeros((cz, cy, cx), F32)
    for k in range(k_count):
        correction = correction + basis_ref[k].astype(F32) * column[k : k + 1][None]
    correction_ref[...] = correction


def exchange(message, axis, count, second):
    if second:
        pairs = [(i, (i - 1) % count if i % 2 == 0 else (i + 1) % count) for i in range(count)]
    else:
        pairs = [(i, i ^ 1) for i in range(count)]
    return lax.ppermute(message, axis, pairs)


def per_device(counts, basis, mobility, accumulation, residual):
    k_count, cz, cy, cx = basis.shape
    devices = counts[0] * counts[1]
    x_message = jax.ShapeDtypeStruct((k_count + TILE, cz * cy), BF16)
    y_message = jax.ShapeDtypeStruct((cz * k_count + round_up(4 * cz, TILE), cx), BF16)
    x1, x2, y1, y2, b = pl.pallas_call(
        functools.partial(edges_kernel, counts),
        out_shape=(x_message, x_message, y_message, y_message, jax.ShapeDtypeStruct((k_count, LANES), F32)),
        in_specs=[VMEM] * 3,
        out_specs=(VMEM,) * 5,
    )(basis, mobility, residual)
    rx1 = exchange(x1, "gx", counts[0], False)
    rx2 = exchange(x2, "gx", counts[0], True)
    ry1 = exchange(y1, "gy", counts[1], False)
    ry2 = exchange(y2, "gy", counts[1], True)
    gram = pl.pallas_call(
        gram_kernel,
        out_shape=jax.ShapeDtypeStruct((k_count, k_count * TILE), F32),
        in_specs=[VMEM] * 3,
        out_specs=VMEM,
        scratch_shapes=[pltpu.VMEM((2 * k_count * TILE, cz * cy // TILE * cx), BF16)],
        cost_estimate=pl.CostEstimate(flops=2 * 10**9, bytes_accessed=10**6, transcendentals=0),
    )(basis, mobility, accumulation)
    row = pl.pallas_call(
        functools.partial(couple_kernel, cz, counts),
        out_shape=jax.ShapeDtypeStruct((devices, LANES), F32),
        in_specs=[VMEM] * 10,
        out_specs=VMEM,
    )(x1, x2, y1, y2, rx1, rx2, ry1, ry2, b, gram)
    gathered = lax.all_to_all(row, ("gx", "gy"), 0, 0, tiled=True)
    correction, solution = pl.pallas_call(
        functools.partial(finish_kernel, counts[1]),
        out_shape=(jax.ShapeDtypeStruct((cz, cy, cx), F32), jax.ShapeDtypeStruct((1, k_count), F32)),
        in_specs=[VMEM] * 3,
        out_specs=(VMEM, VMEM),
    )(gathered, row, basis)
    return correction, solution.reshape(1, 1, k_count)


def solution(mesh):
    counts = (mesh.shape["gx"], mesh.shape["gy"])
    placed = (
        P(None, None, "gy", "gx"),
        P(None, "gy", "gx"),
        P(None, "gy", "gx"),
        P(None, "gy", "gx"),
    )
    return jax.shard_map(
        functools.partial(per_device, counts),
        mesh=mesh,
        in_specs=placed,
        out_specs=(P(None, "gy", "gx"), P("gx", "gy", None)),
        check_vma=False,
    )
```

time: 185 us -> 29.6 us (0.16)
  blocking collectives: 120 us -> 10.2 us
  matrix products: 19.4 us -> 0 us
  other arithmetic: 15.2 us -> 0 us
  local copies, waits for them, and re-layouts: 14.4 us -> 0.61 us
  Pallas kernels: 0 us -> 9.5 us
  between operations: 4.99 us -> 0.66 us
  starting transfers between devices: 10.3 us -> 8.06 us
    all_gather x1 -> x0, blocking collectives: 77.7 us -> none  [per_device(): lax.all_gather(blocks[None], ('gx', 'gy'), axis=0, tiled=True)]
    unnamed x1 -> x0, blocking collectives: 42.4 us -> none
    dot_general x16 -> x0, matrix products: 19.4 us -> none  [the longest x12 13.5 us: gram_sum(): jnp.einsum('kzyx,lzyx->kl', weighted, other, precision=lax.Precision.HIGH...]
    all_to_all x0 -> x1, blocking collectives: none -> 10.2 us  [per_device(): gathered = lax.all_to_all(row, ('gx', 'gy'), 0, 0, tiled=True)]
    pallas_call x0 -> x4, Pallas kernels: none -> 9.5 us  [the longest x1 3.06 us: per_device(): pl.pallas_call(gram_kernel, out_shape=jax.ShapeDtypeStruct((k_count, k_co...]
    mul x9 -> x0, other arithmetic: 5.77 us -> none  [the longest x4 2.86 us: face_blocks(): weighted = edge_cells * harmonic(edge_mobility, ghost_mobility)]
    unnamed x46 -> x8, local copies, waits for them, and re-layouts: 5.82 us -> 0.61 us
    concatenate x2 -> x0, other arithmetic: 4.06 us -> none  [the longest x1 2.46 us: with_halo(): x = jnp.concatenate([before, x, after], axis=dim)]
  transfers between devices with their start and end apart: 4 -> 4, of which waited for: 0 -> 1; matrix products, arithmetic and copies ran while one was open for 4% -> 0% of each run, Pallas kernels for 0% -> 10%
where the time goes in v1:
time: 29.6 us; the launch traced here: 29.3 us
  blocking collectives  10.2 us (34%)
  Pallas kernels  9.5 us (32%)
  starting transfers between devices  8.06 us (27%)
  between operations  0.66 us (2%)
  local copies, waits for them, and re-layouts  0.61 us (2%)
    all_to_all x1, blocking collectives, per_device(): gathered = lax.all_to_all(row, ('gx', 'gy'), 0, 0, tiled=True)  10.2 us
    ppermute x4, starting transfers between devices, exchange(): return lax.ppermute(message, axis, pairs)  8.06 us
    pallas_call x1, Pallas kernels, per_device(): pl.pallas_call(gram_kernel, out_shape=jax.ShapeDtypeStruct((k_count, k_co...  3.06 us
    pallas_call x1, Pallas kernels, per_device(): pl.pallas_call(functools.partial(finish_kernel, counts[1]), out_shape=(ja...  2.48 us
    pallas_call x1, Pallas kernels, per_device(): pl.pallas_call(functools.partial(edges_kernel, counts), out_shape=(x_mess...  2.15 us
    pallas_call x1, Pallas kernels, per_device(): pl.pallas_call(functools.partial(couple_kernel, cz, counts), out_shape=ja...  1.81 us
    unnamed x8, local copies, waits for them, and re-layouts  0.61 us
  transfers between devices with their start and end apart: 4, of which 1 were waited for; matrix products, arithmetic and copies ran while one was open for 0% of the time, Pallas kernels for 10%

profile of v1, /device:TPU:0, one launch (start us, length us, event | category | flops | bytes accessed | tf_op | source)
XLA Modules:
  0.0 29.3 jit_solution(1714841984750947537)
XLA Ops:
  0.6 2.1 %shard_map.59 = (bf16[32,128]{1,0:T(8,128)(2,1)}, bf16[32,128]{1,0:T(8,128)(2,1)}, bf16[80,128]{1,0:T(8,128)(2,1)}, bf16[80,128]{1,0:T(8,128)(2,1)}, f32[16,128]{1,0:T(8,128)}) custom-call(bf16[16,4,32,128]{3,2,1,0:T(8,128)(2,1)} %basis_ref.5, bf16[4,32,128]{2,1,0:T(8,128)(2,1)} %mobility_ref.3, f32[4,32,128]{2,1,0:T(8,128)} %residual_ref.1), custom_call_target="tpu_custom_call" | custom-call | tf_op jit(solution)/shard_map/pallas_call | solution.py:301
  2.8 0.5 %collective-permute-start = (bf16[32,128]{1,0:T(8,128)(2,1)}, bf16[32,128]{1,0:T(8,128)(2,1)S(1)}, u32[]{:S(2)}, u32[]{:S(2)}) collective-permute-start(bf16[32,128]{1,0:T(8,128)(2,1)} %get-tuple-element.9.x1_ref), channel_id=1, source_target_pairs={{0,4},{4,0},{8,12},{12,8},{16,20},{20,16},{24,28},{28,24},{1,5},{5... | collective-permute-start | bytes 24584 | tf_op jit(solution)/shard_map/ppermute | solution.py:293
  3.2 3.6 %collective-permute-start.1 = (bf16[32,128]{1,0:T(8,128)(2,1)}, bf16[32,128]{1,0:T(8,128)(2,1)S(1)}, u32[]{:S(2)}, u32[]{:S(2)}) collective-permute-start(bf16[32,128]{1,0:T(8,128)(2,1)} %get-tuple-element.10.x2_ref), channel_id=1, source_target_pairs={{0,28},{4,8},{8,4},{12,16},{16,12},{20,24},{24,20},{28,0},{1,29},{... | collective-permute-start | bytes 24584 | tf_op jit(solution)/shard_map/ppermute | solution.py:293
  6.8 1.6 %collective-permute-start.2 = (bf16[80,128]{1,0:T(8,128)(2,1)}, bf16[80,128]{1,0:T(8,128)(2,1)S(1)}, u32[]{:S(2)}, u32[]{:S(2)}) collective-permute-start(bf16[80,128]{1,0:T(8,128)(2,1)} %get-tuple-element.11.y1_ref), channel_id=1, source_target_pairs={{0,1},{1,0},{2,3},{3,2},{4,5},{5,4},{6,7},{7,6},{8,9},{9,8},{10,11... | collective-permute-start | bytes 61448 | tf_op jit(solution)/shard_map/ppermute | solution.py:293
  8.4 2.5 %collective-permute-start.3 = (bf16[80,128]{1,0:T(8,128)(2,1)}, bf16[80,128]{1,0:T(8,128)(2,1)S(1)}, u32[]{:S(2)}, u32[]{:S(2)}) collective-permute-start(bf16[80,128]{1,0:T(8,128)(2,1)} %get-tuple-element.12.y2_ref), channel_id=1, source_target_pairs={{0,3},{1,2},{2,1},{3,0},{4,7},{5,6},{6,5},{7,4},{8,11},{9,10},{10,... | collective-permute-start | bytes 61448 | tf_op jit(solution)/shard_map/ppermute | solution.py:293
  10.8 3.1 %shard_map.60.gram_ref = f32[16,256]{1,0:T(8,128)} custom-call(bf16[16,4,32,128]{3,2,1,0:T(8,128)(2,1)} %basis_ref.5, bf16[4,32,128]{2,1,0:T(8,128)(2,1)} %mobility_ref.3, f32[4,32,128]{2,1,0:T(8,128)} %accumulation_ref.1), custom_call_target="tpu_custom_call" | custom-call | flops 2000000000 | bytes 1000000 | tf_op jit(solution)/shard_map/pallas_call | solution.py:311
  13.9 0.0 collective-permute-done.rx1_ref
  13.9 0.0 copy-start.2
  13.9 0.0 collective-permute-done.1.rx2_ref
  13.9 0.0 copy-start.3
  13.9 0.0 collective-permute-done.2.ry1_ref
  13.9 0.0 copy-start
  13.9 0.2 collective-permute-done.3.ry2_ref
  14.2 0.0 copy-start.1
  14.2 0.3 %copy-done.2 = bf16[32,128]{1,0:T(8,128)(2,1)} copy-done((bf16[32,128]{1,0:T(8,128)(2,1)}, bf16[32,128]{1,0:T(8,128)(2,1)S(1)}, u32[]{:S(2)}) %copy-start.2) | copy-done | bytes 8216
  14.5 0.0 copy-done.3
  14.5 0.0 copy-done
  14.5 0.2 copy-done.1
  14.8 1.8 %shard_map.61.own_ref = f32[32,128]{1,0:T(8,128)} custom-call(bf16[32,128]{1,0:T(8,128)(2,1)} %get-tuple-element.9.x1_ref, bf16[32,128]{1,0:T(8,128)(2,1)} %get-tuple-element.10.x2_ref, bf16[80,128]{1,0:T(8,128)(2,1)} %get-tuple-element.11.y1_ref, bf16[80,128]{1,0:T(8,128)(2,1)} %get-tuple-element.12.y2_ref, bf16[32,128]{1,0:T(8,128)(2,1)} %copy-done.2, ...), custom_call_target="tpu_custom_call" | custom-call | tf_op jit(solution)/shard_map/pallas_call | solution.py:319
  16.6 10.2 %all_to_all.11 = f32[32,1,128]{2,1,0:T(1,128)} all-to-all(f32[32,1,128]{2,1,0:T(1,128)} %bitcast.5), channel_id=1, replica_groups=mesh['gx'=8,'gy'=4] {'gx','gy'}, dimensions={0} | all-to-all | bytes 32768 | tf_op jit(solution)/shard_map/all_to_all | solution.py:325
  26.8 2.5 %shard_map.62 = (f32[4,32,128]{2,1,0:T(8,128)}, f32[1,16]{1,0:T(1,128)}) custom-call(f32[32,128]{1,0:T(8,128)} %bitcast.6, f32[32,128]{1,0:T(8,128)} %shard_map.61.own_ref, bf16[16,4,32,128]{3,2,1,0:T(8,128)(2,1)} %basis_ref.5), custom_call_target="tpu_custom_call" | custom-call | tf_op jit(solution)/shard_map/pallas_call | solution.py:326
Async XLA Ops:
  2.8 11.1 %collective-permute-start = (bf16[32,128]{1,0:T(8,128)(2,1)}, bf16[32,128]{1,0:T(8,128)(2,1)S(1)}, u32[]{:S(2)}, u32[]{:S(2)}) collective-permute-start(bf16[32,128]{1,0:T(8,128)(2,1)} %get-tuple-element.9.x1_ref), channel_id=1, source_target_pairs={{0,4},{4,0},{8,12},{12,8},{16,20},{20,16},{24,28},{28,24},{1,5},{5... | collective-permute-start | bytes 24584 | tf_op jit(solution)/shard_map/ppermute | solution.py:293
  3.2 10.7 %collective-permute-start.1 = (bf16[32,128]{1,0:T(8,128)(2,1)}, bf16[32,128]{1,0:T(8,128)(2,1)S(1)}, u32[]{:S(2)}, u32[]{:S(2)}) collective-permute-start(bf16[32,128]{1,0:T(8,128)(2,1)} %get-tuple-element.10.x2_ref), channel_id=1, source_target_pairs={{0,28},{4,8},{8,4},{12,16},{16,12},{20,24},{24,20},{28,0},{1,29},{... | collective-permute-start | bytes 24584 | tf_op jit(solution)/shard_map/ppermute | solution.py:293
  6.8 7.1 %collective-permute-start.2 = (bf16[80,128]{1,0:T(8,128)(2,1)}, bf16[80,128]{1,0:T(8,128)(2,1)S(1)}, u32[]{:S(2)}, u32[]{:S(2)}) collective-permute-start(bf16[80,128]{1,0:T(8,128)(2,1)} %get-tuple-element.11.y1_ref), channel_id=1, source_target_pairs={{0,1},{1,0},{2,3},{3,2},{4,5},{5,4},{6,7},{7,6},{8,9},{9,8},{10,11... | collective-permute-start | bytes 61448 | tf_op jit(solution)/shard_map/ppermute | solution.py:293
  8.4 5.8 %collective-permute-start.3 = (bf16[80,128]{1,0:T(8,128)(2,1)}, bf16[80,128]{1,0:T(8,128)(2,1)S(1)}, u32[]{:S(2)}, u32[]{:S(2)}) collective-permute-start(bf16[80,128]{1,0:T(8,128)(2,1)} %get-tuple-element.12.y2_ref), channel_id=1, source_target_pairs={{0,3},{1,2},{2,1},{3,0},{4,7},{5,6},{6,5},{7,4},{8,11},{9,10},{10,... | collective-permute-start | bytes 61448 | tf_op jit(solution)/shard_map/ppermute | solution.py:293
  13.9 0.6 %copy-start.2 = (bf16[32,128]{1,0:T(8,128)(2,1)}, bf16[32,128]{1,0:T(8,128)(2,1)S(1)}, u32[]{:S(2)}) copy-start(bf16[32,128]{1,0:T(8,128)(2,1)S(1)} %collective-permute-done.rx1_ref) | copy-start | bytes 24580
  13.9 0.6 %copy-start.3 = (bf16[32,128]{1,0:T(8,128)(2,1)}, bf16[32,128]{1,0:T(8,128)(2,1)S(1)}, u32[]{:S(2)}) copy-start(bf16[32,128]{1,0:T(8,128)(2,1)S(1)} %collective-permute-done.1.rx2_ref) | copy-start | bytes 24580
  13.9 0.6 %copy-start = (bf16[80,128]{1,0:T(8,128)(2,1)}, bf16[80,128]{1,0:T(8,128)(2,1)S(1)}, u32[]{:S(2)}) copy-start(bf16[80,128]{1,0:T(8,128)(2,1)S(1)} %collective-permute-done.2.ry1_ref) | copy-start | bytes 61444
  14.2 0.6 %copy-start.1 = (bf16[80,128]{1,0:T(8,128)(2,1)}, bf16[80,128]{1,0:T(8,128)(2,1)S(1)}, u32[]{:S(2)}) copy-start(bf16[80,128]{1,0:T(8,128)(2,1)S(1)} %collective-permute-done.3.ry2_ref) | copy-start | bytes 61444

commit v2 on v1

--- a/solution.py
+++ b/solution.py
@@ -17,6 +17,7 @@
 F32 = jnp.float32
 BF16 = jnp.bfloat16
 VMEM = pl.BlockSpec(memory_space=pltpu.VMEM)
+PARAMS = pltpu.CompilerParams(vmem_limit_bytes=8 * 2**20)
 
 
 def iota(shape, dim):
@@ -303,6 +304,7 @@
         out_shape=(x_message, x_message, y_message, y_message, jax.ShapeDtypeStruct((k_count, LANES), F32)),
         in_specs=[VMEM] * 3,
         out_specs=(VMEM,) * 5,
+        compiler_params=PARAMS,
     )(basis, mobility, residual)
     rx1 = exchange(x1, "gx", counts[0], False)
     rx2 = exchange(x2, "gx", counts[0], True)
@@ -313,6 +315,7 @@
         out_shape=jax.ShapeDtypeStruct((k_count, k_count * TILE), F32),
         in_specs=[VMEM] * 3,
         out_specs=VMEM,
+        compiler_params=PARAMS,
         scratch_shapes=[pltpu.VMEM((2 * k_count * TILE, cz * cy // TILE * cx), BF16)],
         cost_estimate=pl.CostEstimate(flops=2 * 10**9, bytes_accessed=10**6, transcendentals=0),
     )(basis, mobility, accumulation)
@@ -321,6 +324,7 @@
         out_shape=jax.ShapeDtypeStruct((devices, LANES), F32),
         in_specs=[VMEM] * 10,
         out_specs=VMEM,
+        compiler_params=PARAMS,
     )(x1, x2, y1, y2, rx1, rx2, ry1, ry2, b, gram)
     gathered = lax.all_to_all(row, ("gx", "gy"), 0, 0, tiled=True)
     correction, solution = pl.pallas_call(
@@ -328,6 +332,7 @@
         out_shape=(jax.ShapeDtypeStruct((cz, cy, cx), F32), jax.ShapeDtypeStruct((1, k_count), F32)),
         in_specs=[VMEM] * 3,
         out_specs=(VMEM, VMEM),
+        compiler_params=PARAMS,
     )(gathered, row, basis)
     return correction, solution.reshape(1, 1, k_count)
 

time: 29.6 us -> 26.9 us (0.909)
  Pallas kernels: 9.5 us -> 3.61 us
  local copies, waits for them, and re-layouts: 0.61 us -> 2.64 us
  waiting for transfers between devices: 0.22 us -> 1.67 us
  blocking collectives: 10.2 us -> 9.82 us
    unnamed x8 -> x10, local copies, waits for them, and re-layouts: 0.61 us -> 2.64 us
    pallas_call x1, Pallas kernels: 2.15 us -> 0.47 us  [per_device(): pl.pallas_call(functools.partial(edges_kernel, counts), out_shape=(x_mess...]
    pallas_call x1, Pallas kernels: 3.06 us -> 1.4 us  [per_device(): pl.pallas_call(gram_kernel, out_shape=jax.ShapeDtypeStruct((k_count, k_co...]
    pallas_call x1, Pallas kernels: 1.81 us -> 0.35 us  [per_device(): pl.pallas_call(functools.partial(couple_kernel, cz, counts), out_shape=ja...]
    ppermute x4, waiting for transfers between devices: 0.22 us -> 1.67 us  [exchange(): return lax.ppermute(message, axis, pairs)]
    pallas_call x1, Pallas kernels: 2.48 us -> 1.4 us  [per_device(): pl.pallas_call(functools.partial(finish_kernel, counts[1]), out_shape=(ja...]
    all_to_all x1, blocking collectives: 10.2 us -> 9.82 us  [per_device(): gathered = lax.all_to_all(row, ('gx', 'gy'), 0, 0, tiled=True)]
  transfers between devices with their start and end apart: 4 -> 4, of which waited for: 1 -> 1; matrix products, arithmetic and copies ran while one was open for 0% -> 0% of each run, Pallas kernels for 10% -> 5%
where the time goes in v2:
time: 26.9 us; the launch traced here: 26.6 us
  blocking collectives  9.82 us (37%)
  starting transfers between devices  8.13 us (30%)
  Pallas kernels  3.61 us (13%)
  local copies, waits for them, and re-layouts  2.64 us (10%)
  waiting for transfers between devices  1.67 us (6%)
  between operations  0.69 us (3%)
    all_to_all x1, blocking collectives, per_device(): gathered = lax.all_to_all(row, ('gx', 'gy'), 0, 0, tiled=True)  9.82 us
    ppermute x4, starting transfers between devices, exchange(): return lax.ppermute(message, axis, pairs)  8.13 us
    unnamed x10, local copies, waits for them, and re-layouts  2.64 us
    ppermute x4, waiting for transfers between devices, exchange(): return lax.ppermute(message, axis, pairs)  1.67 us
    pallas_call x1, Pallas kernels, per_device(): pl.pallas_call(functools.partial(finish_kernel, counts[1]), out_shape=(ja...  1.4 us
    pallas_call x1, Pallas kernels, per_device(): pl.pallas_call(gram_kernel, out_shape=jax.ShapeDtypeStruct((k_count, k_co...  1.4 us
  transfers between devices with their start and end apart: 4, of which 1 were waited for; matrix products, arithmetic and copies ran while one was open for 0% of the time, Pallas kernels for 5%

profile of v2, /device:TPU:0, one launch (start us, length us, event | category | flops | bytes accessed | tf_op | source)
XLA Modules:
  0.0 26.6 jit_solution(4719251472029614528)
XLA Ops:
  0.6 0.0 copy-start
  0.6 1.0 %copy-done = bf16[16,4,32,128]{3,2,1,0:T(8,128)(2,1)S(1)} copy-done((bf16[16,4,32,128]{3,2,1,0:T(8,128)(2,1)S(1)}, bf16[16,4,32,128]{3,2,1,0:T(8,128)(2,1)}, u32[]{:S(2)}) %copy-start) | copy-done | bytes 524312
  1.7 0.0 copy-start.2
  1.7 0.8 %copy-done.2 = f32[4,32,128]{2,1,0:T(8,128)S(1)} copy-done((f32[4,32,128]{2,1,0:T(8,128)S(1)}, f32[4,32,128]{2,1,0:T(8,128)}, u32[]{:S(2)}) %copy-start.2) | copy-done | bytes 65560
  2.5 0.0 copy-start.3
  2.5 0.8 %copy-done.3 = bf16[4,32,128]{2,1,0:T(8,128)(2,1)S(1)} copy-done((bf16[4,32,128]{2,1,0:T(8,128)(2,1)S(1)}, bf16[4,32,128]{2,1,0:T(8,128)(2,1)}, u32[]{:S(2)}) %copy-start.3) | copy-done | bytes 32792
  3.3 0.0 copy-start.4
  3.3 0.5 %shard_map.59 = (bf16[32,128]{1,0:T(8,128)(2,1)S(1)}, bf16[32,128]{1,0:T(8,128)(2,1)S(1)}, bf16[80,128]{1,0:T(8,128)(2,1)S(1)}, bf16[80,128]{1,0:T(8,128)(2,1)S(1)}, f32[16,128]{1,0:T(8,128)S(1)}) custom-call(bf16[16,4,32,128]{3,2,1,0:T(8,128)(2,1)S(1)} %copy-done, bf16[4,32,128]{2,1,0:T(8,128)(2,1)S(1)} %copy-done.3, f32[4,32,128]{2,1,0:T(8,128)S(1)} %copy-done.2), custom_call_target="tpu_custom_call" | custom-call | tf_op jit(solution)/shard_map/pallas_call | solution.py:302
  3.8 0.5 %collective-permute-start = (bf16[32,128]{1,0:T(8,128)(2,1)S(1)}, bf16[32,128]{1,0:T(8,128)(2,1)S(1)}, u32[]{:S(2)}, u32[]{:S(2)}) collective-permute-start(bf16[32,128]{1,0:T(8,128)(2,1)S(1)} %get-tuple-element.9.x1_ref), channel_id=1, source_target_pairs={{0,4},{4,0},{8,12},{12,8},{16,20},{20,16},{24,28},{28,24},{1,5},{5... | collective-permute-start | bytes 24584 | tf_op jit(solution)/shard_map/ppermute | solution.py:294
  4.3 3.6 %collective-permute-start.1 = (bf16[32,128]{1,0:T(8,128)(2,1)S(1)}, bf16[32,128]{1,0:T(8,128)(2,1)S(1)}, u32[]{:S(2)}, u32[]{:S(2)}) collective-permute-start(bf16[32,128]{1,0:T(8,128)(2,1)S(1)} %get-tuple-element.10.x2_ref), channel_id=1, source_target_pairs={{0,28},{4,8},{8,4},{12,16},{16,12},{20,24},{24,20},{28,0},{1,29},{... | collective-permute-start | bytes 24584 | tf_op jit(solution)/shard_map/ppermute | solution.py:294
  7.8 1.6 %collective-permute-start.2 = (bf16[80,128]{1,0:T(8,128)(2,1)S(1)}, bf16[80,128]{1,0:T(8,128)(2,1)S(1)}, u32[]{:S(2)}, u32[]{:S(2)}) collective-permute-start(bf16[80,128]{1,0:T(8,128)(2,1)S(1)} %get-tuple-element.11.y1_ref), channel_id=1, source_target_pairs={{0,1},{1,0},{2,3},{3,2},{4,5},{5,4},{6,7},{7,6},{8,9},{9,8},{10,11... | collective-permute-start | bytes 61448 | tf_op jit(solution)/shard_map/ppermute | solution.py:294
  9.4 2.5 %collective-permute-start.3 = (bf16[80,128]{1,0:T(8,128)(2,1)S(1)}, bf16[80,128]{1,0:T(8,128)(2,1)S(1)}, u32[]{:S(2)}, u32[]{:S(2)}) collective-permute-start(bf16[80,128]{1,0:T(8,128)(2,1)S(1)} %get-tuple-element.12.y2_ref), channel_id=1, source_target_pairs={{0,3},{1,2},{2,1},{3,0},{4,7},{5,6},{6,5},{7,4},{8,11},{9,10},{10,... | collective-permute-start | bytes 61448 | tf_op jit(solution)/shard_map/ppermute | solution.py:294
  11.9 0.0 copy-done.4
  11.9 0.0 copy-start.1
  11.9 1.4 %shard_map.60.gram_ref = f32[16,256]{1,0:T(8,128)S(1)} custom-call(bf16[16,4,32,128]{3,2,1,0:T(8,128)(2,1)S(1)} %copy-done, bf16[4,32,128]{2,1,0:T(8,128)(2,1)S(1)} %copy-done.3, f32[4,32,128]{2,1,0:T(8,128)S(1)} %copy-done.4), custom_call_target="tpu_custom_call" | custom-call | flops 2000000000 | bytes 1000000 | tf_op jit(solution)/shard_map/pallas_call | solution.py:313
  13.3 0.0 collective-permute-done.rx1_ref
  13.3 0.0 collective-permute-done.1.rx2_ref
  13.3 0.0 collective-permute-done.2.ry1_ref
  13.3 1.7 %collective-permute-done.3.ry2_ref = bf16[80,128]{1,0:T(8,128)(2,1)S(1)} collective-permute-done((bf16[80,128]{1,0:T(8,128)(2,1)S(1)}, bf16[80,128]{1,0:T(8,128)(2,1)S(1)}, u32[]{:S(2)}, u32[]{:S(2)}) %collective-permute-start.3) | collective-permute-done | bytes 20512 | tf_op jit(solution)/shard_map/ppermute | solution.py:294
  15.0 0.3 %shard_map.61.own_ref = f32[32,128]{1,0:T(8,128)S(1)} custom-call(bf16[32,128]{1,0:T(8,128)(2,1)S(1)} %get-tuple-element.9.x1_ref, bf16[32,128]{1,0:T(8,128)(2,1)S(1)} %get-tuple-element.10.x2_ref, bf16[80,128]{1,0:T(8,128)(2,1)S(1)} %get-tuple-element.11.y1_ref, bf16[80,128]{1,0:T(8,128)(2,1)S(1)} %get-tuple-element.12.y2_ref, ...), custom_call_target="tpu_custom_call" | custom-call | tf_op jit(solution)/shard_map/pallas_call | solution.py:322
  15.3 9.8 %all_to_all.11 = f32[32,1,128]{2,1,0:T(1,128)S(1)} all-to-all(f32[32,1,128]{2,1,0:T(1,128)S(1)} %bitcast.5), channel_id=1, replica_groups=mesh['gx'=8,'gy'=4] {'gx','gy'}, dimensions={0} | all-to-all | bytes 32768 | tf_op jit(solution)/shard_map/all_to_all | solution.py:329
  25.2 0.0 copy-done.1
  25.2 1.4 %shard_map.62 = (f32[4,32,128]{2,1,0:T(8,128)}, f32[1,16]{1,0:T(1,128)}) custom-call(f32[32,128]{1,0:T(8,128)S(1)} %bitcast.6, f32[32,128]{1,0:T(8,128)S(1)} %shard_map.61.own_ref, bf16[16,4,32,128]{3,2,1,0:T(8,128)(2,1)S(1)} %copy-done.1), custom_call_target="tpu_custom_call" | custom-call | tf_op jit(solution)/shard_map/pallas_call | solution.py:330
Async XLA Ops:
  0.6 1.0 %copy-start = (bf16[16,4,32,128]{3,2,1,0:T(8,128)(2,1)S(1)}, bf16[16,4,32,128]{3,2,1,0:T(8,128)(2,1)}, u32[]{:S(2)}) copy-start(bf16[16,4,32,128]{3,2,1,0:T(8,128)(2,1)} %basis_ref.5) | copy-start | bytes 1572868
  1.7 0.8 %copy-start.2 = (f32[4,32,128]{2,1,0:T(8,128)S(1)}, f32[4,32,128]{2,1,0:T(8,128)}, u32[]{:S(2)}) copy-start(f32[4,32,128]{2,1,0:T(8,128)} %residual_ref.1) | copy-start | bytes 196612
  2.5 0.8 %copy-start.3 = (bf16[4,32,128]{2,1,0:T(8,128)(2,1)S(1)}, bf16[4,32,128]{2,1,0:T(8,128)(2,1)}, u32[]{:S(2)}) copy-start(bf16[4,32,128]{2,1,0:T(8,128)(2,1)} %mobility_ref.3) | copy-start | bytes 98308
  3.3 8.6 %copy-start.4 = (f32[4,32,128]{2,1,0:T(8,128)S(1)}, f32[4,32,128]{2,1,0:T(8,128)}, u32[]{:S(2)}) copy-start(f32[4,32,128]{2,1,0:T(8,128)} %accumulation_ref.1) | copy-start | bytes 196612
  3.8 9.5 %collective-permute-start = (bf16[32,128]{1,0:T(8,128)(2,1)S(1)}, bf16[32,128]{1,0:T(8,128)(2,1)S(1)}, u32[]{:S(2)}, u32[]{:S(2)}) collective-permute-start(bf16[32,128]{1,0:T(8,128)(2,1)S(1)} %get-tuple-element.9.x1_ref), channel_id=1, source_target_pairs={{0,4},{4,0},{8,12},{12,8},{16,20},{20,16},{24,28},{28,24},{1,5},{5... | collective-permute-start | bytes 24584 | tf_op jit(solution)/shard_map/ppermute | solution.py:294
  4.3 9.0 %collective-permute-start.1 = (bf16[32,128]{1,0:T(8,128)(2,1)S(1)}, bf16[32,128]{1,0:T(8,128)(2,1)S(1)}, u32[]{:S(2)}, u32[]{:S(2)}) collective-permute-start(bf16[32,128]{1,0:T(8,128)(2,1)S(1)} %get-tuple-element.10.x2_ref), channel_id=1, source_target_pairs={{0,28},{4,8},{8,4},{12,16},{16,12},{20,24},{24,20},{28,0},{1,29},{... | collective-permute-start | bytes 24584 | tf_op jit(solution)/shard_map/ppermute | solution.py:294
  7.8 5.5 %collective-permute-start.2 = (bf16[80,128]{1,0:T(8,128)(2,1)S(1)}, bf16[80,128]{1,0:T(8,128)(2,1)S(1)}, u32[]{:S(2)}, u32[]{:S(2)}) collective-permute-start(bf16[80,128]{1,0:T(8,128)(2,1)S(1)} %get-tuple-element.11.y1_ref), channel_id=1, source_target_pairs={{0,1},{1,0},{2,3},{3,2},{4,5},{5,4},{6,7},{7,6},{8,9},{9,8},{10,11... | collective-permute-start | bytes 61448 | tf_op jit(solution)/shard_map/ppermute | solution.py:294
  9.4 5.6 %collective-permute-start.3 = (bf16[80,128]{1,0:T(8,128)(2,1)S(1)}, bf16[80,128]{1,0:T(8,128)(2,1)S(1)}, u32[]{:S(2)}, u32[]{:S(2)}) collective-permute-start(bf16[80,128]{1,0:T(8,128)(2,1)S(1)} %get-tuple-element.12.y2_ref), channel_id=1, source_target_pairs={{0,3},{1,2},{2,1},{3,0},{4,7},{5,6},{6,5},{7,4},{8,11},{9,10},{10,... | collective-permute-start | bytes 61448 | tf_op jit(solution)/shard_map/ppermute | solution.py:294
  11.9 13.3 %copy-start.1 = (bf16[16,4,32,128]{3,2,1,0:T(8,128)(2,1)S(1)}, bf16[16,4,32,128]{3,2,1,0:T(8,128)(2,1)}, u32[]{:S(2)}) copy-start(bf16[16,4,32,128]{3,2,1,0:T(8,128)(2,1)} %basis_ref.5) | copy-start | bytes 1572868

commit v3 on v2

--- a/solution.py
+++ b/solution.py
@@ -17,6 +17,7 @@
 F32 = jnp.float32
 BF16 = jnp.bfloat16
 VMEM = pl.BlockSpec(memory_space=pltpu.VMEM)
+HBM = pl.BlockSpec(memory_space=pltpu.HBM)
 PARAMS = pltpu.CompilerParams(vmem_limit_bytes=8 * 2**20)
 
 
@@ -50,21 +51,42 @@
     return odd, inner
 
 
-def edges_kernel(counts, basis_ref, mobility_ref, residual_ref, x1_ref, x2_ref, y1_ref, y2_ref, b_ref):
+def edges_kernel(
+    counts,
+    basis_hbm,
+    mobility_hbm,
+    accumulation_hbm,
+    residual_hbm,
+    x1_ref,
+    x2_ref,
+    y1_ref,
+    y2_ref,
+    b_ref,
+    basis_ref,
+    mobility_ref,
+    accumulation_ref,
+    residual_ref,
+    chunk_sems,
+    sems,
+):
     k_count, cz, cy, cx = basis_ref.shape
+    chunks = chunk_sems.shape[0]
+    size = k_count // chunks
+    residual_copy = pltpu.make_async_copy(residual_hbm, residual_ref, sems.at[0])
+    residual_copy.start()
+    chunk_copies = []
+    for n in range(chunks):
+        part = slice(n * size, (n + 1) * size)
+        copy = pltpu.make_async_copy(basis_hbm.at[part], basis_ref.at[part], chunk_sems.at[n])
+        copy.start()
+        chunk_copies.append(copy)
+    mobility_copy = pltpu.make_async_copy(mobility_hbm, mobility_ref, sems.at[1])
+    mobility_copy.start()
+    accumulation_copy = pltpu.make_async_copy(accumulation_hbm, accumulation_ref, sems.at[2])
+    accumulation_copy.start()
     cells = cz * cy
     odd_x, inner_x = position("gx", counts[0])
     odd_y, inner_y = position("gy", counts[1])
-
-    residual = residual_ref[...]
-    row = iota((k_count, cx), 0)
-    partial = jnp.zeros((k_count, cx), F32)
-    for k in range(k_count):
-        product = basis_ref[k].astype(F32) * residual
-        total = jnp.sum(jnp.sum(product, axis=0), axis=0, keepdims=True)
-        partial = jnp.where(row == k, total, partial)
-    b = jnp.broadcast_to(jnp.sum(partial, axis=1, keepdims=True), (k_count, LANES))
-    b_ref[...] = b
 
     first = jnp.where(odd_x, 0, cx - 1)
     second = jnp.where(odd_x, cx - 1, 0)
@@ -73,9 +95,21 @@
     wanted = pick_lane == jnp.where(pick_row < k_count, first, second)
     pick_k = jnp.where(pick_row < k_count, pick_row, pick_row - k_count)
     columns = jnp.zeros((2 * k_count, cells), F32)
+    row = iota((k_count, cx), 0)
+    partial = jnp.zeros((k_count, cx), F32)
+    residual_copy.wait()
+    residual = residual_ref[...]
     for k in range(k_count):
+        if k % size == 0:
+            chunk_copies[k // size].wait()
         pick = jnp.where(jnp.logical_and(wanted, pick_k == k), 1.0, 0.0).astype(BF16)
         columns = columns + dot_nt(pick, basis_ref[k].reshape(cells, cx))
+        product = basis_ref[k].astype(F32) * residual
+        total = jnp.sum(jnp.sum(product, axis=0), axis=0, keepdims=True)
+        partial = jnp.where(row == k, total, partial)
+    b = jnp.broadcast_to(jnp.sum(partial, axis=1, keepdims=True), (k_count, LANES))
+    b_ref[...] = b
+    mobility_copy.wait()
     pick_row = iota((TILE, cx), 0)
     pick_lane = iota((TILE, cx), 1)
     pick = jnp.where(pick_lane == jnp.where(pick_row == 0, first, second), 1.0, 0.0).astype(BF16)
@@ -118,6 +152,7 @@
                 extras[number] = jnp.where(extra_row == place * cz + z, value, extras[number])
     for number, ref in ((0, y1_ref), (1, y2_ref)):
         ref[cz * k_count : cz * k_count + extra_rows, :] = extras[number].astype(BF16)
+    accumulation_copy.wait()
 
 
 def gram_kernel(basis_ref, mobility_ref, accumulation_ref, gram_ref, left_ref):
@@ -238,7 +273,7 @@
     out_ref[...] = jnp.broadcast_to(packed, out_ref.shape)
 
 
-def finish_kernel(count_y, gathered_ref, own_ref, basis_ref, correction_ref, solution_ref):
+def finish_kernel(count_y, gathered_ref, own_ref, basis_ref, correction_hbm, solution_ref, correction_ref, sems):
     k_count, cz, cy, cx = basis_ref.shape
     base = 6 * k_count
     every = gathered_ref[...]
@@ -280,10 +315,17 @@
     solution_ref[...] = solution[:, :k_count]
     spread = iota((k_count, LANES), 0) == iota((k_count, LANES), 1)
     column = jnp.sum(jnp.where(spread, solution, 0.0), axis=1, keepdims=True)
-    correction = jnp.zeros((cz, cy, cx), F32)
-    for k in range(k_count):
-        correction = correction + basis_ref[k].astype(F32) * column[k : k + 1][None]
-    correction_ref[...] = correction
+    copies = []
+    for z in range(cz):
+        layer = jnp.zeros((cy, cx), F32)
+        for k in range(k_count):
+            layer = layer + basis_ref[k, z].astype(F32) * column[k : k + 1]
+        correction_ref[z] = layer
+        copy = pltpu.make_async_copy(correction_ref.at[z], correction_hbm.at[z], sems.at[z])
+        copy.start()
+        copies.append(copy)
+    for copy in copies:
+        copy.wait()
 
 
 def exchange(message, axis, count, second):
@@ -299,13 +341,29 @@
     devices = counts[0] * counts[1]
     x_message = jax.ShapeDtypeStruct((k_count + TILE, cz * cy), BF16)
     y_message = jax.ShapeDtypeStruct((cz * k_count + round_up(4 * cz, TILE), cx), BF16)
-    x1, x2, y1, y2, b = pl.pallas_call(
+    chunks = 8 if k_count % 8 == 0 else 1
+    inputs = [pltpu.with_memory_space_constraint(x, pltpu.HBM) for x in (basis, mobility, accumulation, residual)]
+    x1, x2, y1, y2, b, basis, mobility, accumulation = pl.pallas_call(
         functools.partial(edges_kernel, counts),
-        out_shape=(x_message, x_message, y_message, y_message, jax.ShapeDtypeStruct((k_count, LANES), F32)),
-        in_specs=[VMEM] * 3,
-        out_specs=(VMEM,) * 5,
+        out_shape=(
+            x_message,
+            x_message,
+            y_message,
+            y_message,
+            jax.ShapeDtypeStruct((k_count, LANES), F32),
+            jax.ShapeDtypeStruct(basis.shape, BF16),
+            jax.ShapeDtypeStruct(mobility.shape, BF16),
+            jax.ShapeDtypeStruct(accumulation.shape, F32),
+        ),
+        in_specs=[HBM] * 4,
+        out_specs=(VMEM,) * 8,
+        scratch_shapes=[
+            pltpu.VMEM(residual.shape, F32),
+            pltpu.SemaphoreType.DMA((chunks,)),
+            pltpu.SemaphoreType.DMA((3,)),
+        ],
         compiler_params=PARAMS,
-    )(basis, mobility, residual)
+    )(*inputs)
     rx1 = exchange(x1, "gx", counts[0], False)
     rx2 = exchange(x2, "gx", counts[0], True)
     ry1 = exchange(y1, "gy", counts[1], False)
@@ -331,7 +389,8 @@
         functools.partial(finish_kernel, counts[1]),
         out_shape=(jax.ShapeDtypeStruct((cz, cy, cx), F32), jax.ShapeDtypeStruct((1, k_count), F32)),
         in_specs=[VMEM] * 3,
-        out_specs=(VMEM, VMEM),
+        out_specs=(HBM, VMEM),
+        scratch_shapes=[pltpu.VMEM((cz, cy, cx), F32), pltpu.SemaphoreType.DMA((cz,))],
         compiler_params=PARAMS,
     )(gathered, row, basis)
     return correction, solution.reshape(1, 1, k_count)

time: 26.9 us -> 26.2 us (0.974)
  local copies, waits for them, and re-layouts: 2.64 us -> 0 us
  Pallas kernels: 3.61 us -> 5.73 us
    unnamed x10 -> x0, local copies, waits for them, and re-layouts: 2.64 us -> none
    pallas_call x1, Pallas kernels: 0.47 us -> 2.07 us  [per_device(): pl.pallas_call(functools.partial(edges_kernel, counts), out_shape=(x_mess...]
    pallas_call x1, Pallas kernels: 1.4 us -> 1.92 us  [per_device(): pl.pallas_call(functools.partial(finish_kernel, counts[1]), out_shape=(ja...]
where the time goes in v3:
time: 26.2 us; the launch traced here: 26 us
  blocking collectives  9.82 us (37%)
  starting transfers between devices  8.13 us (31%)
  Pallas kernels  5.73 us (22%)
  waiting for transfers between devices  1.68 us (6%)
  between operations  0.68 us (3%)
    all_to_all x1, blocking collectives, per_device(): gathered = lax.all_to_all(row, ('gx', 'gy'), 0, 0, tiled=True)  9.82 us
    ppermute x4, starting transfers between devices, exchange(): return lax.ppermute(message, axis, pairs)  8.13 us
    pallas_call x1, Pallas kernels, per_device(): pl.pallas_call(functools.partial(edges_kernel, counts), out_shape=(x_mess...  2.07 us
    pallas_call x1, Pallas kernels, per_device(): pl.pallas_call(functools.partial(finish_kernel, counts[1]), out_shape=(ja...  1.92 us
    ppermute x4, waiting for transfers between devices, exchange(): return lax.ppermute(message, axis, pairs)  1.68 us
    pallas_call x1, Pallas kernels, per_device(): pl.pallas_call(gram_kernel, out_shape=jax.ShapeDtypeStruct((k_count, k_co...  1.4 us
  transfers between devices with their start and end apart: 4, of which 1 were waited for; matrix products, arithmetic and copies ran while one was open for 0% of the time, Pallas kernels for 5%

profile of v3, /device:TPU:0, one launch (start us, length us, event | category | flops | bytes accessed | tf_op | source)
XLA Modules:
  0.0 26.0 jit_solution(1067432136163522131)
XLA Ops:
  0.6 2.1 %shard_map.59 = (bf16[32,128]{1,0:T(8,128)(2,1)S(1)}, bf16[32,128]{1,0:T(8,128)(2,1)S(1)}, bf16[80,128]{1,0:T(8,128)(2,1)S(1)}, bf16[80,128]{1,0:T(8,128)(2,1)S(...) custom-call(bf16[16,4,32,128]{3,2,1,0:T(8,128)(2,1)} %basis_hbm.1, ...), custom_call_target="tpu_custom_call" | custom-call | tf_op jit(solution)/shard_map/pallas_call | solution.py:346
  2.7 0.5 %collective-permute-start = (bf16[32,128]{1,0:T(8,128)(2,1)S(1)}, bf16[32,128]{1,0:T(8,128)(2,1)S(1)}, u32[]{:S(2)}, u32[]{:S(2)}) collective-permute-start(bf16[32,128]{1,0:T(8,128)(2,1)S(1)} %get-tuple-element.12.x1_ref), channel_id=1, source_target_pairs={{0,4},{4,0},{8,12},{12,8},{16,20},{20,16},{24,28},{28,24},{1,5},{5... | collective-permute-start | bytes 24584 | tf_op jit(solution)/shard_map/ppermute | solution.py:336
  3.2 3.6 %collective-permute-start.1 = (bf16[32,128]{1,0:T(8,128)(2,1)S(1)}, bf16[32,128]{1,0:T(8,128)(2,1)S(1)}, u32[]{:S(2)}, u32[]{:S(2)}) collective-permute-start(bf16[32,128]{1,0:T(8,128)(2,1)S(1)} %get-tuple-element.13.x2_ref), channel_id=1, source_target_pairs={{0,28},{4,8},{8,4},{12,16},{16,12},{20,24},{24,20},{28,0},{1,29},{... | collective-permute-start | bytes 24584 | tf_op jit(solution)/shard_map/ppermute | solution.py:336
  6.8 1.6 %collective-permute-start.2 = (bf16[80,128]{1,0:T(8,128)(2,1)S(1)}, bf16[80,128]{1,0:T(8,128)(2,1)S(1)}, u32[]{:S(2)}, u32[]{:S(2)}) collective-permute-start(bf16[80,128]{1,0:T(8,128)(2,1)S(1)} %get-tuple-element.14.y1_ref), channel_id=1, source_target_pairs={{0,1},{1,0},{2,3},{3,2},{4,5},{5,4},{6,7},{7,6},{8,9},{9,8},{10,11... | collective-permute-start | bytes 61448 | tf_op jit(solution)/shard_map/ppermute | solution.py:336
  8.4 2.5 %collective-permute-start.3 = (bf16[80,128]{1,0:T(8,128)(2,1)S(1)}, bf16[80,128]{1,0:T(8,128)(2,1)S(1)}, u32[]{:S(2)}, u32[]{:S(2)}) collective-permute-start(bf16[80,128]{1,0:T(8,128)(2,1)S(1)} %get-tuple-element.15.y2_ref), channel_id=1, source_target_pairs={{0,3},{1,2},{2,1},{3,0},{4,7},{5,6},{6,5},{7,4},{8,11},{9,10},{10,... | collective-permute-start | bytes 61448 | tf_op jit(solution)/shard_map/ppermute | solution.py:336
  10.8 1.4 %shard_map.60.gram_ref = f32[16,256]{1,0:T(8,128)S(1)} custom-call(bf16[16,4,32,128]{3,2,1,0:T(8,128)(2,1)S(1)} %get-tuple-element.17.basis_ref, bf16[4,32,128]{2,1,0:T(8,128)(2,1)S(1)} %get-tuple-element.18.mobility_ref, f32[4,32,128]{2,1,0:T(8,128)S(1)} %get-tuple-element.19.accumulation_ref), custom_call_target="tpu_custom_call" | custom-call | flops 2000000000 | bytes 1000000 | tf_op jit(solution)/shard_map/pallas_call | solution.py:371
  12.2 0.0 collective-permute-done.rx1_ref
  12.3 0.0 collective-permute-done.1.rx2_ref
  12.3 0.0 collective-permute-done.2.ry1_ref
  12.3 1.7 %collective-permute-done.3.ry2_ref = bf16[80,128]{1,0:T(8,128)(2,1)S(1)} collective-permute-done((bf16[80,128]{1,0:T(8,128)(2,1)S(1)}, bf16[80,128]{1,0:T(8,128)(2,1)S(1)}, u32[]{:S(2)}, u32[]{:S(2)}) %collective-permute-start.3) | collective-permute-done | bytes 20512 | tf_op jit(solution)/shard_map/ppermute | solution.py:336
  13.9 0.3 %shard_map.61.own_ref = f32[32,128]{1,0:T(8,128)S(1)} custom-call(bf16[32,128]{1,0:T(8,128)(2,1)S(1)} %get-tuple-element.12.x1_ref, bf16[32,128]{1,0:T(8,128)(2,1)S(1)} %get-tuple-element.13.x2_ref, bf16[80,128]{1,0:T(8,128)(2,1)S(1)} %get-tuple-element.14.y1_ref, bf16[80,128]{1,0:T(8,128)(2,1)S(1)} %get-tuple-element.15.y2_ref, ...), custom_call_target="tpu_custom_call" | custom-call | tf_op jit(solution)/shard_map/pallas_call | solution.py:380
  14.3 9.8 %all_to_all.11 = f32[32,1,128]{2,1,0:T(1,128)S(1)} all-to-all(f32[32,1,128]{2,1,0:T(1,128)S(1)} %bitcast.5), channel_id=1, replica_groups=mesh['gx'=8,'gy'=4] {'gx','gy'}, dimensions={0} | all-to-all | bytes 32768 | tf_op jit(solution)/shard_map/all_to_all | solution.py:387
  24.1 1.9 %shard_map.62 = (f32[4,32,128]{2,1,0:T(8,128)}, f32[1,16]{1,0:T(1,128)}) custom-call(f32[32,128]{1,0:T(8,128)S(1)} %bitcast.6, f32[32,128]{1,0:T(8,128)S(1)} %shard_map.61.own_ref, bf16[16,4,32,128]{3,2,1,0:T(8,128)(2,1)S(1)} %get-tuple-element.17.basis_ref), custom_call_target="tpu_custom_call" | custom-call | tf_op jit(solution)/shard_map/pallas_call | solution.py:388
Async XLA Ops:
  2.7 9.5 %collective-permute-start = (bf16[32,128]{1,0:T(8,128)(2,1)S(1)}, bf16[32,128]{1,0:T(8,128)(2,1)S(1)}, u32[]{:S(2)}, u32[]{:S(2)}) collective-permute-start(bf16[32,128]{1,0:T(8,128)(2,1)S(1)} %get-tuple-element.12.x1_ref), channel_id=1, source_target_pairs={{0,4},{4,0},{8,12},{12,8},{16,20},{20,16},{24,28},{28,24},{1,5},{5... | collective-permute-start | bytes 24584 | tf_op jit(solution)/shard_map/ppermute | solution.py:336
  3.2 9.0 %collective-permute-start.1 = (bf16[32,128]{1,0:T(8,128)(2,1)S(1)}, bf16[32,128]{1,0:T(8,128)(2,1)S(1)}, u32[]{:S(2)}, u32[]{:S(2)}) collective-permute-start(bf16[32,128]{1,0:T(8,128)(2,1)S(1)} %get-tuple-element.13.x2_ref), channel_id=1, source_target_pairs={{0,28},{4,8},{8,4},{12,16},{16,12},{20,24},{24,20},{28,0},{1,29},{... | collective-permute-start | bytes 24584 | tf_op jit(solution)/shard_map/ppermute | solution.py:336
  6.8 5.5 %collective-permute-start.2 = (bf16[80,128]{1,0:T(8,128)(2,1)S(1)}, bf16[80,128]{1,0:T(8,128)(2,1)S(1)}, u32[]{:S(2)}, u32[]{:S(2)}) collective-permute-start(bf16[80,128]{1,0:T(8,128)(2,1)S(1)} %get-tuple-element.14.y1_ref), channel_id=1, source_target_pairs={{0,1},{1,0},{2,3},{3,2},{4,5},{5,4},{6,7},{7,6},{8,9},{9,8},{10,11... | collective-permute-start | bytes 61448 | tf_op jit(solution)/shard_map/ppermute | solution.py:336
  8.4 5.6 %collective-permute-start.3 = (bf16[80,128]{1,0:T(8,128)(2,1)S(1)}, bf16[80,128]{1,0:T(8,128)(2,1)S(1)}, u32[]{:S(2)}, u32[]{:S(2)}) collective-permute-start(bf16[80,128]{1,0:T(8,128)(2,1)S(1)} %get-tuple-element.15.y2_ref), channel_id=1, source_target_pairs={{0,3},{1,2},{2,1},{3,0},{4,7},{5,6},{6,5},{7,4},{8,11},{9,10},{10,... | collective-permute-start | bytes 61448 | tf_op jit(solution)/shard_map/ppermute | solution.py:336

commit v4 on v3

--- a/solution.py
+++ b/solution.py
@@ -273,7 +273,7 @@
     out_ref[...] = jnp.broadcast_to(packed, out_ref.shape)
 
 
-def finish_kernel(count_y, gathered_ref, own_ref, basis_ref, correction_hbm, solution_ref, correction_ref, sems):
+def finish_kernel(count_y, gathered_ref, own_ref, basis_ref, correction_hbm, solution_hbm, correction_ref, solution_ref, sems):
     k_count, cz, cy, cx = basis_ref.shape
     base = 6 * k_count
     every = gathered_ref[...]
@@ -313,9 +313,10 @@
     own_direction = own_weight * own - step * shifted(own, k_count)
     solution = step * own + last_step * own_direction
     solution_ref[...] = solution[:, :k_count]
+    copies = [pltpu.make_async_copy(solution_ref, solution_hbm, sems.at[cz])]
+    copies[0].start()
     spread = iota((k_count, LANES), 0) == iota((k_count, LANES), 1)
     column = jnp.sum(jnp.where(spread, solution, 0.0), axis=1, keepdims=True)
-    copies = []
     for z in range(cz):
         layer = jnp.zeros((cy, cx), F32)
         for k in range(k_count):
@@ -328,12 +329,21 @@
         copy.wait()
 
 
-def exchange(message, axis, count, second):
-    if second:
-        pairs = [(i, (i - 1) % count if i % 2 == 0 else (i + 1) % count) for i in range(count)]
-    else:
-        pairs = [(i, i ^ 1) for i in range(count)]
-    return lax.ppermute(message, axis, pairs)
+def exchange(message, axis, counts, second):
+    count_x, count_y = counts
+    pairs = []
+    for x in range(count_x):
+        for y in range(count_y):
+            i, count = (x, count_x) if axis == "gx" else (y, count_y)
+            j = i ^ 1
+            if second:
+                j = i - 1 if i % 2 == 0 else i + 1
+            if 0 <= j < count:
+                partner = (j, y) if axis == "gx" else (x, j)
+            else:
+                partner = (x, y ^ 1) if axis == "gx" else (x ^ 1, y)
+            pairs.append((x * count_y + y, partner[0] * count_y + partner[1]))
+    return lax.ppermute(message, ("gx", "gy"), pairs)
 
 
 def per_device(counts, basis, mobility, accumulation, residual):
@@ -364,10 +374,10 @@
         ],
         compiler_params=PARAMS,
     )(*inputs)
-    rx1 = exchange(x1, "gx", counts[0], False)
-    rx2 = exchange(x2, "gx", counts[0], True)
-    ry1 = exchange(y1, "gy", counts[1], False)
-    ry2 = exchange(y2, "gy", counts[1], True)
+    rx1 = exchange(x1, "gx", counts, False)
+    rx2 = exchange(x2, "gx", counts, True)
+    ry1 = exchange(y1, "gy", counts, False)
+    ry2 = exchange(y2, "gy", counts, True)
     gram = pl.pallas_call(
         gram_kernel,
         out_shape=jax.ShapeDtypeStruct((k_count, k_count * TILE), F32),
@@ -389,8 +399,12 @@
         functools.partial(finish_kernel, counts[1]),
         out_shape=(jax.ShapeDtypeStruct((cz, cy, cx), F32), jax.ShapeDtypeStruct((1, k_count), F32)),
         in_specs=[VMEM] * 3,
-        out_specs=(HBM, VMEM),
-        scratch_shapes=[pltpu.VMEM((cz, cy, cx), F32), pltpu.SemaphoreType.DMA((cz,))],
+        out_specs=(HBM, HBM),
+        scratch_shapes=[
+            pltpu.VMEM((cz, cy, cx), F32),
+            pltpu.VMEM((1, k_count), F32),
+            pltpu.SemaphoreType.DMA((cz + 1,)),
+        ],
         compiler_params=PARAMS,
     )(gathered, row, basis)
     return correction, solution.reshape(1, 1, k_count)

time: 26.2 us -> 24 us (0.916)
  starting transfers between devices: 8.13 us -> 4.49 us
  blocking collectives: 9.82 us -> 12.4 us
  waiting for transfers between devices: 1.68 us -> 1.04 us
  Pallas kernels: 5.73 us -> 5.23 us
    ppermute x4, starting transfers between devices: 8.13 us -> 4.49 us  [exchange(): return lax.ppermute(message, ('gx', 'gy'), pairs)]
    all_to_all x1, blocking collectives: 9.82 us -> 12.4 us  [per_device(): gathered = lax.all_to_all(row, ('gx', 'gy'), 0, 0, tiled=True)]
    ppermute x4, waiting for transfers between devices: 1.68 us -> 1.04 us  [exchange(): return lax.ppermute(message, ('gx', 'gy'), pairs)]
    pallas_call x1, Pallas kernels: 1.92 us -> 1.42 us  [per_device(): pl.pallas_call(functools.partial(finish_kernel, counts[1]), out_shape=(ja...]
  transfers between devices with their start and end apart: 4 -> 4, of which waited for: 1 -> 1; matrix products, arithmetic and copies ran while one was open for 0% -> 0% of each run, Pallas kernels for 5% -> 6%
where the time goes in v4:
time: 24 us; the launch traced here: 23.8 us
  blocking collectives  12.4 us (52%)
  Pallas kernels  5.23 us (22%)
  starting transfers between devices  4.49 us (19%)
  waiting for transfers between devices  1.04 us (4%)
  between operations  0.67 us (3%)
    all_to_all x1, blocking collectives, per_device(): gathered = lax.all_to_all(row, ('gx', 'gy'), 0, 0, tiled=True)  12.4 us
    ppermute x4, starting transfers between devices, exchange(): return lax.ppermute(message, ('gx', 'gy'), pairs)  4.49 us
    pallas_call x1, Pallas kernels, per_device(): pl.pallas_call(functools.partial(edges_kernel, counts), out_shape=(x_mess...  2.07 us
    pallas_call x1, Pallas kernels, per_device(): pl.pallas_call(functools.partial(finish_kernel, counts[1]), out_shape=(ja...  1.42 us
    pallas_call x1, Pallas kernels, per_device(): pl.pallas_call(gram_kernel, out_shape=jax.ShapeDtypeStruct((k_count, k_co...  1.4 us
    ppermute x4, waiting for transfers between devices, exchange(): return lax.ppermute(message, ('gx', 'gy'), pairs)  1.04 us
  transfers between devices with their start and end apart: 4, of which 1 were waited for; matrix products, arithmetic and copies ran while one was open for 0% of the time, Pallas kernels for 6%

profile of v4, /device:TPU:0, one launch (start us, length us, event | category | flops | bytes accessed | tf_op | source)
XLA Modules:
  0.0 23.8 jit_solution(13026912328910598294)
XLA Ops:
  0.6 2.1 %shard_map.59 = (bf16[32,128]{1,0:T(8,128)(2,1)S(1)}, bf16[32,128]{1,0:T(8,128)(2,1)S(1)}, bf16[80,128]{1,0:T(8,128)(2,1)S(1)}, bf16[80,128]{1,0:T(8,128)(2,1)S(...) custom-call(bf16[16,4,32,128]{3,2,1,0:T(8,128)(2,1)} %basis_hbm.1, ...), custom_call_target="tpu_custom_call" | custom-call | tf_op jit(solution)/shard_map/pallas_call | solution.py:356
  2.7 0.5 %collective-permute-start = (bf16[32,128]{1,0:T(8,128)(2,1)S(1)}, bf16[32,128]{1,0:T(8,128)(2,1)S(1)}, u32[]{:S(2)}, u32[]{:S(2)}) collective-permute-start(bf16[32,128]{1,0:T(8,128)(2,1)S(1)} %get-tuple-element.12.x1_ref), channel_id=1, source_target_pairs={{0,4},{1,5},{2,6},{3,7},{4,0},{5,1},{6,2},{7,3},{8,12},{9,13},{10,... | collective-permute-start | bytes 24584 | tf_op jit(solution)/shard_map/ppermute | solution.py:346
  3.2 2.6 %collective-permute-start.1 = (bf16[32,128]{1,0:T(8,128)(2,1)S(1)}, bf16[32,128]{1,0:T(8,128)(2,1)S(1)}, u32[]{:S(2)}, u32[]{:S(2)}) collective-permute-start(bf16[32,128]{1,0:T(8,128)(2,1)S(1)} %get-tuple-element.13.x2_ref), channel_id=1, source_target_pairs={{0,1},{1,0},{2,3},{3,2},{4,8},{5,9},{6,10},{7,11},{8,4},{9,5},{10,... | collective-permute-start | bytes 24584 | tf_op jit(solution)/shard_map/ppermute | solution.py:346
  5.9 0.1 collective-permute-start.2
  6.0 1.2 %collective-permute-start.3 = (bf16[80,128]{1,0:T(8,128)(2,1)S(1)}, bf16[80,128]{1,0:T(8,128)(2,1)S(1)}, u32[]{:S(2)}, u32[]{:S(2)}) collective-permute-start(bf16[80,128]{1,0:T(8,128)(2,1)S(1)} %get-tuple-element.15.y2_ref), channel_id=1, source_target_pairs={{0,4},{1,2},{2,1},{3,7},{4,0},{5,6},{6,5},{7,3},{8,12},{9,10},{10,... | collective-permute-start | bytes 61448 | tf_op jit(solution)/shard_map/ppermute | solution.py:346
  7.2 1.4 %shard_map.60.gram_ref = f32[16,256]{1,0:T(8,128)S(1)} custom-call(bf16[16,4,32,128]{3,2,1,0:T(8,128)(2,1)S(1)} %get-tuple-element.17.basis_ref, bf16[4,32,128]{2,1,0:T(8,128)(2,1)S(1)} %get-tuple-element.18.mobility_ref, f32[4,32,128]{2,1,0:T(8,128)S(1)} %get-tuple-element.19.accumulation_ref), custom_call_target="tpu_custom_call" | custom-call | flops 2000000000 | bytes 1000000 | tf_op jit(solution)/shard_map/pallas_call | solution.py:381
  8.6 0.0 collective-permute-done.rx1_ref
  8.6 0.0 collective-permute-done.1.rx2_ref
  8.6 1.0 %collective-permute-done.2.ry1_ref = bf16[80,128]{1,0:T(8,128)(2,1)S(1)} collective-permute-done((bf16[80,128]{1,0:T(8,128)(2,1)S(1)}, bf16[80,128]{1,0:T(8,128)(2,1)S(1)}, u32[]{:S(2)}, u32[]{:S(2)}) %collective-permute-start.2) | collective-permute-done | bytes 20512 | tf_op jit(solution)/shard_map/ppermute | solution.py:346
  9.7 0.0 collective-permute-done.3.ry2_ref
  9.7 0.4 %shard_map.61.own_ref = f32[32,128]{1,0:T(8,128)S(1)} custom-call(bf16[32,128]{1,0:T(8,128)(2,1)S(1)} %get-tuple-element.12.x1_ref, bf16[32,128]{1,0:T(8,128)(2,1)S(1)} %get-tuple-element.13.x2_ref, bf16[80,128]{1,0:T(8,128)(2,1)S(1)} %get-tuple-element.14.y1_ref, bf16[80,128]{1,0:T(8,128)(2,1)S(1)} %get-tuple-element.15.y2_ref, ...), custom_call_target="tpu_custom_call" | custom-call | tf_op jit(solution)/shard_map/pallas_call | solution.py:390
  10.0 12.4 %all_to_all.11 = f32[32,1,128]{2,1,0:T(1,128)S(1)} all-to-all(f32[32,1,128]{2,1,0:T(1,128)S(1)} %bitcast.5), channel_id=1, replica_groups=mesh['gx'=8,'gy'=4] {'gx','gy'}, dimensions={0} | all-to-all | bytes 32768 | tf_op jit(solution)/shard_map/all_to_all | solution.py:397
  22.4 1.4 %shard_map.62 = (f32[4,32,128]{2,1,0:T(8,128)}, f32[1,16]{1,0:T(1,128)}) custom-call(f32[32,128]{1,0:T(8,128)S(1)} %bitcast.6, f32[32,128]{1,0:T(8,128)S(1)} %shard_map.61.own_ref, bf16[16,4,32,128]{3,2,1,0:T(8,128)(2,1)S(1)} %get-tuple-element.17.basis_ref), custom_call_target="tpu_custom_call" | custom-call | tf_op jit(solution)/shard_map/pallas_call | solution.py:398
Async XLA Ops:
  2.7 5.9 %collective-permute-start = (bf16[32,128]{1,0:T(8,128)(2,1)S(1)}, bf16[32,128]{1,0:T(8,128)(2,1)S(1)}, u32[]{:S(2)}, u32[]{:S(2)}) collective-permute-start(bf16[32,128]{1,0:T(8,128)(2,1)S(1)} %get-tuple-element.12.x1_ref), channel_id=1, source_target_pairs={{0,4},{1,5},{2,6},{3,7},{4,0},{5,1},{6,2},{7,3},{8,12},{9,13},{10,... | collective-permute-start | bytes 24584 | tf_op jit(solution)/shard_map/ppermute | solution.py:346
  3.2 5.4 %collective-permute-start.1 = (bf16[32,128]{1,0:T(8,128)(2,1)S(1)}, bf16[32,128]{1,0:T(8,128)(2,1)S(1)}, u32[]{:S(2)}, u32[]{:S(2)}) collective-permute-start(bf16[32,128]{1,0:T(8,128)(2,1)S(1)} %get-tuple-element.13.x2_ref), channel_id=1, source_target_pairs={{0,1},{1,0},{2,3},{3,2},{4,8},{5,9},{6,10},{7,11},{8,4},{9,5},{10,... | collective-permute-start | bytes 24584 | tf_op jit(solution)/shard_map/ppermute | solution.py:346
  5.9 3.8 %collective-permute-start.2 = (bf16[80,128]{1,0:T(8,128)(2,1)S(1)}, bf16[80,128]{1,0:T(8,128)(2,1)S(1)}, u32[]{:S(2)}, u32[]{:S(2)}) collective-permute-start(bf16[80,128]{1,0:T(8,128)(2,1)S(1)} %get-tuple-element.14.y1_ref), channel_id=1, source_target_pairs={{0,1},{1,0},{2,3},{3,2},{4,5},{5,4},{6,7},{7,6},{8,9},{9,8},{10,11... | collective-permute-start | bytes 61448 | tf_op jit(solution)/shard_map/ppermute | solution.py:346
  6.0 3.7 %collective-permute-start.3 = (bf16[80,128]{1,0:T(8,128)(2,1)S(1)}, bf16[80,128]{1,0:T(8,128)(2,1)S(1)}, u32[]{:S(2)}, u32[]{:S(2)}) collective-permute-start(bf16[80,128]{1,0:T(8,128)(2,1)S(1)} %get-tuple-element.15.y2_ref), channel_id=1, source_target_pairs={{0,4},{1,2},{2,1},{3,7},{4,0},{5,6},{6,5},{7,3},{8,12},{9,10},{10,... | collective-permute-start | bytes 61448 | tf_op jit(solution)/shard_map/ppermute | solution.py:346

commit v5 on v4

--- a/solution.py
+++ b/solution.py
@@ -42,6 +42,13 @@
     rest = x - high
     middle = rest.astype(BF16).astype(F32)
     return high, middle, rest - middle
+
+
+def expand(basis_ref, column):
+    field = basis_ref[0].astype(F32) * column[0:1][None]
+    for k in range(1, basis_ref.shape[0]):
+        field = field + basis_ref[k].astype(F32) * column[k : k + 1][None]
+    return field
 
 
 def position(axis, count):
@@ -94,26 +101,28 @@
     pick_lane = iota((2 * k_count, cx), 1)
     wanted = pick_lane == jnp.where(pick_row < k_count, first, second)
     pick_k = jnp.where(pick_row < k_count, pick_row, pick_row - k_count)
-    columns = jnp.zeros((2 * k_count, cells), F32)
+    picks = [jnp.where(jnp.logical_and(wanted, pick_k == k), 1.0, 0.0).astype(BF16) for k in range(k_count)]
+    pick_row = iota((TILE, cx), 0)
+    pick_lane = iota((TILE, cx), 1)
+    pick = jnp.where(pick_lane == jnp.where(pick_row == 0, first, second), 1.0, 0.0).astype(BF16)
+    mobility_copy.wait()
+    edge_mobility = dot_nt(pick, mobility_ref[...].reshape(cells, cx))
+    residual_copy.wait()
+    residual = residual_ref[...]
+
     row = iota((k_count, cx), 0)
     partial = jnp.zeros((k_count, cx), F32)
-    residual_copy.wait()
-    residual = residual_ref[...]
+    for copy in chunk_copies:
+        copy.wait()
+    columns = dot_nt(
+        jnp.concatenate(picks, axis=1), jnp.concatenate([basis_ref[k].reshape(cells, cx) for k in range(k_count)], axis=1)
+    )
     for k in range(k_count):
-        if k % size == 0:
-            chunk_copies[k // size].wait()
-        pick = jnp.where(jnp.logical_and(wanted, pick_k == k), 1.0, 0.0).astype(BF16)
-        columns = columns + dot_nt(pick, basis_ref[k].reshape(cells, cx))
         product = basis_ref[k].astype(F32) * residual
         total = jnp.sum(jnp.sum(product, axis=0), axis=0, keepdims=True)
         partial = jnp.where(row == k, total, partial)
     b = jnp.broadcast_to(jnp.sum(partial, axis=1, keepdims=True), (k_count, LANES))
     b_ref[...] = b
-    mobility_copy.wait()
-    pick_row = iota((TILE, cx), 0)
-    pick_lane = iota((TILE, cx), 1)
-    pick = jnp.where(pick_lane == jnp.where(pick_row == 0, first, second), 1.0, 0.0).astype(BF16)
-    edge_mobility = dot_nt(pick, mobility_ref[...].reshape(cells, cx))
 
     for number, ref in ((0, x1_ref), (1, x2_ref)):
         edge = columns[number * k_count : (number + 1) * k_count]
@@ -155,54 +164,65 @@
     accumulation_copy.wait()
 
 
-def gram_kernel(basis_ref, mobility_ref, accumulation_ref, gram_ref, left_ref):
+def image_kernel(basis_ref, mobility_ref, accumulation_ref, b_ref, along_x_ref, along_y_ref, along_z_ref, image_ref):
     k_count, cz, cy, cx = basis_ref.shape
     mobility = mobility_ref[...].astype(F32)
-    accumulation = accumulation_ref[...]
     shape = mobility.shape
     along_x = jnp.where(iota(shape, 2) < cx - 1, harmonic(mobility, pltpu.roll(mobility, cx - 1, 2)), 0.0)
     along_y = jnp.where(iota(shape, 1) < cy - 1, harmonic(mobility, pltpu.roll(mobility, cy - 1, 1)), 0.0)
     along_z = VERTICAL_RATIO * harmonic(mobility[:-1], mobility[1:])
-    rows = k_count * TILE
-    strips = [(z, y) for z in range(cz) for y in range(0, cy, TILE)]
+    along_x_ref[...] = along_x
+    along_y_ref[...] = along_y
+    along_z_ref[...] = along_z
+    field = expand(basis_ref, b_ref[...])
+    flow_x = along_x * (field - pltpu.roll(field, cx - 1, 2))
+    image = accumulation_ref[...] * field + flow_x - pltpu.roll(flow_x, 1, 2)
+    flow_y = along_y * (field - pltpu.roll(field, cy - 1, 1))
+    image = image + flow_y - pltpu.roll(flow_y, 1, 1)
+    flow_z = along_z * (field[:-1] - field[1:])
+    nothing = jnp.zeros_like(field[:1])
+    image = image + jnp.concatenate([flow_z, nothing], axis=0) - jnp.concatenate([nothing, flow_z], axis=0)
+    row = iota((k_count, cx), 0)
+    partial = jnp.zeros((k_count, cx), F32)
     for k in range(k_count):
-        field = basis_ref[k].astype(F32)
-        flow_x = along_x * (field - pltpu.roll(field, cx - 1, 2))
-        image = accumulation * field + flow_x - pltpu.roll(flow_x, 1, 2)
-        flow_y = along_y * (field - pltpu.roll(field, cy - 1, 1))
-        image = image + flow_y - pltpu.roll(flow_y, 1, 1)
-        flow_z = along_z * (field[:-1] - field[1:])
-        nothing = jnp.zeros_like(field[:1])
-        image = image + jnp.concatenate([flow_z, nothing], axis=0) - jnp.concatenate([nothing, flow_z], axis=0)
-        high = image.astype(BF16)
-        low = (image - high.astype(F32)).astype(BF16)
-        for place, (z, y) in enumerate(strips):
-            lanes = slice(place * cx, (place + 1) * cx)
-            left_ref[k * TILE : (k + 1) * TILE, lanes] = high[z, y : y + TILE]
-            left_ref[rows + k * TILE : rows + (k + 1) * TILE, lanes] = low[z, y : y + TILE]
-    total = jnp.zeros((2 * rows, rows), F32)
-    for place, (z, y) in enumerate(strips):
-        right = basis_ref[:, z, y : y + TILE, :].reshape(rows, cx)
-        total = total + dot_nt(left_ref[:, place * cx : (place + 1) * cx], right)
-    total = total[:rows] + total[rows:]
-    same = lax.rem(iota((rows, rows), 0), TILE) == lax.rem(iota((rows, rows), 1), TILE)
-    total = jnp.where(same, total, 0.0)
-    gram_ref[...] = jnp.sum(total.reshape(k_count, TILE, rows), axis=1)
+        total = jnp.sum(jnp.sum(basis_ref[k].astype(F32) * image, axis=0), axis=0, keepdims=True)
+        partial = jnp.where(row == k, total, partial)
+    image_ref[...] = partial
+
+
+def energy(field, accumulation, along_x, along_y, along_z):
+    _, cy, cx = field.shape
+    change_x = field - pltpu.roll(field, cx - 1, 2)
+    change_y = field - pltpu.roll(field, cy - 1, 1)
+    change_z = field[:-1] - field[1:]
+    square = accumulation * field * field + along_x * change_x * change_x + along_y * change_y * change_y
+    square = jnp.sum(square, axis=0) + jnp.sum(along_z * change_z * change_z, axis=0)
+    return jnp.sum(square, axis=0, keepdims=True)
 
 
 def couple_kernel(
-    cz, counts, x1_ref, x2_ref, y1_ref, y2_ref, rx1_ref, rx2_ref, ry1_ref, ry2_ref, b_ref, gram_ref, out_ref
+    counts,
+    x1_ref,
+    x2_ref,
+    y1_ref,
+    y2_ref,
+    rx2_ref,
+    ry2_ref,
+    ry1_ref,
+    rx1_ref,
+    b_ref,
+    image_ref,
+    basis_ref,
+    accumulation_ref,
+    along_x_ref,
+    along_y_ref,
+    along_z_ref,
+    out_ref,
 ):
-    k_count = b_ref.shape[0]
+    k_count, cz, _, _ = basis_ref.shape
     odd_x, _ = position("gx", counts[0])
     odd_y, _ = position("gy", counts[1])
-    b = b_ref[...]
-    gram = gram_ref[...]
-    wide = gram.shape[1]
-    spread = iota((k_count, wide), 1) // TILE == iota((k_count, wide), 0)
-
-    def as_row(column):
-        return jnp.sum(jnp.where(spread, column[:, :1], 0.0), axis=0, keepdims=True)
+    b_col = b_ref[...]
 
     def unpack(ref, layers):
         blocks = [ref[z * k_count : (z + 1) * k_count, :].astype(F32) for z in range(layers)]
@@ -222,21 +242,24 @@
         other, other_mobility, other_field = unpack(other_ref, layers)
         faces.append((own, other, harmonic(own_mobility, other_mobility), own_field, other_field))
 
-    b_row = as_row(b)
-    along = jnp.zeros((k_count, LANES), F32)
+    own_image = image_ref[...]
+    along = own_image
     for own, _, conductance, own_field, other_field in faces:
         flow = conductance * (own_field - other_field)
         for z, block in enumerate(own):
             along = along + block * flow[z : z + 1]
-    image = jnp.sum(along, axis=1, keepdims=True) + jnp.sum(gram * b_row, axis=1, keepdims=True)
-    b_col = b[:, :1]
-    source_square = jnp.sum(b_col * b_col, axis=0, keepdims=True)
-    source_image = jnp.sum(b_col * image, axis=0, keepdims=True)
+    image = jnp.sum(along, axis=1, keepdims=True)
+    source_square = jnp.sum(b_col * b_col, axis=0, keepdims=True)[:, :1]
+    source_image = jnp.sum(b_col * image, axis=0, keepdims=True)[:, :1]
     quotient = source_image / jnp.maximum(source_square, TINY)
     v_col = image - quotient * b_col
-    v_row = as_row(v_col)
-
-    squares = [jnp.zeros((1, LANES), F32) for _ in range(3)]
+
+    field = expand(basis_ref, v_col)
+    squares = [
+        jnp.sum(b_col * own_image, axis=0, keepdims=True),
+        jnp.sum(v_col * own_image, axis=0, keepdims=True),
+        energy(field, accumulation_ref[...], along_x_ref[...], along_y_ref[...], along_z_ref[...]),
+    ]
     toward = []
     for own, other, conductance, own_field, _ in faces:
         v_field = jnp.concatenate([jnp.sum(block * v_col, axis=0, keepdims=True) for block in own], axis=0)
@@ -245,10 +268,6 @@
         for n, value in enumerate((flow_b * own_field, flow_b * v_field, flow_v * v_field)):
             squares[n] = squares[n] + jnp.sum(value, axis=0, keepdims=True)
         toward.append((other, flow_b, flow_v))
-    for n, (left, right) in enumerate(((b_col, b_row), (b_col, v_row), (v_col, v_row))):
-        value = jnp.sum(left * gram, axis=0, keepdims=True) * right
-        for start in range(0, wide, LANES):
-            squares[n] = squares[n] + value[:, start : start + LANES]
     squares = [jnp.sum(value, axis=1, keepdims=True) for value in squares]
 
     columns = [b_col, v_col]
@@ -351,7 +370,7 @@
     devices = counts[0] * counts[1]
     x_message = jax.ShapeDtypeStruct((k_count + TILE, cz * cy), BF16)
     y_message = jax.ShapeDtypeStruct((cz * k_count + round_up(4 * cz, TILE), cx), BF16)
-    chunks = 8 if k_count % 8 == 0 else 1
+    chunks = 1
     inputs = [pltpu.with_memory_space_constraint(x, pltpu.HBM) for x in (basis, mobility, accumulation, residual)]
     x1, x2, y1, y2, b, basis, mobility, accumulation = pl.pallas_call(
         functools.partial(edges_kernel, counts),
@@ -378,22 +397,23 @@
     rx2 = exchange(x2, "gx", counts, True)
     ry1 = exchange(y1, "gy", counts, False)
     ry2 = exchange(y2, "gy", counts, True)
-    gram = pl.pallas_call(
-        gram_kernel,
-        out_shape=jax.ShapeDtypeStruct((k_count, k_count * TILE), F32),
-        in_specs=[VMEM] * 3,
+    conductance = jax.ShapeDtypeStruct((cz, cy, cx), F32)
+    layered = jax.ShapeDtypeStruct((cz - 1, cy, cx), F32)
+    along_x, along_y, along_z, image = pl.pallas_call(
+        image_kernel,
+        out_shape=(conductance, conductance, layered, jax.ShapeDtypeStruct((k_count, cx), F32)),
+        in_specs=[VMEM] * 4,
+        out_specs=(VMEM,) * 4,
+        compiler_params=PARAMS,
+        cost_estimate=pl.CostEstimate(flops=10**8, bytes_accessed=10**6, transcendentals=0),
+    )(basis, mobility, accumulation, b)
+    row = pl.pallas_call(
+        functools.partial(couple_kernel, counts),
+        out_shape=jax.ShapeDtypeStruct((devices, LANES), F32),
+        in_specs=[VMEM] * 15,
         out_specs=VMEM,
         compiler_params=PARAMS,
-        scratch_shapes=[pltpu.VMEM((2 * k_count * TILE, cz * cy // TILE * cx), BF16)],
-        cost_estimate=pl.CostEstimate(flops=2 * 10**9, bytes_accessed=10**6, transcendentals=0),
-    )(basis, mobility, accumulation)
-    row = pl.pallas_call(
-        functools.partial(couple_kernel, cz, counts),
-        out_shape=jax.ShapeDtypeStruct((devices, LANES), F32),
-        in_specs=[VMEM] * 10,
-        out_specs=VMEM,
-        compiler_params=PARAMS,
-    )(x1, x2, y1, y2, rx1, rx2, ry1, ry2, b, gram)
+    )(x1, x2, y1, y2, rx2, ry2, ry1, rx1, b, image, basis, accumulation, along_x, along_y, along_z)
     gathered = lax.all_to_all(row, ("gx", "gy"), 0, 0, tiled=True)
     correction, solution = pl.pallas_call(
         functools.partial(finish_kernel, counts[1]),

time: 24 us -> 22.5 us (0.938)
  blocking collectives: 12.4 us -> 10 us
  starting transfers between devices: 4.49 us -> 6.27 us
  Pallas kernels: 5.23 us -> 3.69 us
  waiting for transfers between devices: 1.04 us -> 1.71 us
    all_to_all x1, blocking collectives: 12.4 us -> 10 us  [per_device(): gathered = lax.all_to_all(row, ('gx', 'gy'), 0, 0, tiled=True)]
    ppermute x4, starting transfers between devices: 4.49 us -> 6.27 us  [exchange(): return lax.ppermute(message, ('gx', 'gy'), pairs)]
    pallas_call x2, Pallas kernels: 1.75 us -> 0.81 us  [the longest x1 0.47 us: per_device(): pl.pallas_call(functools.partial(couple_kernel, counts), out_shape=jax.Sh...]
    ppermute x4, waiting for transfers between devices: 1.04 us -> 1.71 us  [exchange(): return lax.ppermute(message, ('gx', 'gy'), pairs)]
    pallas_call x1, Pallas kernels: 2.07 us -> 1.47 us  [per_device(): pl.pallas_call(functools.partial(edges_kernel, counts), out_shape=(x_mess...]
  transfers between devices with their start and end apart: 4 -> 4, of which waited for: 1 -> 1; matrix products, arithmetic and copies ran while one was open for 0% -> 0% of each run, Pallas kernels for 6% -> 2%
where the time goes in v5:
time: 22.5 us; the launch traced here: 22.3 us
  blocking collectives  10 us (44%)
  starting transfers between devices  6.27 us (28%)
  Pallas kernels  3.69 us (16%)
  waiting for transfers between devices  1.71 us (8%)
  between operations  0.65 us (3%)
    all_to_all x1, blocking collectives, per_device(): gathered = lax.all_to_all(row, ('gx', 'gy'), 0, 0, tiled=True)  10 us
    ppermute x4, starting transfers between devices, exchange(): return lax.ppermute(message, ('gx', 'gy'), pairs)  6.27 us
    ppermute x4, waiting for transfers between devices, exchange(): return lax.ppermute(message, ('gx', 'gy'), pairs)  1.71 us
    pallas_call x1, Pallas kernels, per_device(): pl.pallas_call(functools.partial(edges_kernel, counts), out_shape=(x_mess...  1.47 us
    pallas_call x1, Pallas kernels, per_device(): pl.pallas_call(functools.partial(finish_kernel, counts[1]), out_shape=(ja...  1.42 us
    pallas_call x1, Pallas kernels, per_device(): pl.pallas_call(functools.partial(couple_kernel, counts), out_shape=jax.Sh...  0.47 us
  transfers between devices with their start and end apart: 4, of which 1 were waited for; matrix products, arithmetic and copies ran while one was open for 0% of the time, Pallas kernels for 2%

profile of v5, /device:TPU:0, one launch (start us, length us, event | category | flops | bytes accessed | tf_op | source)
XLA Modules:
  0.0 22.3 jit_solution(5225021544562412117)
XLA Ops:
  0.6 1.5 %shard_map.59 = (bf16[32,128]{1,0:T(8,128)(2,1)S(1)}, bf16[32,128]{1,0:T(8,128)(2,1)S(1)}, bf16[80,128]{1,0:T(8,128)(2,1)S(1)}, bf16[80,128]{1,0:T(8,128)(2,1)S(...) custom-call(bf16[16,4,32,128]{3,2,1,0:T(8,128)(2,1)} %basis_hbm.1, ...), custom_call_target="tpu_custom_call" | custom-call | tf_op jit(solution)/shard_map/pallas_call | solution.py:375
  2.1 0.5 %collective-permute-start.1 = (bf16[80,128]{1,0:T(8,128)(2,1)S(1)}, bf16[80,128]{1,0:T(8,128)(2,1)S(1)}, u32[]{:S(2)}, u32[]{:S(2)}) collective-permute-start(bf16[80,128]{1,0:T(8,128)(2,1)S(1)} %get-tuple-element.19.y2_ref), channel_id=1, source_target_pairs={{0,4},{1,2},{2,1},{3,7},{4,0},{5,6},{6,5},{7,3},{8,12},{9,10},{10,... | collective-permute-start | bytes 61448 | tf_op jit(solution)/shard_map/ppermute | solution.py:365
  2.6 4.1 %collective-permute-start.2 = (bf16[80,128]{1,0:T(8,128)(2,1)S(1)}, bf16[80,128]{1,0:T(8,128)(2,1)S(1)}, u32[]{:S(2)}, u32[]{:S(2)}) collective-permute-start(bf16[80,128]{1,0:T(8,128)(2,1)S(1)} %get-tuple-element.18.y1_ref), channel_id=1, source_target_pairs={{0,1},{1,0},{2,3},{3,2},{4,5},{5,4},{6,7},{7,6},{8,9},{9,8},{10,11... | collective-permute-start | bytes 61448 | tf_op jit(solution)/shard_map/ppermute | solution.py:365
  6.8 0.0 collective-permute-start
  6.8 1.6 %collective-permute-start.3 = (bf16[32,128]{1,0:T(8,128)(2,1)S(1)}, bf16[32,128]{1,0:T(8,128)(2,1)S(1)}, u32[]{:S(2)}, u32[]{:S(2)}) collective-permute-start(bf16[32,128]{1,0:T(8,128)(2,1)S(1)} %get-tuple-element.16.x1_ref), channel_id=1, source_target_pairs={{0,4},{1,5},{2,6},{3,7},{4,0},{5,1},{6,2},{7,3},{8,12},{9,13},{10,... | collective-permute-start | bytes 24584 | tf_op jit(solution)/shard_map/ppermute | solution.py:365
  8.4 0.3 %shard_map.60 = (f32[4,32,128]{2,1,0:T(8,128)S(1)}, f32[4,32,128]{2,1,0:T(8,128)S(1)}, f32[3,32,128]{2,1,0:T(8,128)S(1)}, f32[16,128]{1,0:T(8,128)S(1)}) custom-call(bf16[16,4,32,128]{3,2,1,0:T(8,128)(2,1)S(1)} %get-tuple-element.21.basis_ref, bf16[4,32,128]{2,1,0:T(8,128)(2,1)S(1)} %get-tuple-element.22.mobility_ref, ...), custom_call_target="tpu_custom_call" | custom-call | flops 100000000 | bytes 1000000 | tf_op jit(solution)/shard_map/pallas_call | solution.py:402
  8.7 1.7 %collective-permute-done.rx2_ref = bf16[32,128]{1,0:T(8,128)(2,1)S(1)} collective-permute-done((bf16[32,128]{1,0:T(8,128)(2,1)S(1)}, bf16[32,128]{1,0:T(8,128)(2,1)S(1)}, u32[]{:S(2)}, u32[]{:S(2)}) %collective-permute-start) | collective-permute-done | bytes 8224 | tf_op jit(solution)/shard_map/ppermute | solution.py:365
  10.4 0.0 collective-permute-done.3.rx1_ref
  10.4 0.0 collective-permute-done.1.ry2_ref
  10.4 0.0 collective-permute-done.2.ry1_ref
  10.4 0.5 %shard_map.61.own_ref = f32[32,128]{1,0:T(8,128)S(1)} custom-call(bf16[32,128]{1,0:T(8,128)(2,1)S(1)} %get-tuple-element.16.x1_ref, bf16[32,128]{1,0:T(8,128)(2,1)S(1)} %get-tuple-element.17.x2_ref, bf16[80,128]{1,0:T(8,128)(2,1)S(1)} %get-tuple-element.18.y1_ref, bf16[80,128]{1,0:T(8,128)(2,1)S(1)} %get-tuple-element.19.y2_ref, ...), custom_call_target="tpu_custom_call" | custom-call | tf_op jit(solution)/shard_map/pallas_call | solution.py:410
  10.9 10.0 %all_to_all.11 = f32[32,1,128]{2,1,0:T(1,128)S(1)} all-to-all(f32[32,1,128]{2,1,0:T(1,128)S(1)} %bitcast.5), channel_id=1, replica_groups=mesh['gx'=8,'gy'=4] {'gx','gy'}, dimensions={0} | all-to-all | bytes 32768 | tf_op jit(solution)/shard_map/all_to_all | solution.py:417
  20.9 1.4 %shard_map.62 = (f32[4,32,128]{2,1,0:T(8,128)}, f32[1,16]{1,0:T(1,128)}) custom-call(f32[32,128]{1,0:T(8,128)S(1)} %bitcast.6, f32[32,128]{1,0:T(8,128)S(1)} %shard_map.61.own_ref, bf16[16,4,32,128]{3,2,1,0:T(8,128)(2,1)S(1)} %get-tuple-element.21.basis_ref), custom_call_target="tpu_custom_call" | custom-call | tf_op jit(solution)/shard_map/pallas_call | solution.py:418
Async XLA Ops:
  2.1 8.3 %collective-permute-start.1 = (bf16[80,128]{1,0:T(8,128)(2,1)S(1)}, bf16[80,128]{1,0:T(8,128)(2,1)S(1)}, u32[]{:S(2)}, u32[]{:S(2)}) collective-permute-start(bf16[80,128]{1,0:T(8,128)(2,1)S(1)} %get-tuple-element.19.y2_ref), channel_id=1, source_target_pairs={{0,4},{1,2},{2,1},{3,7},{4,0},{5,6},{6,5},{7,3},{8,12},{9,10},{10,... | collective-permute-start | bytes 61448 | tf_op jit(solution)/shard_map/ppermute | solution.py:365
  2.6 7.8 %collective-permute-start.2 = (bf16[80,128]{1,0:T(8,128)(2,1)S(1)}, bf16[80,128]{1,0:T(8,128)(2,1)S(1)}, u32[]{:S(2)}, u32[]{:S(2)}) collective-permute-start(bf16[80,128]{1,0:T(8,128)(2,1)S(1)} %get-tuple-element.18.y1_ref), channel_id=1, source_target_pairs={{0,1},{1,0},{2,3},{3,2},{4,5},{5,4},{6,7},{7,6},{8,9},{9,8},{10,11... | collective-permute-start | bytes 61448 | tf_op jit(solution)/shard_map/ppermute | solution.py:365
  6.8 3.7 %collective-permute-start = (bf16[32,128]{1,0:T(8,128)(2,1)S(1)}, bf16[32,128]{1,0:T(8,128)(2,1)S(1)}, u32[]{:S(2)}, u32[]{:S(2)}) collective-permute-start(bf16[32,128]{1,0:T(8,128)(2,1)S(1)} %get-tuple-element.17.x2_ref), channel_id=1, source_target_pairs={{0,1},{1,0},{2,3},{3,2},{4,8},{5,9},{6,10},{7,11},{8,4},{9,5},{10,... | collective-permute-start | bytes 24584 | tf_op jit(solution)/shard_map/ppermute | solution.py:365
  6.8 3.6 %collective-permute-start.3 = (bf16[32,128]{1,0:T(8,128)(2,1)S(1)}, bf16[32,128]{1,0:T(8,128)(2,1)S(1)}, u32[]{:S(2)}, u32[]{:S(2)}) collective-permute-start(bf16[32,128]{1,0:T(8,128)(2,1)S(1)} %get-tuple-element.16.x1_ref), channel_id=1, source_target_pairs={{0,4},{1,5},{2,6},{3,7},{4,0},{5,1},{6,2},{7,3},{8,12},{9,13},{10,... | collective-permute-start | bytes 24584 | tf_op jit(solution)/shard_map/ppermute | solution.py:365

commit v6 on v5

--- a/solution.py
+++ b/solution.py
@@ -218,6 +218,7 @@
     along_y_ref,
     along_z_ref,
     out_ref,
+    v_ref,
 ):
     k_count, cz, _, _ = basis_ref.shape
     odd_x, _ = position("gx", counts[0])
@@ -249,10 +250,12 @@
         for z, block in enumerate(own):
             along = along + block * flow[z : z + 1]
     image = jnp.sum(along, axis=1, keepdims=True)
-    source_square = jnp.sum(b_col * b_col, axis=0, keepdims=True)[:, :1]
-    source_image = jnp.sum(b_col * image, axis=0, keepdims=True)[:, :1]
+    source_square = jnp.sum(b_col * b_col, axis=0, keepdims=True)
+    source_image = jnp.sum(b_col * image, axis=0, keepdims=True)
     quotient = source_image / jnp.maximum(source_square, TINY)
     v_col = image - quotient * b_col
+    v_ref[0:k_count, :] = v_col
+    v_ref[k_count : k_count + 8, :] = jnp.broadcast_to(quotient, (8, LANES))
 
     field = expand(basis_ref, v_col)
     squares = [
@@ -261,85 +264,113 @@
         energy(field, accumulation_ref[...], along_x_ref[...], along_y_ref[...], along_z_ref[...]),
     ]
     toward = []
-    for own, other, conductance, own_field, _ in faces:
+    for own, other, conductance, own_field, other_field in faces:
         v_field = jnp.concatenate([jnp.sum(block * v_col, axis=0, keepdims=True) for block in own], axis=0)
         flow_b = conductance * own_field
         flow_v = conductance * v_field
         for n, value in enumerate((flow_b * own_field, flow_b * v_field, flow_v * v_field)):
             squares[n] = squares[n] + jnp.sum(value, axis=0, keepdims=True)
-        toward.append((other, flow_b, flow_v))
-    squares = [jnp.sum(value, axis=1, keepdims=True) for value in squares]
-
-    columns = [b_col, v_col]
+        toward.append(
+            (
+                other,
+                flow_v,
+                jnp.sum(-flow_b * other_field, axis=0, keepdims=True),
+                jnp.sum(-flow_v * other_field, axis=0, keepdims=True),
+            )
+        )
+
+    columns = [v_col]
+    source_pairs = []
+    image_pairs = []
     for first, second, odd in ((toward[0], toward[1], odd_x), (toward[2], toward[3], odd_y)):
-        for which in (1, 2):
-            product = jnp.zeros((k_count, LANES), F32)
-            for z in range(len(first[0])):
-                block = jnp.where(odd, second[0][z], first[0][z])
-                flow = jnp.where(odd, second[which], first[which])
-                product = product - block * flow[z : z + 1]
-            columns.append(jnp.sum(product, axis=1, keepdims=True))
-    lane = iota((k_count, LANES), 1)
-    own_lane = lane - iota((k_count, LANES), 0)
-    placed = jnp.zeros((k_count, LANES), F32)
-    for n, column in enumerate(columns):
-        placed = jnp.where(own_lane == n * k_count, column, placed)
-    packed = jnp.sum(placed, axis=0, keepdims=True)
-    lane = iota((1, LANES), 1)
-    base = len(columns) * k_count
-    for n, value in enumerate((quotient, *squares, source_square, source_image)):
-        packed = jnp.where(lane == base + n, value, packed)
+        product = jnp.zeros((k_count, LANES), F32)
+        for z in range(len(first[0])):
+            block = jnp.where(odd, second[0][z], first[0][z])
+            flow = jnp.where(odd, second[1], first[1])
+            product = product - block * flow[z : z + 1]
+        columns.append(jnp.sum(product, axis=1, keepdims=True))
+        source_pairs.append(jnp.where(odd, second[2], first[2]))
+        image_pairs.append(jnp.where(odd, second[3], first[3]))
+        image_pairs.append(jnp.where(odd, first[3], second[3]))
+    row = iota((TILE, LANES), 0)
+    sums = jnp.zeros((TILE, LANES), F32)
+    for n, value in enumerate((*squares, *source_pairs, *image_pairs)):
+        sums = jnp.where(row == n, value, sums)
+    scalars = jnp.broadcast_to(jnp.sum(sums, axis=1, keepdims=True), (TILE, LANES))
+    v_square = jnp.sum(v_col * v_col, axis=0, keepdims=True)
+    source_v = jnp.sum(v_col * b_col, axis=0, keepdims=True)
+    for n, value in enumerate((quotient, source_square, source_image, source_v, v_square)):
+        scalars = jnp.where(row == 9 + n, value, scalars)
+    packed = jnp.zeros((1, LANES), F32)
+    for n, column in enumerate((*columns, scalars)):
+        size = column.shape[0]
+        place = iota((size, LANES), 1) - iota((size, LANES), 0) == n * k_count
+        packed = packed + jnp.sum(jnp.where(place, column, 0.0), axis=0, keepdims=True)
     out_ref[...] = jnp.broadcast_to(packed, out_ref.shape)
 
 
-def finish_kernel(count_y, gathered_ref, own_ref, basis_ref, correction_hbm, solution_hbm, correction_ref, solution_ref, sems):
+def finish_kernel(
+    count_y,
+    gathered_ref,
+    b_ref,
+    v_ref,
+    basis_ref,
+    correction_hbm,
+    solution_hbm,
+    correction_ref,
+    solution_ref,
+    sems,
+):
     k_count, cz, cy, cx = basis_ref.shape
-    base = 6 * k_count
+    base = 3 * k_count
     every = gathered_ref[...]
+
+    def rows(x, amount):
+        amount = amount % x.shape[0]
+        return jnp.concatenate([x[amount:], x[:amount]], axis=0)
+
+    def column(n):
+        return jnp.broadcast_to(every[:, base + n : base + n + 1], every.shape)
+
+    def total(x):
+        return jnp.sum(x, axis=0, keepdims=True)
+
+    sums = total(every)
+    energy_sum = jnp.broadcast_to(sums[:, base + 10 : base + 11], sums.shape)
+    image_sum = jnp.broadcast_to(sums[:, base + 11 : base + 12], sums.shape)
     lane = iota(every.shape, 1)
-
-    def total(x):
-        return jnp.sum(jnp.sum(x, axis=0, keepdims=True), axis=1, keepdims=True)
-
-    def shifted(x, amount):
-        return pltpu.roll(x, LANES - amount, 1)
-
-    def up_rows(x, amount):
-        return jnp.concatenate([x[amount:], x[:amount]], axis=0)
-
-    sums = jnp.sum(every, axis=0, keepdims=True)
-    energy = sums[:, base + 4 : base + 5]
-    step = energy / (sums[:, base + 5 : base + 6] + EPSILON)
-    quotient = every[:, base : base + 1]
-    beside = shifted(every, k_count)
-    remainder = every - step * (quotient * every + beside)
-    renewed = total(jnp.where(lane < k_count, remainder * remainder, 0.0))
-    ratio = renewed / (energy + EPSILON)
-    weight = 1.0 + ratio - step * quotient
-    mixed = weight * every - step * beside
-    direction = jnp.where(lane < k_count, mixed, 0.0)
-    cross = shifted(mixed, 2 * k_count) * up_rows(direction, count_y) + shifted(mixed, 4 * k_count) * up_rows(direction, 1)
-    own_part = (
-        weight * weight * every[:, base + 1 : base + 2]
-        - 2.0 * weight * step * every[:, base + 2 : base + 3]
-        + step * step * every[:, base + 3 : base + 4]
-    )
-    curvature = total(2.0 * cross) + jnp.sum(own_part, axis=0, keepdims=True)
+    vectors = pltpu.roll(every, LANES - k_count, 1) * rows(every, count_y)
+    vectors = vectors + pltpu.roll(every, LANES - 2 * k_count, 1) * rows(every, 1)
+    v_image_v = jnp.where(lane < k_count, 2.0 * vectors, jnp.where(lane == base + 2, every, 0.0))
+    v_image_v = jnp.sum(total(v_image_v), axis=1, keepdims=True)
+    quotient = column(9)
+    quotient_x = rows(quotient, count_y)
+    quotient_y = rows(quotient, 1)
+    square_b, b_v, square_v = column(10), column(12), column(13)
+    b_image_b, pair_x, pair_y = column(0), 2.0 * column(3), 2.0 * column(4)
+    b_image_v = column(1) + rows(column(5), -count_y) + rows(column(6), count_y) + rows(column(7), -1) + rows(column(8), 1)
+
+    step = energy_sum / (image_sum + EPSILON)
+    left = 1.0 - step * quotient
+    renewed = total(left * (left * square_b - 2.0 * step * b_v) + step * step * square_v)
+    ratio = renewed / (energy_sum + EPSILON)
+    weight = left + ratio
+    weight_x = 1.0 + ratio - step * quotient_x
+    weight_y = 1.0 + ratio - step * quotient_y
+    curvature = total(weight * (weight * b_image_b + weight_x * pair_x + weight_y * pair_y - 2.0 * step * b_image_v))
+    curvature = curvature + step * step * v_image_v
     last_step = renewed / (curvature + EPSILON)
 
-    own = own_ref[0:1, :]
-    own_weight = 1.0 + ratio - step * own[:, base : base + 1]
-    own_direction = own_weight * own - step * shifted(own, k_count)
-    solution = step * own + last_step * own_direction
-    solution_ref[...] = solution[:, :k_count]
+    own_weight = 1.0 + ratio - step * v_ref[k_count : k_count + 1, :]
+    solution = (step + last_step * own_weight) * b_ref[...] - last_step * step * v_ref[0:k_count, :]
+    place = iota(solution.shape, 0) == iota(solution.shape, 1)
+    solution_ref[...] = total(jnp.where(place, solution, 0.0))[:, :k_count]
     copies = [pltpu.make_async_copy(solution_ref, solution_hbm, sems.at[cz])]
     copies[0].start()
-    spread = iota((k_count, LANES), 0) == iota((k_count, LANES), 1)
-    column = jnp.sum(jnp.where(spread, solution, 0.0), axis=1, keepdims=True)
     for z in range(cz):
         layer = jnp.zeros((cy, cx), F32)
         for k in range(k_count):
-            layer = layer + basis_ref[k, z].astype(F32) * column[k : k + 1]
+            layer = layer + basis_ref[k, z].astype(F32) * solution[k : k + 1]
         correction_ref[z] = layer
         copy = pltpu.make_async_copy(correction_ref.at[z], correction_hbm.at[z], sems.at[z])
         copy.start()
@@ -407,18 +438,18 @@
         compiler_params=PARAMS,
         cost_estimate=pl.CostEstimate(flops=10**8, bytes_accessed=10**6, transcendentals=0),
     )(basis, mobility, accumulation, b)
-    row = pl.pallas_call(
+    row, v = pl.pallas_call(
         functools.partial(couple_kernel, counts),
-        out_shape=jax.ShapeDtypeStruct((devices, LANES), F32),
+        out_shape=(jax.ShapeDtypeStruct((devices, LANES), F32), jax.ShapeDtypeStruct((k_count + 8, LANES), F32)),
         in_specs=[VMEM] * 15,
-        out_specs=VMEM,
+        out_specs=(VMEM, VMEM),
         compiler_params=PARAMS,
     )(x1, x2, y1, y2, rx2, ry2, ry1, rx1, b, image, basis, accumulation, along_x, along_y, along_z)
     gathered = lax.all_to_all(row, ("gx", "gy"), 0, 0, tiled=True)
     correction, solution = pl.pallas_call(
         functools.partial(finish_kernel, counts[1]),
         out_shape=(jax.ShapeDtypeStruct((cz, cy, cx), F32), jax.ShapeDtypeStruct((1, k_count), F32)),
-        in_specs=[VMEM] * 3,
+        in_specs=[VMEM] * 4,
         out_specs=(HBM, HBM),
         scratch_shapes=[
             pltpu.VMEM((cz, cy, cx), F32),
@@ -426,7 +457,7 @@
             pltpu.SemaphoreType.DMA((cz + 1,)),
         ],
         compiler_params=PARAMS,
-    )(gathered, row, basis)
+    )(gathered, b, v, basis)
     return correction, solution.reshape(1, 1, k_count)
 
 

time: 22.5 us -> 22 us (0.978)
  Pallas kernels: 3.69 us -> 3.18 us
    pallas_call x1, Pallas kernels: 1.42 us -> 0.95 us  [per_device(): pl.pallas_call(functools.partial(finish_kernel, counts[1]), out_shape=(ja...]
where the time goes in v6:
time: 22 us; the launch traced here: 21.8 us
  blocking collectives  9.99 us (45%)
  starting transfers between devices  6.27 us (28%)
  Pallas kernels  3.18 us (14%)
  waiting for transfers between devices  1.7 us (8%)
  between operations  0.65 us (3%)
    all_to_all x1, blocking collectives, per_device(): gathered = lax.all_to_all(row, ('gx', 'gy'), 0, 0, tiled=True)  9.99 us
    ppermute x4, starting transfers between devices, exchange(): return lax.ppermute(message, ('gx', 'gy'), pairs)  6.27 us
    ppermute x4, waiting for transfers between devices, exchange(): return lax.ppermute(message, ('gx', 'gy'), pairs)  1.7 us
    pallas_call x1, Pallas kernels, per_device(): pl.pallas_call(functools.partial(edges_kernel, counts), out_shape=(x_mess...  1.47 us
    pallas_call x1, Pallas kernels, per_device(): pl.pallas_call(functools.partial(finish_kernel, counts[1]), out_shape=(ja...  0.95 us
  transfers between devices with their start and end apart: 4, of which 1 were waited for; matrix products, arithmetic and copies ran while one was open for 0% of the time, Pallas kernels for 2%

profile of v6, /device:TPU:0, one launch (start us, length us, event | category | flops | bytes accessed | tf_op | source)
XLA Modules:
  0.0 21.8 jit_solution(2740160093771396950)
XLA Ops:
  0.6 1.5 %shard_map.59 = (bf16[32,128]{1,0:T(8,128)(2,1)S(1)}, bf16[32,128]{1,0:T(8,128)(2,1)S(1)}, bf16[80,128]{1,0:T(8,128)(2,1)S(1)}, bf16[80,128]{1,0:T(8,128)(2,1)S(...) custom-call(bf16[16,4,32,128]{3,2,1,0:T(8,128)(2,1)} %basis_hbm.1, ...), custom_call_target="tpu_custom_call" | custom-call | tf_op jit(solution)/shard_map/pallas_call | solution.py:406
  2.1 0.5 %collective-permute-start.1 = (bf16[80,128]{1,0:T(8,128)(2,1)S(1)}, bf16[80,128]{1,0:T(8,128)(2,1)S(1)}, u32[]{:S(2)}, u32[]{:S(2)}) collective-permute-start(bf16[80,128]{1,0:T(8,128)(2,1)S(1)} %get-tuple-element.21.y2_ref), channel_id=1, source_target_pairs={{0,4},{1,2},{2,1},{3,7},{4,0},{5,6},{6,5},{7,3},{8,12},{9,10},{10,... | collective-permute-start | bytes 61448 | tf_op jit(solution)/shard_map/ppermute | solution.py:396
  2.6 4.1 %collective-permute-start.2 = (bf16[80,128]{1,0:T(8,128)(2,1)S(1)}, bf16[80,128]{1,0:T(8,128)(2,1)S(1)}, u32[]{:S(2)}, u32[]{:S(2)}) collective-permute-start(bf16[80,128]{1,0:T(8,128)(2,1)S(1)} %get-tuple-element.20.y1_ref), channel_id=1, source_target_pairs={{0,1},{1,0},{2,3},{3,2},{4,5},{5,4},{6,7},{7,6},{8,9},{9,8},{10,11... | collective-permute-start | bytes 61448 | tf_op jit(solution)/shard_map/ppermute | solution.py:396
  6.8 0.0 collective-permute-start
  6.8 1.6 %collective-permute-start.3 = (bf16[32,128]{1,0:T(8,128)(2,1)S(1)}, bf16[32,128]{1,0:T(8,128)(2,1)S(1)}, u32[]{:S(2)}, u32[]{:S(2)}) collective-permute-start(bf16[32,128]{1,0:T(8,128)(2,1)S(1)} %get-tuple-element.18.x1_ref), channel_id=1, source_target_pairs={{0,4},{1,5},{2,6},{3,7},{4,0},{5,1},{6,2},{7,3},{8,12},{9,13},{10,... | collective-permute-start | bytes 24584 | tf_op jit(solution)/shard_map/ppermute | solution.py:396
  8.4 0.3 %shard_map.60 = (f32[4,32,128]{2,1,0:T(8,128)S(1)}, f32[4,32,128]{2,1,0:T(8,128)S(1)}, f32[3,32,128]{2,1,0:T(8,128)S(1)}, f32[16,128]{1,0:T(8,128)S(1)}) custom-call(bf16[16,4,32,128]{3,2,1,0:T(8,128)(2,1)S(1)} %get-tuple-element.23.basis_ref, bf16[4,32,128]{2,1,0:T(8,128)(2,1)S(1)} %get-tuple-element.24.mobility_ref, ...), custom_call_target="tpu_custom_call" | custom-call | flops 100000000 | bytes 1000000 | tf_op jit(solution)/shard_map/pallas_call | solution.py:433
  8.7 1.7 %collective-permute-done.rx2_ref = bf16[32,128]{1,0:T(8,128)(2,1)S(1)} collective-permute-done((bf16[32,128]{1,0:T(8,128)(2,1)S(1)}, bf16[32,128]{1,0:T(8,128)(2,1)S(1)}, u32[]{:S(2)}, u32[]{:S(2)}) %collective-permute-start) | collective-permute-done | bytes 8224 | tf_op jit(solution)/shard_map/ppermute | solution.py:396
  10.4 0.0 collective-permute-done.3.rx1_ref
  10.4 0.0 collective-permute-done.1.ry2_ref
  10.4 0.0 collective-permute-done.2.ry1_ref
  10.4 0.4 %shard_map.61 = (f32[32,128]{1,0:T(8,128)S(1)}, f32[24,128]{1,0:T(8,128)S(1)}) custom-call(bf16[32,128]{1,0:T(8,128)(2,1)S(1)} %get-tuple-element.18.x1_ref, bf16[32,128]{1,0:T(8,128)(2,1)S(1)} %get-tuple-element.19.x2_ref, bf16[80,128]{1,0:T(8,128)(2,1)S(1)} %get-tuple-element.20.y1_ref, bf16[80,128]{1,0:T(8,128)(2,1)S(1)} %get-tuple-element.21.y2_ref, ...), custom_call_target="tpu_custom_call" | custom-call | tf_op jit(solution)/shard_map/pallas_call | solution.py:441
  10.9 10.0 %all_to_all.11 = f32[32,1,128]{2,1,0:T(1,128)S(1)} all-to-all(f32[32,1,128]{2,1,0:T(1,128)S(1)} %bitcast.6), channel_id=1, replica_groups=mesh['gx'=8,'gy'=4] {'gx','gy'}, dimensions={0} | all-to-all | bytes 32768 | tf_op jit(solution)/shard_map/all_to_all | solution.py:448
  20.8 1.0 %shard_map.62 = (f32[4,32,128]{2,1,0:T(8,128)}, f32[1,16]{1,0:T(1,128)}) custom-call(f32[32,128]{1,0:T(8,128)S(1)} %bitcast.5, f32[16,128]{1,0:T(8,128)S(1)} %get-tuple-element.22.b_ref, f32[24,128]{1,0:T(8,128)S(1)} %get-tuple-element.31.v_ref, bf16[16,4,32,128]{3,2,1,0:T(8,128)(2,1)S(1)} %get-tuple-element.23.basis_ref), custom_call_target="tpu_custom_call" | custom-call | tf_op jit(solution)/shard_map/pallas_call | solution.py:449
Async XLA Ops:
  2.1 8.3 %collective-permute-start.1 = (bf16[80,128]{1,0:T(8,128)(2,1)S(1)}, bf16[80,128]{1,0:T(8,128)(2,1)S(1)}, u32[]{:S(2)}, u32[]{:S(2)}) collective-permute-start(bf16[80,128]{1,0:T(8,128)(2,1)S(1)} %get-tuple-element.21.y2_ref), channel_id=1, source_target_pairs={{0,4},{1,2},{2,1},{3,7},{4,0},{5,6},{6,5},{7,3},{8,12},{9,10},{10,... | collective-permute-start | bytes 61448 | tf_op jit(solution)/shard_map/ppermute | solution.py:396
  2.6 7.8 %collective-permute-start.2 = (bf16[80,128]{1,0:T(8,128)(2,1)S(1)}, bf16[80,128]{1,0:T(8,128)(2,1)S(1)}, u32[]{:S(2)}, u32[]{:S(2)}) collective-permute-start(bf16[80,128]{1,0:T(8,128)(2,1)S(1)} %get-tuple-element.20.y1_ref), channel_id=1, source_target_pairs={{0,1},{1,0},{2,3},{3,2},{4,5},{5,4},{6,7},{7,6},{8,9},{9,8},{10,11... | collective-permute-start | bytes 61448 | tf_op jit(solution)/shard_map/ppermute | solution.py:396
  6.8 3.7 %collective-permute-start = (bf16[32,128]{1,0:T(8,128)(2,1)S(1)}, bf16[32,128]{1,0:T(8,128)(2,1)S(1)}, u32[]{:S(2)}, u32[]{:S(2)}) collective-permute-start(bf16[32,128]{1,0:T(8,128)(2,1)S(1)} %get-tuple-element.19.x2_ref), channel_id=1, source_target_pairs={{0,1},{1,0},{2,3},{3,2},{4,8},{5,9},{6,10},{7,11},{8,4},{9,5},{10,... | collective-permute-start | bytes 24584 | tf_op jit(solution)/shard_map/ppermute | solution.py:396
  6.8 3.6 %collective-permute-start.3 = (bf16[32,128]{1,0:T(8,128)(2,1)S(1)}, bf16[32,128]{1,0:T(8,128)(2,1)S(1)}, u32[]{:S(2)}, u32[]{:S(2)}) collective-permute-start(bf16[32,128]{1,0:T(8,128)(2,1)S(1)} %get-tuple-element.18.x1_ref), channel_id=1, source_target_pairs={{0,4},{1,5},{2,6},{3,7},{4,0},{5,1},{6,2},{7,3},{8,12},{9,13},{10,... | collective-permute-start | bytes 24584 | tf_op jit(solution)/shard_map/ppermute | solution.py:396

commit v7 on v6

--- a/solution.py
+++ b/solution.py
@@ -73,22 +73,15 @@
     mobility_ref,
     accumulation_ref,
     residual_ref,
-    chunk_sems,
     sems,
 ):
     k_count, cz, cy, cx = basis_ref.shape
-    chunks = chunk_sems.shape[0]
-    size = k_count // chunks
+    mobility_copy = pltpu.make_async_copy(mobility_hbm, mobility_ref, sems.at[1])
+    mobility_copy.start()
     residual_copy = pltpu.make_async_copy(residual_hbm, residual_ref, sems.at[0])
     residual_copy.start()
-    chunk_copies = []
-    for n in range(chunks):
-        part = slice(n * size, (n + 1) * size)
-        copy = pltpu.make_async_copy(basis_hbm.at[part], basis_ref.at[part], chunk_sems.at[n])
-        copy.start()
-        chunk_copies.append(copy)
-    mobility_copy = pltpu.make_async_copy(mobility_hbm, mobility_ref, sems.at[1])
-    mobility_copy.start()
+    basis_copy = pltpu.make_async_copy(basis_hbm, basis_ref, sems.at[3])
+    basis_copy.start()
     accumulation_copy = pltpu.make_async_copy(accumulation_hbm, accumulation_ref, sems.at[2])
     accumulation_copy.start()
     cells = cz * cy
@@ -112,8 +105,7 @@
 
     row = iota((k_count, cx), 0)
     partial = jnp.zeros((k_count, cx), F32)
-    for copy in chunk_copies:
-        copy.wait()
+    basis_copy.wait()
     columns = dot_nt(
         jnp.concatenate(picks, axis=1), jnp.concatenate([basis_ref[k].reshape(cells, cx) for k in range(k_count)], axis=1)
     )
@@ -164,7 +156,9 @@
     accumulation_copy.wait()
 
 
-def image_kernel(basis_ref, mobility_ref, accumulation_ref, b_ref, along_x_ref, along_y_ref, along_z_ref, image_ref):
+def image_kernel(
+    basis_ref, mobility_ref, accumulation_ref, b_ref, along_x_ref, along_y_ref, along_z_ref, image_ref, field_ref
+):
     k_count, cz, cy, cx = basis_ref.shape
     mobility = mobility_ref[...].astype(F32)
     shape = mobility.shape
@@ -175,6 +169,7 @@
     along_y_ref[...] = along_y
     along_z_ref[...] = along_z
     field = expand(basis_ref, b_ref[...])
+    field_ref[...] = field
     flow_x = along_x * (field - pltpu.roll(field, cx - 1, 2))
     image = accumulation_ref[...] * field + flow_x - pltpu.roll(flow_x, 1, 2)
     flow_y = along_y * (field - pltpu.roll(field, cy - 1, 1))
@@ -202,10 +197,10 @@
 
 def couple_kernel(
     counts,
+    y2_ref,
+    y1_ref,
+    x2_ref,
     x1_ref,
-    x2_ref,
-    y1_ref,
-    y2_ref,
     rx2_ref,
     ry2_ref,
     ry1_ref,
@@ -219,6 +214,7 @@
     along_z_ref,
     out_ref,
     v_ref,
+    field_ref,
 ):
     k_count, cz, _, _ = basis_ref.shape
     odd_x, _ = position("gx", counts[0])
@@ -258,6 +254,7 @@
     v_ref[k_count : k_count + 8, :] = jnp.broadcast_to(quotient, (8, LANES))
 
     field = expand(basis_ref, v_col)
+    field_ref[...] = field
     squares = [
         jnp.sum(b_col * own_image, axis=0, keepdims=True),
         jnp.sum(v_col * own_image, axis=0, keepdims=True),
@@ -314,14 +311,16 @@
     gathered_ref,
     b_ref,
     v_ref,
-    basis_ref,
+    b_field_ref,
+    v_field_ref,
     correction_hbm,
     solution_hbm,
     correction_ref,
     solution_ref,
     sems,
 ):
-    k_count, cz, cy, cx = basis_ref.shape
+    k_count = b_ref.shape[0]
+    cz = correction_ref.shape[0]
     base = 3 * k_count
     every = gathered_ref[...]
 
@@ -362,16 +361,15 @@
     last_step = renewed / (curvature + EPSILON)
 
     own_weight = 1.0 + ratio - step * v_ref[k_count : k_count + 1, :]
-    solution = (step + last_step * own_weight) * b_ref[...] - last_step * step * v_ref[0:k_count, :]
+    b_part = step + last_step * own_weight
+    v_part = -last_step * step
+    solution = b_part * b_ref[...] + v_part * v_ref[0:k_count, :]
     place = iota(solution.shape, 0) == iota(solution.shape, 1)
     solution_ref[...] = total(jnp.where(place, solution, 0.0))[:, :k_count]
     copies = [pltpu.make_async_copy(solution_ref, solution_hbm, sems.at[cz])]
     copies[0].start()
     for z in range(cz):
-        layer = jnp.zeros((cy, cx), F32)
-        for k in range(k_count):
-            layer = layer + basis_ref[k, z].astype(F32) * solution[k : k + 1]
-        correction_ref[z] = layer
+        correction_ref[z] = b_part * b_field_ref[z] + v_part * v_field_ref[z]
         copy = pltpu.make_async_copy(correction_ref.at[z], correction_hbm.at[z], sems.at[z])
         copy.start()
         copies.append(copy)
@@ -401,7 +399,6 @@
     devices = counts[0] * counts[1]
     x_message = jax.ShapeDtypeStruct((k_count + TILE, cz * cy), BF16)
     y_message = jax.ShapeDtypeStruct((cz * k_count + round_up(4 * cz, TILE), cx), BF16)
-    chunks = 1
     inputs = [pltpu.with_memory_space_constraint(x, pltpu.HBM) for x in (basis, mobility, accumulation, residual)]
     x1, x2, y1, y2, b, basis, mobility, accumulation = pl.pallas_call(
         functools.partial(edges_kernel, counts),
@@ -419,8 +416,7 @@
         out_specs=(VMEM,) * 8,
         scratch_shapes=[
             pltpu.VMEM(residual.shape, F32),
-            pltpu.SemaphoreType.DMA((chunks,)),
-            pltpu.SemaphoreType.DMA((3,)),
+            pltpu.SemaphoreType.DMA((4,)),
         ],
         compiler_params=PARAMS,
     )(*inputs)
@@ -430,26 +426,30 @@
     ry2 = exchange(y2, "gy", counts, True)
     conductance = jax.ShapeDtypeStruct((cz, cy, cx), F32)
     layered = jax.ShapeDtypeStruct((cz - 1, cy, cx), F32)
-    along_x, along_y, along_z, image = pl.pallas_call(
+    along_x, along_y, along_z, image, b_field = pl.pallas_call(
         image_kernel,
-        out_shape=(conductance, conductance, layered, jax.ShapeDtypeStruct((k_count, cx), F32)),
+        out_shape=(conductance, conductance, layered, jax.ShapeDtypeStruct((k_count, cx), F32), conductance),
         in_specs=[VMEM] * 4,
-        out_specs=(VMEM,) * 4,
+        out_specs=(VMEM,) * 5,
         compiler_params=PARAMS,
         cost_estimate=pl.CostEstimate(flops=10**8, bytes_accessed=10**6, transcendentals=0),
     )(basis, mobility, accumulation, b)
-    row, v = pl.pallas_call(
+    row, v, v_field = pl.pallas_call(
         functools.partial(couple_kernel, counts),
-        out_shape=(jax.ShapeDtypeStruct((devices, LANES), F32), jax.ShapeDtypeStruct((k_count + 8, LANES), F32)),
+        out_shape=(
+            jax.ShapeDtypeStruct((devices, LANES), F32),
+            jax.ShapeDtypeStruct((k_count + 8, LANES), F32),
+            conductance,
+        ),
         in_specs=[VMEM] * 15,
-        out_specs=(VMEM, VMEM),
+        out_specs=(VMEM,) * 3,
         compiler_params=PARAMS,
-    )(x1, x2, y1, y2, rx2, ry2, ry1, rx1, b, image, basis, accumulation, along_x, along_y, along_z)
+    )(y2, y1, x2, x1, rx2, ry2, ry1, rx1, b, image, basis, accumulation, along_x, along_y, along_z)
     gathered = lax.all_to_all(row, ("gx", "gy"), 0, 0, tiled=True)
     correction, solution = pl.pallas_call(
         functools.partial(finish_kernel, counts[1]),
         out_shape=(jax.ShapeDtypeStruct((cz, cy, cx), F32), jax.ShapeDtypeStruct((1, k_count), F32)),
-        in_specs=[VMEM] * 4,
+        in_specs=[VMEM] * 5,
         out_specs=(HBM, HBM),
         scratch_shapes=[
             pltpu.VMEM((cz, cy, cx), F32),
@@ -457,7 +457,7 @@
             pltpu.SemaphoreType.DMA((cz + 1,)),
         ],
         compiler_params=PARAMS,
-    )(gathered, b, v, basis)
+    )(gathered, b, v, b_field, v_field)
     return correction, solution.reshape(1, 1, k_count)
 
 

time: 22 us -> 21.9 us (level)
  no operation moved by 1% of the time
where the time goes in v7:
time: 21.9 us; the launch traced here: 21.7 us
  blocking collectives  9.99 us (46%)
  starting transfers between devices  6.27 us (29%)
  Pallas kernels  3.12 us (14%)
  waiting for transfers between devices  1.69 us (8%)
  between operations  0.65 us (3%)
    all_to_all x1, blocking collectives, per_device(): gathered = lax.all_to_all(row, ('gx', 'gy'), 0, 0, tiled=True)  9.99 us
    ppermute x4, starting transfers between devices, exchange(): return lax.ppermute(message, ('gx', 'gy'), pairs)  6.27 us
    ppermute x4, waiting for transfers between devices, exchange(): return lax.ppermute(message, ('gx', 'gy'), pairs)  1.69 us
    pallas_call x1, Pallas kernels, per_device(): pl.pallas_call(functools.partial(edges_kernel, counts), out_shape=(x_mess...  1.47 us
    pallas_call x1, Pallas kernels, per_device(): pl.pallas_call(functools.partial(finish_kernel, counts[1]), out_shape=(ja...  0.88 us
  transfers between devices with their start and end apart: 4, of which 1 were waited for; matrix products, arithmetic and copies ran while one was open for 0% of the time, Pallas kernels for 2%

profile of v7, /device:TPU:0, one launch (start us, length us, event | category | flops | bytes accessed | tf_op | source)
XLA Modules:
  0.0 21.7 jit_solution(10352006209984007437)
XLA Ops:
  0.6 1.5 %shard_map.59 = (bf16[32,128]{1,0:T(8,128)(2,1)S(1)}, bf16[32,128]{1,0:T(8,128)(2,1)S(1)}, bf16[80,128]{1,0:T(8,128)(2,1)S(1)}, bf16[80,128]{1,0:T(8,128)(2,1)S(...) custom-call(bf16[16,4,32,128]{3,2,1,0:T(8,128)(2,1)} %basis_hbm.1, ...), custom_call_target="tpu_custom_call" | custom-call | tf_op jit(solution)/shard_map/pallas_call | solution.py:403
  2.1 0.5 %collective-permute-start.1 = (bf16[80,128]{1,0:T(8,128)(2,1)S(1)}, bf16[80,128]{1,0:T(8,128)(2,1)S(1)}, u32[]{:S(2)}, u32[]{:S(2)}) collective-permute-start(bf16[80,128]{1,0:T(8,128)(2,1)S(1)} %get-tuple-element.20.y2_ref), channel_id=1, source_target_pairs={{0,4},{1,2},{2,1},{3,7},{4,0},{5,6},{6,5},{7,3},{8,12},{9,10},{10,... | collective-permute-start | bytes 61448 | tf_op jit(solution)/shard_map/ppermute | solution.py:394
  2.6 4.1 %collective-permute-start.2 = (bf16[80,128]{1,0:T(8,128)(2,1)S(1)}, bf16[80,128]{1,0:T(8,128)(2,1)S(1)}, u32[]{:S(2)}, u32[]{:S(2)}) collective-permute-start(bf16[80,128]{1,0:T(8,128)(2,1)S(1)} %get-tuple-element.21.y1_ref), channel_id=1, source_target_pairs={{0,1},{1,0},{2,3},{3,2},{4,5},{5,4},{6,7},{7,6},{8,9},{9,8},{10,11... | collective-permute-start | bytes 61448 | tf_op jit(solution)/shard_map/ppermute | solution.py:394
  6.8 0.0 collective-permute-start
  6.8 1.6 %collective-permute-start.3 = (bf16[32,128]{1,0:T(8,128)(2,1)S(1)}, bf16[32,128]{1,0:T(8,128)(2,1)S(1)}, u32[]{:S(2)}, u32[]{:S(2)}) collective-permute-start(bf16[32,128]{1,0:T(8,128)(2,1)S(1)} %get-tuple-element.23.x1_ref), channel_id=1, source_target_pairs={{0,4},{1,5},{2,6},{3,7},{4,0},{5,1},{6,2},{7,3},{8,12},{9,13},{10,... | collective-permute-start | bytes 24584 | tf_op jit(solution)/shard_map/ppermute | solution.py:394
  8.4 0.4 %shard_map.60 = (f32[4,32,128]{2,1,0:T(8,128)S(1)}, f32[4,32,128]{2,1,0:T(8,128)S(1)}, f32[3,32,128]{2,1,0:T(8,128)S(1)}, f32[16,128]{1,0:T(8,128)S(1)}, f32[4,32,128]{2,1,0:T(8,128)S(1)}) custom-call(bf16[16,4,32,128]{3,2,1,0:T(8,128)(2,1)S(1)} %get-tuple-element.25.basis_ref, bf16[4,32,128]{2,1,0:T(8,128)(2,1)S(1)} %get-tuple-element.26.mobility_ref, ...), custom_call_target="tpu_custom_call" | custom-call | flops 100000000 | bytes 1000000 | tf_op jit(solution)/shard_map/pallas_call | solution.py:429
  8.7 1.7 %collective-permute-done.rx2_ref = bf16[32,128]{1,0:T(8,128)(2,1)S(1)} collective-permute-done((bf16[32,128]{1,0:T(8,128)(2,1)S(1)}, bf16[32,128]{1,0:T(8,128)(2,1)S(1)}, u32[]{:S(2)}, u32[]{:S(2)}) %collective-permute-start) | collective-permute-done | bytes 8224 | tf_op jit(solution)/shard_map/ppermute | solution.py:394
  10.4 0.0 collective-permute-done.3.rx1_ref
  10.4 0.0 collective-permute-done.1.ry2_ref
  10.4 0.0 collective-permute-done.2.ry1_ref
  10.4 0.4 %shard_map.61 = (f32[32,128]{1,0:T(8,128)S(1)}, f32[24,128]{1,0:T(8,128)S(1)}, f32[4,32,128]{2,1,0:T(8,128)S(1)}) custom-call(bf16[80,128]{1,0:T(8,128)(2,1)S(1)} %get-tuple-element.20.y2_ref, bf16[80,128]{1,0:T(8,128)(2,1)S(1)} %get-tuple-element.21.y1_ref, bf16[32,128]{1,0:T(8,128)(2,1)S(1)} %get-tuple-element.22.x2_ref, ...), custom_call_target="tpu_custom_call" | custom-call | tf_op jit(solution)/shard_map/pallas_call | solution.py:437
  10.9 10.0 %all_to_all.11 = f32[32,1,128]{2,1,0:T(1,128)S(1)} all-to-all(f32[32,1,128]{2,1,0:T(1,128)S(1)} %bitcast.6), channel_id=1, replica_groups=mesh['gx'=8,'gy'=4] {'gx','gy'}, dimensions={0} | all-to-all | bytes 32768 | tf_op jit(solution)/shard_map/all_to_all | solution.py:448
  20.8 0.9 %shard_map.62 = (f32[4,32,128]{2,1,0:T(8,128)}, f32[1,16]{1,0:T(1,128)}) custom-call(f32[32,128]{1,0:T(8,128)S(1)} %bitcast.5, f32[16,128]{1,0:T(8,128)S(1)} %get-tuple-element.24.b_ref, f32[24,128]{1,0:T(8,128)S(1)} %get-tuple-element.33.v_ref, f32[4,32,128]{2,1,0:T(8,128)S(1)} %get-tuple-element.34.b_field_ref, f32[4,32,128]{2,1,0:T(8,128)S(1)} %get-tuple-element.35.v_field_ref), custom_call_target="tpu_custom_call" | custom-call | tf_op jit(solution)/shard_map/pallas_call | solution.py:449
Async XLA Ops:
  2.1 8.3 %collective-permute-start.1 = (bf16[80,128]{1,0:T(8,128)(2,1)S(1)}, bf16[80,128]{1,0:T(8,128)(2,1)S(1)}, u32[]{:S(2)}, u32[]{:S(2)}) collective-permute-start(bf16[80,128]{1,0:T(8,128)(2,1)S(1)} %get-tuple-element.20.y2_ref), channel_id=1, source_target_pairs={{0,4},{1,2},{2,1},{3,7},{4,0},{5,6},{6,5},{7,3},{8,12},{9,10},{10,... | collective-permute-start | bytes 61448 | tf_op jit(solution)/shard_map/ppermute | solution.py:394
  2.6 7.8 %collective-permute-start.2 = (bf16[80,128]{1,0:T(8,128)(2,1)S(1)}, bf16[80,128]{1,0:T(8,128)(2,1)S(1)}, u32[]{:S(2)}, u32[]{:S(2)}) collective-permute-start(bf16[80,128]{1,0:T(8,128)(2,1)S(1)} %get-tuple-element.21.y1_ref), channel_id=1, source_target_pairs={{0,1},{1,0},{2,3},{3,2},{4,5},{5,4},{6,7},{7,6},{8,9},{9,8},{10,11... | collective-permute-start | bytes 61448 | tf_op jit(solution)/shard_map/ppermute | solution.py:394
  6.8 3.7 %collective-permute-start = (bf16[32,128]{1,0:T(8,128)(2,1)S(1)}, bf16[32,128]{1,0:T(8,128)(2,1)S(1)}, u32[]{:S(2)}, u32[]{:S(2)}) collective-permute-start(bf16[32,128]{1,0:T(8,128)(2,1)S(1)} %get-tuple-element.22.x2_ref), channel_id=1, source_target_pairs={{0,1},{1,0},{2,3},{3,2},{4,8},{5,9},{6,10},{7,11},{8,4},{9,5},{10,... | collective-permute-start | bytes 24584 | tf_op jit(solution)/shard_map/ppermute | solution.py:394
  6.8 3.6 %collective-permute-start.3 = (bf16[32,128]{1,0:T(8,128)(2,1)S(1)}, bf16[32,128]{1,0:T(8,128)(2,1)S(1)}, u32[]{:S(2)}, u32[]{:S(2)}) collective-permute-start(bf16[32,128]{1,0:T(8,128)(2,1)S(1)} %get-tuple-element.23.x1_ref), channel_id=1, source_target_pairs={{0,4},{1,5},{2,6},{3,7},{4,0},{5,1},{6,2},{7,3},{8,12},{9,13},{10,... | collective-permute-start | bytes 24584 | tf_op jit(solution)/shard_map/ppermute | solution.py:394

commit v8 on v7

--- a/solution.py
+++ b/solution.py
@@ -156,96 +156,126 @@
     accumulation_copy.wait()
 
 
-def image_kernel(
-    basis_ref, mobility_ref, accumulation_ref, b_ref, along_x_ref, along_y_ref, along_z_ref, image_ref, field_ref
-):
+def gram_kernel(basis_ref, mobility_ref, accumulation_ref, b_ref, gram_ref, field_ref, left_ref):
     k_count, cz, cy, cx = basis_ref.shape
     mobility = mobility_ref[...].astype(F32)
+    accumulation = accumulation_ref[...]
     shape = mobility.shape
     along_x = jnp.where(iota(shape, 2) < cx - 1, harmonic(mobility, pltpu.roll(mobility, cx - 1, 2)), 0.0)
     along_y = jnp.where(iota(shape, 1) < cy - 1, harmonic(mobility, pltpu.roll(mobility, cy - 1, 1)), 0.0)
     along_z = VERTICAL_RATIO * harmonic(mobility[:-1], mobility[1:])
-    along_x_ref[...] = along_x
-    along_y_ref[...] = along_y
-    along_z_ref[...] = along_z
-    field = expand(basis_ref, b_ref[...])
-    field_ref[...] = field
-    flow_x = along_x * (field - pltpu.roll(field, cx - 1, 2))
-    image = accumulation_ref[...] * field + flow_x - pltpu.roll(flow_x, 1, 2)
-    flow_y = along_y * (field - pltpu.roll(field, cy - 1, 1))
-    image = image + flow_y - pltpu.roll(flow_y, 1, 1)
-    flow_z = along_z * (field[:-1] - field[1:])
-    nothing = jnp.zeros_like(field[:1])
-    image = image + jnp.concatenate([flow_z, nothing], axis=0) - jnp.concatenate([nothing, flow_z], axis=0)
-    row = iota((k_count, cx), 0)
-    partial = jnp.zeros((k_count, cx), F32)
+    rows = k_count * TILE
+    strips = [(z, y) for z in range(cz) for y in range(0, cy, TILE)]
     for k in range(k_count):
-        total = jnp.sum(jnp.sum(basis_ref[k].astype(F32) * image, axis=0), axis=0, keepdims=True)
-        partial = jnp.where(row == k, total, partial)
-    image_ref[...] = partial
-
-
-def energy(field, accumulation, along_x, along_y, along_z):
-    _, cy, cx = field.shape
-    change_x = field - pltpu.roll(field, cx - 1, 2)
-    change_y = field - pltpu.roll(field, cy - 1, 1)
-    change_z = field[:-1] - field[1:]
-    square = accumulation * field * field + along_x * change_x * change_x + along_y * change_y * change_y
-    square = jnp.sum(square, axis=0) + jnp.sum(along_z * change_z * change_z, axis=0)
-    return jnp.sum(square, axis=0, keepdims=True)
+        field = basis_ref[k].astype(F32)
+        flow_x = along_x * (field - pltpu.roll(field, cx - 1, 2))
+        image = accumulation * field + flow_x - pltpu.roll(flow_x, 1, 2)
+        flow_y = along_y * (field - pltpu.roll(field, cy - 1, 1))
+        image = image + flow_y - pltpu.roll(flow_y, 1, 1)
+        flow_z = along_z * (field[:-1] - field[1:])
+        nothing = jnp.zeros_like(field[:1])
+        image = image + jnp.concatenate([flow_z, nothing], axis=0) - jnp.concatenate([nothing, flow_z], axis=0)
+        high = image.astype(BF16)
+        low = (image - high.astype(F32)).astype(BF16)
+        for place, (z, y) in enumerate(strips):
+            lanes = slice(place * cx, (place + 1) * cx)
+            left_ref[k * TILE : (k + 1) * TILE, lanes] = high[z, y : y + TILE]
+            left_ref[rows + k * TILE : rows + (k + 1) * TILE, lanes] = low[z, y : y + TILE]
+    total = jnp.zeros((2 * rows, rows), F32)
+    for place, (z, y) in enumerate(strips):
+        right = basis_ref[:, z, y : y + TILE, :].reshape(rows, cx)
+        total = total + dot_nt(left_ref[:, place * cx : (place + 1) * cx], right)
+    total = total[:rows] + total[rows:]
+    same = lax.rem(iota((rows, rows), 0), TILE) == lax.rem(iota((rows, rows), 1), TILE)
+    total = jnp.where(same, total, 0.0)
+    gram_ref[...] = jnp.sum(total.reshape(k_count, TILE, rows), axis=1)
+    field_ref[...] = expand(basis_ref, b_ref[...])
+
+
+def unpack(ref, k_count, layers):
+    blocks = [ref[z * k_count : (z + 1) * k_count, :].astype(F32) for z in range(layers)]
+    start = layers * k_count
+    extra = ref[start : start + round_up(4 * layers, TILE), :].astype(F32)
+    mobility, high, middle, low = (extra[n * layers : (n + 1) * layers] for n in range(4))
+    return blocks, mobility, high + middle + low
+
+
+def as_row(column, width):
+    k_count = column.shape[0]
+    shape = (k_count, max(k_count * width, LANES))
+    place = iota(shape, 1) // width == iota(shape, 0)
+    return jnp.sum(jnp.where(place, column[:, :1], 0.0), axis=0, keepdims=True)
+
+
+def fold_lanes(x):
+    return sum(x[:, start : start + LANES] for start in range(0, x.shape[1], LANES))
+
+
+def rows_kernel(counts, y2_ref, y1_ref, ry2_ref, ry1_ref, b_ref, gram_ref, own_ref, pull_ref, edge_ref, cross_ref):
+    k_count = b_ref.shape[0]
+    cz = (y1_ref.shape[0] - TILE) // k_count
+    odd_y, _ = position("gy", counts[1])
+    own_image = fold_lanes(gram_ref[...] * as_row(b_ref[...], TILE))
+    weighted, plain, others = [], [], []
+    for n, (own_ref_, other_ref) in enumerate(((y1_ref, ry1_ref), (y2_ref, ry2_ref))):
+        own, own_mobility, own_field = unpack(own_ref_, k_count, cz)
+        other, other_mobility, other_field = unpack(other_ref, k_count, cz)
+        conductance = harmonic(own_mobility, other_mobility)
+        heavy = [block * conductance[z : z + 1] for z, block in enumerate(own)]
+        pull = jnp.zeros((k_count, LANES), F32)
+        for z, block in enumerate(heavy):
+            own_image = own_image + block * own_field[z : z + 1]
+            pull = pull + block * other_field[z : z + 1]
+        pull_ref[n * k_count : (n + 1) * k_count, :] = pull
+        weighted.append(jnp.concatenate(heavy, axis=1))
+        plain.append(jnp.concatenate(own, axis=1))
+        others.append(jnp.concatenate(other, axis=1))
+    own_ref[...] = own_image
+
+    def product(left, right):
+        right = jnp.concatenate([right, jnp.zeros((LANES - k_count, right.shape[1]), F32)], axis=0)
+        high = right.astype(BF16)
+        low = (right - high.astype(F32)).astype(BF16)
+        left = left.astype(BF16)
+        return dot_nt(left, high) + dot_nt(left, low)
+
+    edge_ref[...] = product(jnp.concatenate(plain, axis=1), jnp.concatenate(weighted, axis=1))
+    cross_ref[...] = product(jnp.where(odd_y, others[1], others[0]), jnp.where(odd_y, weighted[1], weighted[0]))
 
 
 def couple_kernel(
     counts,
-    y2_ref,
-    y1_ref,
     x2_ref,
     x1_ref,
     rx2_ref,
-    ry2_ref,
-    ry1_ref,
     rx1_ref,
     b_ref,
-    image_ref,
-    basis_ref,
-    accumulation_ref,
-    along_x_ref,
-    along_y_ref,
-    along_z_ref,
+    gram_ref,
+    own_ref,
+    pull_ref,
+    edge_ref,
+    cross_ref,
     out_ref,
     v_ref,
-    field_ref,
 ):
-    k_count, cz, _, _ = basis_ref.shape
+    k_count = b_ref.shape[0]
     odd_x, _ = position("gx", counts[0])
     odd_y, _ = position("gy", counts[1])
     b_col = b_ref[...]
-
-    def unpack(ref, layers):
-        blocks = [ref[z * k_count : (z + 1) * k_count, :].astype(F32) for z in range(layers)]
-        start = layers * k_count
-        extra = ref[start : start + round_up(4 * layers, TILE), :].astype(F32)
-        mobility, high, middle, low = (extra[n * layers : (n + 1) * layers] for n in range(4))
-        return blocks, mobility, high + middle + low
-
+    pulls = [pull_ref[0:k_count, :], pull_ref[k_count : 2 * k_count, :]]
     faces = []
-    for own_ref, other_ref, layers in (
-        (x1_ref, rx1_ref, 1),
-        (x2_ref, rx2_ref, 1),
-        (y1_ref, ry1_ref, cz),
-        (y2_ref, ry2_ref, cz),
-    ):
-        own, own_mobility, own_field = unpack(own_ref, layers)
-        other, other_mobility, other_field = unpack(other_ref, layers)
-        faces.append((own, other, harmonic(own_mobility, other_mobility), own_field, other_field))
-
-    own_image = image_ref[...]
-    along = own_image
-    for own, _, conductance, own_field, other_field in faces:
-        flow = conductance * (own_field - other_field)
-        for z, block in enumerate(own):
-            along = along + block * flow[z : z + 1]
-    image = jnp.sum(along, axis=1, keepdims=True)
+    own_image = own_ref[...]
+    along = -pulls[0] - pulls[1]
+    for own_ref_, other_ref in ((x1_ref, rx1_ref), (x2_ref, rx2_ref)):
+        (own,), own_mobility, own_field = unpack(own_ref_, k_count, 1)
+        (other,), other_mobility, other_field = unpack(other_ref, k_count, 1)
+        conductance = harmonic(own_mobility, other_mobility)
+        own_image = own_image + own * (conductance * own_field)
+        pull = own * (conductance * other_field)
+        along = along - pull
+        pulls.append(pull)
+        faces.append((own, other, conductance))
+    image = jnp.sum(along + own_image, axis=1, keepdims=True)
     source_square = jnp.sum(b_col * b_col, axis=0, keepdims=True)
     source_image = jnp.sum(b_col * image, axis=0, keepdims=True)
     quotient = source_image / jnp.maximum(source_square, TINY)
@@ -253,42 +283,29 @@
     v_ref[0:k_count, :] = v_col
     v_ref[k_count : k_count + 8, :] = jnp.broadcast_to(quotient, (8, LANES))
 
-    field = expand(basis_ref, v_col)
-    field_ref[...] = field
+    v_row = as_row(v_col, 1)
+    v_image = fold_lanes(gram_ref[...] * as_row(v_col, TILE)) + edge_ref[...] * v_row
     squares = [
         jnp.sum(b_col * own_image, axis=0, keepdims=True),
         jnp.sum(v_col * own_image, axis=0, keepdims=True),
-        energy(field, accumulation_ref[...], along_x_ref[...], along_y_ref[...], along_z_ref[...]),
+        jnp.sum(v_col * v_image, axis=0, keepdims=True),
     ]
-    toward = []
-    for own, other, conductance, own_field, other_field in faces:
-        v_field = jnp.concatenate([jnp.sum(block * v_col, axis=0, keepdims=True) for block in own], axis=0)
-        flow_b = conductance * own_field
-        flow_v = conductance * v_field
-        for n, value in enumerate((flow_b * own_field, flow_b * v_field, flow_v * v_field)):
-            squares[n] = squares[n] + jnp.sum(value, axis=0, keepdims=True)
-        toward.append(
-            (
-                other,
-                flow_v,
-                jnp.sum(-flow_b * other_field, axis=0, keepdims=True),
-                jnp.sum(-flow_v * other_field, axis=0, keepdims=True),
-            )
-        )
-
+    flows = []
+    for own, _, conductance in faces:
+        v_field = jnp.sum(own * v_col, axis=0, keepdims=True)
+        flows.append(conductance * v_field)
+        squares[2] = squares[2] + flows[-1] * v_field
+    beside = -jnp.where(odd_x, faces[1][1], faces[0][1]) * jnp.where(odd_x, flows[1], flows[0])
     columns = [v_col]
+    for product in (beside, -cross_ref[...] * v_row):
+        columns.append(jnp.sum(product, axis=1, keepdims=True))
     source_pairs = []
     image_pairs = []
-    for first, second, odd in ((toward[0], toward[1], odd_x), (toward[2], toward[3], odd_y)):
-        product = jnp.zeros((k_count, LANES), F32)
-        for z in range(len(first[0])):
-            block = jnp.where(odd, second[0][z], first[0][z])
-            flow = jnp.where(odd, second[1], first[1])
-            product = product - block * flow[z : z + 1]
-        columns.append(jnp.sum(product, axis=1, keepdims=True))
-        source_pairs.append(jnp.where(odd, second[2], first[2]))
-        image_pairs.append(jnp.where(odd, second[3], first[3]))
-        image_pairs.append(jnp.where(odd, first[3], second[3]))
+    for first, second, odd in ((pulls[2], pulls[3], odd_x), (pulls[0], pulls[1], odd_y)):
+        right, left = jnp.where(odd, second, first), jnp.where(odd, first, second)
+        source_pairs.append(-jnp.sum(b_col * right, axis=0, keepdims=True))
+        image_pairs.append(-jnp.sum(v_col * right, axis=0, keepdims=True))
+        image_pairs.append(-jnp.sum(v_col * left, axis=0, keepdims=True))
     row = iota((TILE, LANES), 0)
     sums = jnp.zeros((TILE, LANES), F32)
     for n, value in enumerate((*squares, *source_pairs, *image_pairs)):
@@ -312,7 +329,7 @@
     b_ref,
     v_ref,
     b_field_ref,
-    v_field_ref,
+    basis_ref,
     correction_hbm,
     solution_hbm,
     correction_ref,
@@ -323,6 +340,7 @@
     cz = correction_ref.shape[0]
     base = 3 * k_count
     every = gathered_ref[...]
+    v_field = expand(basis_ref, v_ref[0:k_count, :])
 
     def rows(x, amount):
         amount = amount % x.shape[0]
@@ -369,7 +387,7 @@
     copies = [pltpu.make_async_copy(solution_ref, solution_hbm, sems.at[cz])]
     copies[0].start()
     for z in range(cz):
-        correction_ref[z] = b_part * b_field_ref[z] + v_part * v_field_ref[z]
+        correction_ref[z] = b_part * b_field_ref[z] + v_part * v_field[z]
         copy = pltpu.make_async_copy(correction_ref.at[z], correction_hbm.at[z], sems.at[z])
         copy.start()
         copies.append(copy)
@@ -425,26 +443,34 @@
     ry1 = exchange(y1, "gy", counts, False)
     ry2 = exchange(y2, "gy", counts, True)
     conductance = jax.ShapeDtypeStruct((cz, cy, cx), F32)
-    layered = jax.ShapeDtypeStruct((cz - 1, cy, cx), F32)
-    along_x, along_y, along_z, image, b_field = pl.pallas_call(
-        image_kernel,
-        out_shape=(conductance, conductance, layered, jax.ShapeDtypeStruct((k_count, cx), F32), conductance),
+    gram, b_field = pl.pallas_call(
+        gram_kernel,
+        out_shape=(jax.ShapeDtypeStruct((k_count, k_count * TILE), F32), conductance),
         in_specs=[VMEM] * 4,
-        out_specs=(VMEM,) * 5,
+        out_specs=(VMEM,) * 2,
         compiler_params=PARAMS,
+        scratch_shapes=[pltpu.VMEM((2 * k_count * TILE, cz * cy // TILE * cx), BF16)],
         cost_estimate=pl.CostEstimate(flops=10**8, bytes_accessed=10**6, transcendentals=0),
     )(basis, mobility, accumulation, b)
-    row, v, v_field = pl.pallas_call(
+    square = jax.ShapeDtypeStruct((k_count, LANES), F32)
+    own, pull, edge, cross = pl.pallas_call(
+        functools.partial(rows_kernel, counts),
+        out_shape=(square, jax.ShapeDtypeStruct((2 * k_count, LANES), F32), square, square),
+        in_specs=[VMEM] * 6,
+        out_specs=(VMEM,) * 4,
+        compiler_params=PARAMS,
+        cost_estimate=pl.CostEstimate(flops=10**7, bytes_accessed=10**6, transcendentals=0),
+    )(y2, y1, ry2, ry1, b, gram)
+    row, v = pl.pallas_call(
         functools.partial(couple_kernel, counts),
         out_shape=(
             jax.ShapeDtypeStruct((devices, LANES), F32),
             jax.ShapeDtypeStruct((k_count + 8, LANES), F32),
-            conductance,
         ),
-        in_specs=[VMEM] * 15,
-        out_specs=(VMEM,) * 3,
+        in_specs=[VMEM] * 10,
+        out_specs=(VMEM,) * 2,
         compiler_params=PARAMS,
-    )(y2, y1, x2, x1, rx2, ry2, ry1, rx1, b, image, basis, accumulation, along_x, along_y, along_z)
+    )(x2, x1, rx2, rx1, b, gram, own, pull, edge, cross)
     gathered = lax.all_to_all(row, ("gx", "gy"), 0, 0, tiled=True)
     correction, solution = pl.pallas_call(
         functools.partial(finish_kernel, counts[1]),
@@ -457,7 +483,7 @@
             pltpu.SemaphoreType.DMA((cz + 1,)),
         ],
         compiler_params=PARAMS,
-    )(gathered, b, v, b_field, v_field)
+    )(gathered, b, v, b_field, basis)
     return correction, solution.reshape(1, 1, k_count)
 
 

time: 21.9 us -> 21.9 us (level)
  waiting for transfers between devices: 1.69 us -> 0.26 us
  Pallas kernels: 3.12 us -> 4.41 us
    ppermute x4, waiting for transfers between devices: 1.69 us -> 0.26 us  [exchange(): return lax.ppermute(message, ('gx', 'gy'), pairs)]
    pallas_call x1 -> x2, Pallas kernels: 0.36 us -> 1.76 us  [the longest x1 1.51 us: per_device(): pl.pallas_call(gram_kernel, out_shape=(jax.ShapeDtypeStruct((k_count, k_c...]
  transfers between devices with their start and end apart: 4 -> 4, of which waited for: 1 -> 1; matrix products, arithmetic and copies ran while one was open for 0% -> 0% of each run, Pallas kernels for 2% -> 8%
where the time goes in v8:
time: 21.9 us; the launch traced here: 21.8 us
  blocking collectives  10.1 us (46%)
  starting transfers between devices  6.27 us (29%)
  Pallas kernels  4.41 us (20%)
  between operations  0.67 us (3%)
  waiting for transfers between devices  0.26 us (1%)
    all_to_all x1, blocking collectives, per_device(): gathered = lax.all_to_all(row, ('gx', 'gy'), 0, 0, tiled=True)  10.1 us
    ppermute x4, starting transfers between devices, exchange(): return lax.ppermute(message, ('gx', 'gy'), pairs)  6.27 us
    pallas_call x1, Pallas kernels, per_device(): pl.pallas_call(gram_kernel, out_shape=(jax.ShapeDtypeStruct((k_count, k_c...  1.51 us
    pallas_call x1, Pallas kernels, per_device(): pl.pallas_call(functools.partial(edges_kernel, counts), out_shape=(x_mess...  1.47 us
    pallas_call x1, Pallas kernels, per_device(): pl.pallas_call(functools.partial(finish_kernel, counts[1]), out_shape=(ja...  0.89 us
  transfers between devices with their start and end apart: 4, of which 1 were waited for; matrix products, arithmetic and copies ran while one was open for 0% of the time, Pallas kernels for 8%

profile of v8, /device:TPU:0, one launch (start us, length us, event | category | flops | bytes accessed | tf_op | source)
XLA Modules:
  0.0 21.8 jit_solution(12765486765698298356)
XLA Ops:
  0.6 1.5 %shard_map.59 = (bf16[32,128]{1,0:T(8,128)(2,1)S(1)}, bf16[32,128]{1,0:T(8,128)(2,1)S(1)}, bf16[80,128]{1,0:T(8,128)(2,1)S(1)}, bf16[80,128]{1,0:T(8,128)(2,1)S(...) custom-call(bf16[16,4,32,128]{3,2,1,0:T(8,128)(2,1)} %basis_hbm.1, ...), custom_call_target="tpu_custom_call" | custom-call | tf_op jit(solution)/shard_map/pallas_call | solution.py:421
  2.1 0.5 %collective-permute-start.2 = (bf16[80,128]{1,0:T(8,128)(2,1)S(1)}, bf16[80,128]{1,0:T(8,128)(2,1)S(1)}, u32[]{:S(2)}, u32[]{:S(2)}) collective-permute-start(bf16[80,128]{1,0:T(8,128)(2,1)S(1)} %get-tuple-element.27.y2_ref), channel_id=1, source_target_pairs={{0,4},{1,2},{2,1},{3,7},{4,0},{5,6},{6,5},{7,3},{8,12},{9,10},{10,... | collective-permute-start | bytes 61448 | tf_op jit(solution)/shard_map/ppermute | solution.py:412
  2.6 4.1 %collective-permute-start.3 = (bf16[80,128]{1,0:T(8,128)(2,1)S(1)}, bf16[80,128]{1,0:T(8,128)(2,1)S(1)}, u32[]{:S(2)}, u32[]{:S(2)}) collective-permute-start(bf16[80,128]{1,0:T(8,128)(2,1)S(1)} %get-tuple-element.28.y1_ref), channel_id=1, source_target_pairs={{0,1},{1,0},{2,3},{3,2},{4,5},{5,4},{6,7},{7,6},{8,9},{9,8},{10,11... | collective-permute-start | bytes 61448 | tf_op jit(solution)/shard_map/ppermute | solution.py:412
  6.8 0.0 collective-permute-start
  6.8 1.6 %collective-permute-start.1 = (bf16[32,128]{1,0:T(8,128)(2,1)S(1)}, bf16[32,128]{1,0:T(8,128)(2,1)S(1)}, u32[]{:S(2)}, u32[]{:S(2)}) collective-permute-start(bf16[32,128]{1,0:T(8,128)(2,1)S(1)} %get-tuple-element.21.x1_ref), channel_id=1, source_target_pairs={{0,4},{1,5},{2,6},{3,7},{4,0},{5,1},{6,2},{7,3},{8,12},{9,13},{10,... | collective-permute-start | bytes 24584 | tf_op jit(solution)/shard_map/ppermute | solution.py:412
  8.4 1.5 %shard_map.60 = (f32[16,256]{1,0:T(8,128)S(1)}, f32[4,32,128]{2,1,0:T(8,128)S(1)}) custom-call(bf16[16,4,32,128]{3,2,1,0:T(8,128)(2,1)S(1)} %get-tuple-element.23.basis_ref, bf16[4,32,128]{2,1,0:T(8,128)(2,1)S(1)} %get-tuple-element.24.mobility_ref, f32[4,32,128]{2,1,0:T(8,128)S(1)} %get-tuple-element.25.accumulation_ref, f32[16,128]{1,0:T(8,128)S(1)} %get-tuple-element.22.b_ref), custom_call_target="tpu_custom_call" | custom-call | flops 100000000 | bytes 1000000 | tf_op jit(solution)/shard_map/pallas_call | solution.py:446
  9.9 0.0 collective-permute-done.2.ry2_ref
  9.9 0.0 collective-permute-done.3.ry1_ref
  9.9 0.3 %shard_map.61 = (f32[16,128]{1,0:T(8,128)S(1)}, f32[32,128]{1,0:T(8,128)S(1)}, f32[16,128]{1,0:T(8,128)S(1)}, f32[16,128]{1,0:T(8,128)S(1)}) custom-call(bf16[80,128]{1,0:T(8,128)(2,1)S(1)} %get-tuple-element.27.y2_ref, bf16[80,128]{1,0:T(8,128)(2,1)S(1)} %get-tuple-element.28.y1_ref, bf16[80,128]{1,0:T(8,128)(2,1)S(1)} %collective-permute-done.2.ry2_ref, ...), custom_call_target="tpu_custom_call" | custom-call | flops 10000000 | bytes 1000000 | tf_op jit(solution)/shard_map/pallas_call | solution.py:456
  10.2 0.3 %collective-permute-done.rx2_ref = bf16[32,128]{1,0:T(8,128)(2,1)S(1)} collective-permute-done((bf16[32,128]{1,0:T(8,128)(2,1)S(1)}, bf16[32,128]{1,0:T(8,128)(2,1)S(1)}, u32[]{:S(2)}, u32[]{:S(2)}) %collective-permute-start) | collective-permute-done | bytes 8224 | tf_op jit(solution)/shard_map/ppermute | solution.py:412
  10.4 0.0 collective-permute-done.1.rx1_ref
  10.4 0.3 %shard_map.62 = (f32[32,128]{1,0:T(8,128)S(1)}, f32[24,128]{1,0:T(8,128)S(1)}) custom-call(bf16[32,128]{1,0:T(8,128)(2,1)S(1)} %get-tuple-element.20.x2_ref, bf16[32,128]{1,0:T(8,128)(2,1)S(1)} %get-tuple-element.21.x1_ref, bf16[32,128]{1,0:T(8,128)(2,1)S(1)} %collective-permute-done.rx2_ref, bf16[32,128]{1,0:T(8,128)(2,1)S(1)} %collective-permute-done.1.rx1_ref, ...), custom_call_target="tpu_custom_call" | custom-call | tf_op jit(solution)/shard_map/pallas_call | solution.py:464
  10.7 10.1 %all_to_all.11 = f32[32,1,128]{2,1,0:T(1,128)S(1)} all-to-all(f32[32,1,128]{2,1,0:T(1,128)S(1)} %bitcast.6), channel_id=1, replica_groups=mesh['gx'=8,'gy'=4] {'gx','gy'}, dimensions={0} | all-to-all | bytes 32768 | tf_op jit(solution)/shard_map/all_to_all | solution.py:474
  20.9 0.9 %shard_map.63 = (f32[4,32,128]{2,1,0:T(8,128)}, f32[1,16]{1,0:T(1,128)}) custom-call(f32[32,128]{1,0:T(8,128)S(1)} %bitcast.5, f32[16,128]{1,0:T(8,128)S(1)} %get-tuple-element.22.b_ref, f32[24,128]{1,0:T(8,128)S(1)} %get-tuple-element.34.v_ref, f32[4,32,128]{2,1,0:T(8,128)S(1)} %get-tuple-element.35.b_field_ref, ...), custom_call_target="tpu_custom_call" | custom-call | tf_op jit(solution)/shard_map/pallas_call | solution.py:475
Async XLA Ops:
  2.1 7.8 %collective-permute-start.2 = (bf16[80,128]{1,0:T(8,128)(2,1)S(1)}, bf16[80,128]{1,0:T(8,128)(2,1)S(1)}, u32[]{:S(2)}, u32[]{:S(2)}) collective-permute-start(bf16[80,128]{1,0:T(8,128)(2,1)S(1)} %get-tuple-element.27.y2_ref), channel_id=1, source_target_pairs={{0,4},{1,2},{2,1},{3,7},{4,0},{5,6},{6,5},{7,3},{8,12},{9,10},{10,... | collective-permute-start | bytes 61448 | tf_op jit(solution)/shard_map/ppermute | solution.py:412
  2.6 7.3 %collective-permute-start.3 = (bf16[80,128]{1,0:T(8,128)(2,1)S(1)}, bf16[80,128]{1,0:T(8,128)(2,1)S(1)}, u32[]{:S(2)}, u32[]{:S(2)}) collective-permute-start(bf16[80,128]{1,0:T(8,128)(2,1)S(1)} %get-tuple-element.28.y1_ref), channel_id=1, source_target_pairs={{0,1},{1,0},{2,3},{3,2},{4,5},{5,4},{6,7},{7,6},{8,9},{9,8},{10,11... | collective-permute-start | bytes 61448 | tf_op jit(solution)/shard_map/ppermute | solution.py:412
  6.8 3.7 %collective-permute-start = (bf16[32,128]{1,0:T(8,128)(2,1)S(1)}, bf16[32,128]{1,0:T(8,128)(2,1)S(1)}, u32[]{:S(2)}, u32[]{:S(2)}) collective-permute-start(bf16[32,128]{1,0:T(8,128)(2,1)S(1)} %get-tuple-element.20.x2_ref), channel_id=1, source_target_pairs={{0,1},{1,0},{2,3},{3,2},{4,8},{5,9},{6,10},{7,11},{8,4},{9,5},{10,... | collective-permute-start | bytes 24584 | tf_op jit(solution)/shard_map/ppermute | solution.py:412
  6.8 3.6 %collective-permute-start.1 = (bf16[32,128]{1,0:T(8,128)(2,1)S(1)}, bf16[32,128]{1,0:T(8,128)(2,1)S(1)}, u32[]{:S(2)}, u32[]{:S(2)}) collective-permute-start(bf16[32,128]{1,0:T(8,128)(2,1)S(1)} %get-tuple-element.21.x1_ref), channel_id=1, source_target_pairs={{0,4},{1,5},{2,6},{3,7},{4,0},{5,1},{6,2},{7,3},{8,12},{9,13},{10,... | collective-permute-start | bytes 24584 | tf_op jit(solution)/shard_map/ppermute | solution.py:412

commit v9 on v7

--- a/solution.py
+++ b/solution.py
@@ -90,11 +90,6 @@
 
     first = jnp.where(odd_x, 0, cx - 1)
     second = jnp.where(odd_x, cx - 1, 0)
-    pick_row = iota((2 * k_count, cx), 0)
-    pick_lane = iota((2 * k_count, cx), 1)
-    wanted = pick_lane == jnp.where(pick_row < k_count, first, second)
-    pick_k = jnp.where(pick_row < k_count, pick_row, pick_row - k_count)
-    picks = [jnp.where(jnp.logical_and(wanted, pick_k == k), 1.0, 0.0).astype(BF16) for k in range(k_count)]
     pick_row = iota((TILE, cx), 0)
     pick_lane = iota((TILE, cx), 1)
     pick = jnp.where(pick_lane == jnp.where(pick_row == 0, first, second), 1.0, 0.0).astype(BF16)
@@ -106,9 +101,12 @@
     row = iota((k_count, cx), 0)
     partial = jnp.zeros((k_count, cx), F32)
     basis_copy.wait()
-    columns = dot_nt(
-        jnp.concatenate(picks, axis=1), jnp.concatenate([basis_ref[k].reshape(cells, cx) for k in range(k_count)], axis=1)
-    )
+    flat = dot_nt(pick, basis_ref[...].reshape(k_count * cells, cx))
+    columns = [jnp.zeros((k_count, cells), F32) for _ in range(2)]
+    for k in range(k_count):
+        for number in range(2):
+            value = flat[number : number + 1, k * cells : (k + 1) * cells]
+            columns[number] = jnp.where(row == k, value, columns[number])
     for k in range(k_count):
         product = basis_ref[k].astype(F32) * residual
         total = jnp.sum(jnp.sum(product, axis=0), axis=0, keepdims=True)
@@ -117,7 +115,7 @@
     b_ref[...] = b
 
     for number, ref in ((0, x1_ref), (1, x2_ref)):
-        edge = columns[number * k_count : (number + 1) * k_count]
+        edge = columns[number]
         ref[0:k_count, :] = edge.astype(BF16)
         field = jnp.sum(edge * b[:, :1], axis=0, keepdims=True)
         mobility = edge_mobility[number : number + 1]
@@ -156,43 +154,40 @@
     accumulation_copy.wait()
 
 
-def image_kernel(
-    basis_ref, mobility_ref, accumulation_ref, b_ref, along_x_ref, along_y_ref, along_z_ref, image_ref, field_ref
-):
+def gram_kernel(basis_ref, mobility_ref, accumulation_ref, b_ref, gram_ref, field_ref, left_ref):
     k_count, cz, cy, cx = basis_ref.shape
     mobility = mobility_ref[...].astype(F32)
+    accumulation = accumulation_ref[...]
     shape = mobility.shape
     along_x = jnp.where(iota(shape, 2) < cx - 1, harmonic(mobility, pltpu.roll(mobility, cx - 1, 2)), 0.0)
     along_y = jnp.where(iota(shape, 1) < cy - 1, harmonic(mobility, pltpu.roll(mobility, cy - 1, 1)), 0.0)
     along_z = VERTICAL_RATIO * harmonic(mobility[:-1], mobility[1:])
-    along_x_ref[...] = along_x
-    along_y_ref[...] = along_y
-    along_z_ref[...] = along_z
-    field = expand(basis_ref, b_ref[...])
-    field_ref[...] = field
-    flow_x = along_x * (field - pltpu.roll(field, cx - 1, 2))
-    image = accumulation_ref[...] * field + flow_x - pltpu.roll(flow_x, 1, 2)
-    flow_y = along_y * (field - pltpu.roll(field, cy - 1, 1))
-    image = image + flow_y - pltpu.roll(flow_y, 1, 1)
-    flow_z = along_z * (field[:-1] - field[1:])
-    nothing = jnp.zeros_like(field[:1])
-    image = image + jnp.concatenate([flow_z, nothing], axis=0) - jnp.concatenate([nothing, flow_z], axis=0)
-    row = iota((k_count, cx), 0)
-    partial = jnp.zeros((k_count, cx), F32)
+    rows = k_count * TILE
+    strips = [(z, y) for z in range(cz) for y in range(0, cy, TILE)]
     for k in range(k_count):
-        total = jnp.sum(jnp.sum(basis_ref[k].astype(F32) * image, axis=0), axis=0, keepdims=True)
-        partial = jnp.where(row == k, total, partial)
-    image_ref[...] = partial
-
-
-def energy(field, accumulation, along_x, along_y, along_z):
-    _, cy, cx = field.shape
-    change_x = field - pltpu.roll(field, cx - 1, 2)
-    change_y = field - pltpu.roll(field, cy - 1, 1)
-    change_z = field[:-1] - field[1:]
-    square = accumulation * field * field + along_x * change_x * change_x + along_y * change_y * change_y
-    square = jnp.sum(square, axis=0) + jnp.sum(along_z * change_z * change_z, axis=0)
-    return jnp.sum(square, axis=0, keepdims=True)
+        field = basis_ref[k].astype(F32)
+        flow_x = along_x * (field - pltpu.roll(field, cx - 1, 2))
+        image = accumulation * field + flow_x - pltpu.roll(flow_x, 1, 2)
+        flow_y = along_y * (field - pltpu.roll(field, cy - 1, 1))
+        image = image + flow_y - pltpu.roll(flow_y, 1, 1)
+        flow_z = along_z * (field[:-1] - field[1:])
+        nothing = jnp.zeros_like(field[:1])
+        image = image + jnp.concatenate([flow_z, nothing], axis=0) - jnp.concatenate([nothing, flow_z], axis=0)
+        high = image.astype(BF16)
+        low = (image - high.astype(F32)).astype(BF16)
+        for place, (z, y) in enumerate(strips):
+            lanes = slice(place * cx, (place + 1) * cx)
+            left_ref[k * TILE : (k + 1) * TILE, lanes] = high[z, y : y + TILE]
+            left_ref[rows + k * TILE : rows + (k + 1) * TILE, lanes] = low[z, y : y + TILE]
+    total = jnp.zeros((2 * rows, rows), F32)
+    for place, (z, y) in enumerate(strips):
+        right = basis_ref[:, z, y : y + TILE, :].reshape(rows, cx)
+        total = total + dot_nt(left_ref[:, place * cx : (place + 1) * cx], right)
+    total = total[:rows] + total[rows:]
+    same = lax.rem(iota((rows, rows), 0), TILE) == lax.rem(iota((rows, rows), 1), TILE)
+    total = jnp.where(same, total, 0.0)
+    gram_ref[...] = jnp.sum(total.reshape(k_count, TILE, rows), axis=1)
+    field_ref[...] = expand(basis_ref, b_ref[...])
 
 
 def couple_kernel(
@@ -206,17 +201,12 @@
     ry1_ref,
     rx1_ref,
     b_ref,
-    image_ref,
-    basis_ref,
-    accumulation_ref,
-    along_x_ref,
-    along_y_ref,
-    along_z_ref,
+    gram_ref,
     out_ref,
     v_ref,
-    field_ref,
 ):
-    k_count, cz, _, _ = basis_ref.shape
+    k_count = b_ref.shape[0]
+    cz = (y1_ref.shape[0] - TILE) // k_count
     odd_x, _ = position("gx", counts[0])
     odd_y, _ = position("gy", counts[1])
     b_col = b_ref[...]
@@ -239,7 +229,17 @@
         other, other_mobility, other_field = unpack(other_ref, layers)
         faces.append((own, other, harmonic(own_mobility, other_mobility), own_field, other_field))
 
-    own_image = image_ref[...]
+    gram = gram_ref[...]
+    wide = gram.shape[1]
+    spread = iota((k_count, wide), 1) // TILE == iota((k_count, wide), 0)
+
+    def as_row(column):
+        return jnp.sum(jnp.where(spread, column[:, :1], 0.0), axis=0, keepdims=True)
+
+    def fold(x):
+        return sum(x[:, start : start + LANES] for start in range(0, wide, LANES))
+
+    own_image = fold(gram * as_row(b_col))
     along = own_image
     for own, _, conductance, own_field, other_field in faces:
         flow = conductance * (own_field - other_field)
@@ -253,12 +253,10 @@
     v_ref[0:k_count, :] = v_col
     v_ref[k_count : k_count + 8, :] = jnp.broadcast_to(quotient, (8, LANES))
 
-    field = expand(basis_ref, v_col)
-    field_ref[...] = field
     squares = [
         jnp.sum(b_col * own_image, axis=0, keepdims=True),
         jnp.sum(v_col * own_image, axis=0, keepdims=True),
-        energy(field, accumulation_ref[...], along_x_ref[...], along_y_ref[...], along_z_ref[...]),
+        jnp.sum(v_col * fold(gram * as_row(v_col)), axis=0, keepdims=True),
     ]
     toward = []
     for own, other, conductance, own_field, other_field in faces:
@@ -312,7 +310,7 @@
     b_ref,
     v_ref,
     b_field_ref,
-    v_field_ref,
+    basis_ref,
     correction_hbm,
     solution_hbm,
     correction_ref,
@@ -323,6 +321,7 @@
     cz = correction_ref.shape[0]
     base = 3 * k_count
     every = gathered_ref[...]
+    v_field = expand(basis_ref, v_ref[0:k_count, :])
 
     def rows(x, amount):
         amount = amount % x.shape[0]
@@ -369,7 +368,7 @@
     copies = [pltpu.make_async_copy(solution_ref, solution_hbm, sems.at[cz])]
     copies[0].start()
     for z in range(cz):
-        correction_ref[z] = b_part * b_field_ref[z] + v_part * v_field_ref[z]
+        correction_ref[z] = b_part * b_field_ref[z] + v_part * v_field[z]
         copy = pltpu.make_async_copy(correction_ref.at[z], correction_hbm.at[z], sems.at[z])
         copy.start()
         copies.append(copy)
@@ -425,26 +424,25 @@
     ry1 = exchange(y1, "gy", counts, False)
     ry2 = exchange(y2, "gy", counts, True)
     conductance = jax.ShapeDtypeStruct((cz, cy, cx), F32)
-    layered = jax.ShapeDtypeStruct((cz - 1, cy, cx), F32)
-    along_x, along_y, along_z, image, b_field = pl.pallas_call(
-        image_kernel,
-        out_shape=(conductance, conductance, layered, jax.ShapeDtypeStruct((k_count, cx), F32), conductance),
+    gram, b_field = pl.pallas_call(
+        gram_kernel,
+        out_shape=(jax.ShapeDtypeStruct((k_count, k_count * TILE), F32), conductance),
         in_specs=[VMEM] * 4,
-        out_specs=(VMEM,) * 5,
+        out_specs=(VMEM,) * 2,
         compiler_params=PARAMS,
+        scratch_shapes=[pltpu.VMEM((2 * k_count * TILE, cz * cy // TILE * cx), BF16)],
         cost_estimate=pl.CostEstimate(flops=10**8, bytes_accessed=10**6, transcendentals=0),
     )(basis, mobility, accumulation, b)
-    row, v, v_field = pl.pallas_call(
+    row, v = pl.pallas_call(
         functools.partial(couple_kernel, counts),
         out_shape=(
             jax.ShapeDtypeStruct((devices, LANES), F32),
             jax.ShapeDtypeStruct((k_count + 8, LANES), F32),
-            conductance,
         ),
-        in_specs=[VMEM] * 15,
-        out_specs=(VMEM,) * 3,
+        in_specs=[VMEM] * 10,
+        out_specs=(VMEM,) * 2,
         compiler_params=PARAMS,
-    )(y2, y1, x2, x1, rx2, ry2, ry1, rx1, b, image, basis, accumulation, along_x, along_y, along_z)
+    )(y2, y1, x2, x1, rx2, ry2, ry1, rx1, b, gram)
     gathered = lax.all_to_all(row, ("gx", "gy"), 0, 0, tiled=True)
     correction, solution = pl.pallas_call(
         functools.partial(finish_kernel, counts[1]),
@@ -457,7 +455,7 @@
             pltpu.SemaphoreType.DMA((cz + 1,)),
         ],
         compiler_params=PARAMS,
-    )(gathered, b, v, b_field, v_field)
+    )(gathered, b, v, b_field, basis)
     return correction, solution.reshape(1, 1, k_count)
 
 

time: 21.9 us -> 21.8 us (level)
  waiting for transfers between devices: 1.69 us -> 0.53 us
  Pallas kernels: 3.12 us -> 4.19 us
    ppermute x4, waiting for transfers between devices: 1.69 us -> 0.53 us  [exchange(): return lax.ppermute(message, ('gx', 'gy'), pairs)]
    pallas_call x1, Pallas kernels: 0.36 us -> 1.51 us  [per_device(): pl.pallas_call(gram_kernel, out_shape=(jax.ShapeDtypeStruct((k_count, k_c...]
  transfers between devices with their start and end apart: 4 -> 4, of which waited for: 1 -> 1; matrix products, arithmetic and copies ran while one was open for 0% -> 0% of each run, Pallas kernels for 2% -> 7%
where the time goes in v9:
time: 21.8 us; the launch traced here: 21.6 us
  blocking collectives  9.99 us (46%)
  starting transfers between devices  6.27 us (29%)
  Pallas kernels  4.19 us (19%)
  between operations  0.65 us (3%)
  waiting for transfers between devices  0.53 us (2%)
    all_to_all x1, blocking collectives, per_device(): gathered = lax.all_to_all(row, ('gx', 'gy'), 0, 0, tiled=True)  9.99 us
    ppermute x4, starting transfers between devices, exchange(): return lax.ppermute(message, ('gx', 'gy'), pairs)  6.27 us
    pallas_call x1, Pallas kernels, per_device(): pl.pallas_call(gram_kernel, out_shape=(jax.ShapeDtypeStruct((k_count, k_c...  1.51 us
    pallas_call x1, Pallas kernels, per_device(): pl.pallas_call(functools.partial(edges_kernel, counts), out_shape=(x_mess...  1.43 us
    pallas_call x1, Pallas kernels, per_device(): pl.pallas_call(functools.partial(finish_kernel, counts[1]), out_shape=(ja...  0.89 us
    ppermute x4, waiting for transfers between devices, exchange(): return lax.ppermute(message, ('gx', 'gy'), pairs)  0.53 us
  transfers between devices with their start and end apart: 4, of which 1 were waited for; matrix products, arithmetic and copies ran while one was open for 0% of the time, Pallas kernels for 7%

profile of v9, /device:TPU:0, one launch (start us, length us, event | category | flops | bytes accessed | tf_op | source)
XLA Modules:
  0.0 21.6 jit_solution(4603264898242731962)
XLA Ops:
  0.6 1.4 %shard_map.59 = (bf16[32,128]{1,0:T(8,128)(2,1)S(1)}, bf16[32,128]{1,0:T(8,128)(2,1)S(1)}, bf16[80,128]{1,0:T(8,128)(2,1)S(1)}, bf16[80,128]{1,0:T(8,128)(2,1)S(...) custom-call(bf16[16,4,32,128]{3,2,1,0:T(8,128)(2,1)} %basis_hbm.1, ...), custom_call_target="tpu_custom_call" | custom-call | tf_op jit(solution)/shard_map/pallas_call | solution.py:402
  2.1 0.5 %collective-permute-start.1 = (bf16[80,128]{1,0:T(8,128)(2,1)S(1)}, bf16[80,128]{1,0:T(8,128)(2,1)S(1)}, u32[]{:S(2)}, u32[]{:S(2)}) collective-permute-start(bf16[80,128]{1,0:T(8,128)(2,1)S(1)} %get-tuple-element.16.y2_ref), channel_id=1, source_target_pairs={{0,4},{1,2},{2,1},{3,7},{4,0},{5,6},{6,5},{7,3},{8,12},{9,10},{10,... | collective-permute-start | bytes 61448 | tf_op jit(solution)/shard_map/ppermute | solution.py:393
  2.6 4.1 %collective-permute-start.2 = (bf16[80,128]{1,0:T(8,128)(2,1)S(1)}, bf16[80,128]{1,0:T(8,128)(2,1)S(1)}, u32[]{:S(2)}, u32[]{:S(2)}) collective-permute-start(bf16[80,128]{1,0:T(8,128)(2,1)S(1)} %get-tuple-element.17.y1_ref), channel_id=1, source_target_pairs={{0,1},{1,0},{2,3},{3,2},{4,5},{5,4},{6,7},{7,6},{8,9},{9,8},{10,11... | collective-permute-start | bytes 61448 | tf_op jit(solution)/shard_map/ppermute | solution.py:393
  6.7 0.0 collective-permute-start
  6.8 1.6 %collective-permute-start.3 = (bf16[32,128]{1,0:T(8,128)(2,1)S(1)}, bf16[32,128]{1,0:T(8,128)(2,1)S(1)}, u32[]{:S(2)}, u32[]{:S(2)}) collective-permute-start(bf16[32,128]{1,0:T(8,128)(2,1)S(1)} %get-tuple-element.19.x1_ref), channel_id=1, source_target_pairs={{0,4},{1,5},{2,6},{3,7},{4,0},{5,1},{6,2},{7,3},{8,12},{9,13},{10,... | collective-permute-start | bytes 24584 | tf_op jit(solution)/shard_map/ppermute | solution.py:393
  8.3 1.5 %shard_map.60 = (f32[16,256]{1,0:T(8,128)S(1)}, f32[4,32,128]{2,1,0:T(8,128)S(1)}) custom-call(bf16[16,4,32,128]{3,2,1,0:T(8,128)(2,1)S(1)} %get-tuple-element.21.basis_ref, bf16[4,32,128]{2,1,0:T(8,128)(2,1)S(1)} %get-tuple-element.22.mobility_ref, f32[4,32,128]{2,1,0:T(8,128)S(1)} %get-tuple-element.23.accumulation_ref, f32[16,128]{1,0:T(8,128)S(1)} %get-tuple-element.20.b_ref), custom_call_target="tpu_custom_call" | custom-call | flops 100000000 | bytes 1000000 | tf_op jit(solution)/shard_map/pallas_call | solution.py:427
  9.9 0.5 %collective-permute-done.rx2_ref = bf16[32,128]{1,0:T(8,128)(2,1)S(1)} collective-permute-done((bf16[32,128]{1,0:T(8,128)(2,1)S(1)}, bf16[32,128]{1,0:T(8,128)(2,1)S(1)}, u32[]{:S(2)}, u32[]{:S(2)}) %collective-permute-start) | collective-permute-done | bytes 8224 | tf_op jit(solution)/shard_map/ppermute | solution.py:393
  10.4 0.0 collective-permute-done.3.rx1_ref
  10.4 0.0 collective-permute-done.1.ry2_ref
  10.4 0.0 collective-permute-done.2.ry1_ref
  10.4 0.4 %shard_map.61 = (f32[32,128]{1,0:T(8,128)S(1)}, f32[24,128]{1,0:T(8,128)S(1)}) custom-call(bf16[80,128]{1,0:T(8,128)(2,1)S(1)} %get-tuple-element.16.y2_ref, bf16[80,128]{1,0:T(8,128)(2,1)S(1)} %get-tuple-element.17.y1_ref, bf16[32,128]{1,0:T(8,128)(2,1)S(1)} %get-tuple-element.18.x2_ref, bf16[32,128]{1,0:T(8,128)(2,1)S(1)} %get-tuple-element.19.x1_ref, ...), custom_call_target="tpu_custom_call" | custom-call | tf_op jit(solution)/shard_map/pallas_call | solution.py:436
  10.8 10.0 %all_to_all.11 = f32[32,1,128]{2,1,0:T(1,128)S(1)} all-to-all(f32[32,1,128]{2,1,0:T(1,128)S(1)} %bitcast.6), channel_id=1, replica_groups=mesh['gx'=8,'gy'=4] {'gx','gy'}, dimensions={0} | all-to-all | bytes 32768 | tf_op jit(solution)/shard_map/all_to_all | solution.py:446
  20.8 0.9 %shard_map.62 = (f32[4,32,128]{2,1,0:T(8,128)}, f32[1,16]{1,0:T(1,128)}) custom-call(f32[32,128]{1,0:T(8,128)S(1)} %bitcast.5, f32[16,128]{1,0:T(8,128)S(1)} %get-tuple-element.20.b_ref, f32[24,128]{1,0:T(8,128)S(1)} %get-tuple-element.26.v_ref, f32[4,32,128]{2,1,0:T(8,128)S(1)} %get-tuple-element.27.b_field_ref, ...), custom_call_target="tpu_custom_call" | custom-call | tf_op jit(solution)/shard_map/pallas_call | solution.py:447
Async XLA Ops:
  2.1 8.3 %collective-permute-start.1 = (bf16[80,128]{1,0:T(8,128)(2,1)S(1)}, bf16[80,128]{1,0:T(8,128)(2,1)S(1)}, u32[]{:S(2)}, u32[]{:S(2)}) collective-permute-start(bf16[80,128]{1,0:T(8,128)(2,1)S(1)} %get-tuple-element.16.y2_ref), channel_id=1, source_target_pairs={{0,4},{1,2},{2,1},{3,7},{4,0},{5,6},{6,5},{7,3},{8,12},{9,10},{10,... | collective-permute-start | bytes 61448 | tf_op jit(solution)/shard_map/ppermute | solution.py:393
  2.6 7.8 %collective-permute-start.2 = (bf16[80,128]{1,0:T(8,128)(2,1)S(1)}, bf16[80,128]{1,0:T(8,128)(2,1)S(1)}, u32[]{:S(2)}, u32[]{:S(2)}) collective-permute-start(bf16[80,128]{1,0:T(8,128)(2,1)S(1)} %get-tuple-element.17.y1_ref), channel_id=1, source_target_pairs={{0,1},{1,0},{2,3},{3,2},{4,5},{5,4},{6,7},{7,6},{8,9},{9,8},{10,11... | collective-permute-start | bytes 61448 | tf_op jit(solution)/shard_map/ppermute | solution.py:393
  6.7 3.7 %collective-permute-start = (bf16[32,128]{1,0:T(8,128)(2,1)S(1)}, bf16[32,128]{1,0:T(8,128)(2,1)S(1)}, u32[]{:S(2)}, u32[]{:S(2)}) collective-permute-start(bf16[32,128]{1,0:T(8,128)(2,1)S(1)} %get-tuple-element.18.x2_ref), channel_id=1, source_target_pairs={{0,1},{1,0},{2,3},{3,2},{4,8},{5,9},{6,10},{7,11},{8,4},{9,5},{10,... | collective-permute-start | bytes 24584 | tf_op jit(solution)/shard_map/ppermute | solution.py:393
  6.8 3.6 %collective-permute-start.3 = (bf16[32,128]{1,0:T(8,128)(2,1)S(1)}, bf16[32,128]{1,0:T(8,128)(2,1)S(1)}, u32[]{:S(2)}, u32[]{:S(2)}) collective-permute-start(bf16[32,128]{1,0:T(8,128)(2,1)S(1)} %get-tuple-element.19.x1_ref), channel_id=1, source_target_pairs={{0,4},{1,5},{2,6},{3,7},{4,0},{5,1},{6,2},{7,3},{8,12},{9,13},{10,... | collective-permute-start | bytes 24584 | tf_op jit(solution)/shard_map/ppermute | solution.py:393

commit v10 on v9

--- a/solution.py
+++ b/solution.py
@@ -154,7 +154,7 @@
     accumulation_copy.wait()
 
 
-def gram_kernel(basis_ref, mobility_ref, accumulation_ref, b_ref, gram_ref, field_ref, left_ref):
+def gram_kernel(basis_ref, mobility_ref, accumulation_ref, b_ref, gram_ref, image_ref, field_ref, left_ref):
     k_count, cz, cy, cx = basis_ref.shape
     mobility = mobility_ref[...].astype(F32)
     accumulation = accumulation_ref[...]
@@ -186,7 +186,11 @@
     total = total[:rows] + total[rows:]
     same = lax.rem(iota((rows, rows), 0), TILE) == lax.rem(iota((rows, rows), 1), TILE)
     total = jnp.where(same, total, 0.0)
-    gram_ref[...] = jnp.sum(total.reshape(k_count, TILE, rows), axis=1)
+    gram = jnp.sum(total.reshape(k_count, TILE, rows), axis=1)
+    gram_ref[...] = gram
+    place = iota((k_count, rows), 1) // TILE == iota((k_count, rows), 0)
+    b_row = jnp.sum(jnp.where(place, b_ref[:, :1], 0.0), axis=0, keepdims=True)
+    image_ref[...] = sum((gram * b_row)[:, start : start + LANES] for start in range(0, rows, LANES))
     field_ref[...] = expand(basis_ref, b_ref[...])
 
 
@@ -202,6 +206,7 @@
     rx1_ref,
     b_ref,
     gram_ref,
+    image_ref,
     out_ref,
     v_ref,
 ):
@@ -239,7 +244,7 @@
     def fold(x):
         return sum(x[:, start : start + LANES] for start in range(0, wide, LANES))
 
-    own_image = fold(gram * as_row(b_col))
+    own_image = image_ref[...]
     along = own_image
     for own, _, conductance, own_field, other_field in faces:
         flow = conductance * (own_field - other_field)
@@ -424,11 +429,15 @@
     ry1 = exchange(y1, "gy", counts, False)
     ry2 = exchange(y2, "gy", counts, True)
     conductance = jax.ShapeDtypeStruct((cz, cy, cx), F32)
-    gram, b_field = pl.pallas_call(
+    gram, image, b_field = pl.pallas_call(
         gram_kernel,
-        out_shape=(jax.ShapeDtypeStruct((k_count, k_count * TILE), F32), conductance),
+        out_shape=(
+            jax.ShapeDtypeStruct((k_count, k_count * TILE), F32),
+            jax.ShapeDtypeStruct((k_count, LANES), F32),
+            conductance,
+        ),
         in_specs=[VMEM] * 4,
-        out_specs=(VMEM,) * 2,
+        out_specs=(VMEM,) * 3,
         compiler_params=PARAMS,
         scratch_shapes=[pltpu.VMEM((2 * k_count * TILE, cz * cy // TILE * cx), BF16)],
         cost_estimate=pl.CostEstimate(flops=10**8, bytes_accessed=10**6, transcendentals=0),
@@ -439,10 +448,10 @@
             jax.ShapeDtypeStruct((devices, LANES), F32),
             jax.ShapeDtypeStruct((k_count + 8, LANES), F32),
         ),
-        in_specs=[VMEM] * 10,
+        in_specs=[VMEM] * 11,
         out_specs=(VMEM,) * 2,
         compiler_params=PARAMS,
-    )(y2, y1, x2, x1, rx2, ry2, ry1, rx1, b, gram)
+    )(y2, y1, x2, x1, rx2, ry2, ry1, rx1, b, gram, image)
     gathered = lax.all_to_all(row, ("gx", "gy"), 0, 0, tiled=True)
     correction, solution = pl.pallas_call(
         functools.partial(finish_kernel, counts[1]),

time: 21.8 us -> 21.8 us (level)
  no operation moved by 1% of the time
where the time goes in v10:
time: 21.8 us; the launch traced here: 21.6 us
  blocking collectives  9.99 us (46%)
  starting transfers between devices  6.27 us (29%)
  Pallas kernels  4.04 us (19%)
  between operations  0.65 us (3%)
  waiting for transfers between devices  0.63 us (3%)
    all_to_all x1, blocking collectives, per_device(): gathered = lax.all_to_all(row, ('gx', 'gy'), 0, 0, tiled=True)  9.99 us
    ppermute x4, starting transfers between devices, exchange(): return lax.ppermute(message, ('gx', 'gy'), pairs)  6.27 us
    pallas_call x1, Pallas kernels, per_device(): pl.pallas_call(functools.partial(edges_kernel, counts), out_shape=(x_mess...  1.43 us
    pallas_call x1, Pallas kernels, per_device(): pl.pallas_call(gram_kernel, out_shape=(jax.ShapeDtypeStruct((k_count, k_c...  1.42 us
    pallas_call x1, Pallas kernels, per_device(): pl.pallas_call(functools.partial(finish_kernel, counts[1]), out_shape=(ja...  0.89 us
    ppermute x4, waiting for transfers between devices, exchange(): return lax.ppermute(message, ('gx', 'gy'), pairs)  0.63 us
  transfers between devices with their start and end apart: 4, of which 1 were waited for; matrix products, arithmetic and copies ran while one was open for 0% of the time, Pallas kernels for 7%

profile of v10, /device:TPU:0, one launch (start us, length us, event | category | flops | bytes accessed | tf_op | source)
XLA Modules:
  0.0 21.6 jit_solution(8501491518210117483)
XLA Ops:
  0.6 1.4 %shard_map.59 = (bf16[32,128]{1,0:T(8,128)(2,1)S(1)}, bf16[32,128]{1,0:T(8,128)(2,1)S(1)}, bf16[80,128]{1,0:T(8,128)(2,1)S(1)}, bf16[80,128]{1,0:T(8,128)(2,1)S(...) custom-call(bf16[16,4,32,128]{3,2,1,0:T(8,128)(2,1)} %basis_hbm.1, ...), custom_call_target="tpu_custom_call" | custom-call | tf_op jit(solution)/shard_map/pallas_call | solution.py:407
  2.1 0.5 %collective-permute-start.1 = (bf16[80,128]{1,0:T(8,128)(2,1)S(1)}, bf16[80,128]{1,0:T(8,128)(2,1)S(1)}, u32[]{:S(2)}, u32[]{:S(2)}) collective-permute-start(bf16[80,128]{1,0:T(8,128)(2,1)S(1)} %get-tuple-element.17.y2_ref), channel_id=1, source_target_pairs={{0,4},{1,2},{2,1},{3,7},{4,0},{5,6},{6,5},{7,3},{8,12},{9,10},{10,... | collective-permute-start | bytes 61448 | tf_op jit(solution)/shard_map/ppermute | solution.py:398
  2.6 4.1 %collective-permute-start.2 = (bf16[80,128]{1,0:T(8,128)(2,1)S(1)}, bf16[80,128]{1,0:T(8,128)(2,1)S(1)}, u32[]{:S(2)}, u32[]{:S(2)}) collective-permute-start(bf16[80,128]{1,0:T(8,128)(2,1)S(1)} %get-tuple-element.18.y1_ref), channel_id=1, source_target_pairs={{0,1},{1,0},{2,3},{3,2},{4,5},{5,4},{6,7},{7,6},{8,9},{9,8},{10,11... | collective-permute-start | bytes 61448 | tf_op jit(solution)/shard_map/ppermute | solution.py:398
  6.7 0.0 collective-permute-start
  6.8 1.6 %collective-permute-start.3 = (bf16[32,128]{1,0:T(8,128)(2,1)S(1)}, bf16[32,128]{1,0:T(8,128)(2,1)S(1)}, u32[]{:S(2)}, u32[]{:S(2)}) collective-permute-start(bf16[32,128]{1,0:T(8,128)(2,1)S(1)} %get-tuple-element.20.x1_ref), channel_id=1, source_target_pairs={{0,4},{1,5},{2,6},{3,7},{4,0},{5,1},{6,2},{7,3},{8,12},{9,13},{10,... | collective-permute-start | bytes 24584 | tf_op jit(solution)/shard_map/ppermute | solution.py:398
  8.3 1.4 %shard_map.60 = (f32[16,256]{1,0:T(8,128)S(1)}, f32[16,128]{1,0:T(8,128)S(1)}, f32[4,32,128]{2,1,0:T(8,128)S(1)}) custom-call(bf16[16,4,32,128]{3,2,1,0:T(8,128)(2,1)S(1)} %get-tuple-element.22.basis_ref, bf16[4,32,128]{2,1,0:T(8,128)(2,1)S(1)} %get-tuple-element.23.mobility_ref, f32[4,32,128]{2,1,0:T(8,128)S(1)} %get-tuple-element.24.accumulation_ref, ...), custom_call_target="tpu_custom_call" | custom-call | flops 100000000 | bytes 1000000 | tf_op jit(solution)/shard_map/pallas_call | solution.py:432
  9.8 0.6 %collective-permute-done.rx2_ref = bf16[32,128]{1,0:T(8,128)(2,1)S(1)} collective-permute-done((bf16[32,128]{1,0:T(8,128)(2,1)S(1)}, bf16[32,128]{1,0:T(8,128)(2,1)S(1)}, u32[]{:S(2)}, u32[]{:S(2)}) %collective-permute-start) | collective-permute-done | bytes 8224 | tf_op jit(solution)/shard_map/ppermute | solution.py:398
  10.4 0.0 collective-permute-done.3.rx1_ref
  10.4 0.0 collective-permute-done.1.ry2_ref
  10.4 0.0 collective-permute-done.2.ry1_ref
  10.4 0.3 %shard_map.61 = (f32[32,128]{1,0:T(8,128)S(1)}, f32[24,128]{1,0:T(8,128)S(1)}) custom-call(bf16[80,128]{1,0:T(8,128)(2,1)S(1)} %get-tuple-element.17.y2_ref, bf16[80,128]{1,0:T(8,128)(2,1)S(1)} %get-tuple-element.18.y1_ref, bf16[32,128]{1,0:T(8,128)(2,1)S(1)} %get-tuple-element.19.x2_ref, bf16[32,128]{1,0:T(8,128)(2,1)S(1)} %get-tuple-element.20.x1_ref, ...), custom_call_target="tpu_custom_call" | custom-call | tf_op jit(solution)/shard_map/pallas_call | solution.py:445
  10.7 10.0 %all_to_all.11 = f32[32,1,128]{2,1,0:T(1,128)S(1)} all-to-all(f32[32,1,128]{2,1,0:T(1,128)S(1)} %bitcast.6), channel_id=1, replica_groups=mesh['gx'=8,'gy'=4] {'gx','gy'}, dimensions={0} | all-to-all | bytes 32768 | tf_op jit(solution)/shard_map/all_to_all | solution.py:455
  20.7 0.9 %shard_map.62 = (f32[4,32,128]{2,1,0:T(8,128)}, f32[1,16]{1,0:T(1,128)}) custom-call(f32[32,128]{1,0:T(8,128)S(1)} %bitcast.5, f32[16,128]{1,0:T(8,128)S(1)} %get-tuple-element.21.b_ref, f32[24,128]{1,0:T(8,128)S(1)} %get-tuple-element.28.v_ref, f32[4,32,128]{2,1,0:T(8,128)S(1)} %get-tuple-element.29.b_field_ref, ...), custom_call_target="tpu_custom_call" | custom-call | tf_op jit(solution)/shard_map/pallas_call | solution.py:456
Async XLA Ops:
  2.1 8.3 %collective-permute-start.1 = (bf16[80,128]{1,0:T(8,128)(2,1)S(1)}, bf16[80,128]{1,0:T(8,128)(2,1)S(1)}, u32[]{:S(2)}, u32[]{:S(2)}) collective-permute-start(bf16[80,128]{1,0:T(8,128)(2,1)S(1)} %get-tuple-element.17.y2_ref), channel_id=1, source_target_pairs={{0,4},{1,2},{2,1},{3,7},{4,0},{5,6},{6,5},{7,3},{8,12},{9,10},{10,... | collective-permute-start | bytes 61448 | tf_op jit(solution)/shard_map/ppermute | solution.py:398
  2.6 7.8 %collective-permute-start.2 = (bf16[80,128]{1,0:T(8,128)(2,1)S(1)}, bf16[80,128]{1,0:T(8,128)(2,1)S(1)}, u32[]{:S(2)}, u32[]{:S(2)}) collective-permute-start(bf16[80,128]{1,0:T(8,128)(2,1)S(1)} %get-tuple-element.18.y1_ref), channel_id=1, source_target_pairs={{0,1},{1,0},{2,3},{3,2},{4,5},{5,4},{6,7},{7,6},{8,9},{9,8},{10,11... | collective-permute-start | bytes 61448 | tf_op jit(solution)/shard_map/ppermute | solution.py:398
  6.7 3.7 %collective-permute-start = (bf16[32,128]{1,0:T(8,128)(2,1)S(1)}, bf16[32,128]{1,0:T(8,128)(2,1)S(1)}, u32[]{:S(2)}, u32[]{:S(2)}) collective-permute-start(bf16[32,128]{1,0:T(8,128)(2,1)S(1)} %get-tuple-element.19.x2_ref), channel_id=1, source_target_pairs={{0,1},{1,0},{2,3},{3,2},{4,8},{5,9},{6,10},{7,11},{8,4},{9,5},{10,... | collective-permute-start | bytes 24584 | tf_op jit(solution)/shard_map/ppermute | solution.py:398
  6.8 3.6 %collective-permute-start.3 = (bf16[32,128]{1,0:T(8,128)(2,1)S(1)}, bf16[32,128]{1,0:T(8,128)(2,1)S(1)}, u32[]{:S(2)}, u32[]{:S(2)}) collective-permute-start(bf16[32,128]{1,0:T(8,128)(2,1)S(1)} %get-tuple-element.20.x1_ref), channel_id=1, source_target_pairs={{0,4},{1,5},{2,6},{3,7},{4,0},{5,1},{6,2},{7,3},{8,12},{9,13},{10,... | collective-permute-start | bytes 24584 | tf_op jit(solution)/shard_map/ppermute | solution.py:398
